TPU v7x, 32 devices: a whole 2x2x4 slice. The times are simulated.
32 devices in a mesh: groups: 2 (over y), tx: 4 (over z), ty: 2 (over x), rep: 2 (over core).
Axes of the slice: x: 2, y: 2, z: 4, core: 2. Of those that a mesh axis runs over, the one named last changes fastest.
Arguments:
- features: bfloat16 [65536, 128], P(('groups', 'tx', 'ty', 'rep')), parts along dimension 0, may hold values from -6 to 6
- conv_weight: bfloat16 [27, 128, 128], replicated, may hold values from -0.109375 to 0.109375
- classifier: bfloat16 [128, 19], replicated, may hold values from -0.5 to 0.5
- send_rows: int32 [128, 128], P(('groups', 'tx', 'ty', 'rep')), parts along dimension 0, may hold values from 0 to 2048
- neighbour_map: int32 [27, 65536], P(None, ('groups', 'tx', 'ty', 'rep')), parts along dimension 1, may hold values from 0 to 2560
- labels: int32 [65536], P(('groups', 'tx', 'ty', 'rep')), parts along dimension 0, may hold values from 0 to 18
Outputs:
- grad_input: float32 [65536, 128], P(('groups', 'tx', 'ty', 'rep')), parts along dimension 0
- grad_conv: float32 [54, 128, 128], P('groups'), parts along dimension 0
- grad_head: float32 [256, 19], P('groups'), parts along dimension 0
There are 2 independent parts, one for each index of `groups`. A program takes and returns all parts, laid end to end along the dimension named above; an argument that names none is the same for every part. Nothing has to cross between parts.
Inputs may be any that keep to these rules, and one draw needn't show every extreme that they name: `send_rows`: an entry 2048 is padding; other entries are rows of the sending tile. `neighbour_map`: rows below 2048 are the tile's own voxels, row 2048 is zero, then 128 received rows from each of the four neighbours in the order lower tx, higher tx, lower ty, higher ty.
All inputs are finite; a program needn't handle non-finite values.
Results may differ from a plain program's by a relative error of at most 0.0035.
Values may be sent and summed in bfloat16 or wider, within the bound.
No kernel may reach another device: no remote copies, remote signals or barrier semaphores. Data moves between devices by JAX's collectives and lax.ppermute only.
A program may use at most 128 MiB of HBM per device.

v0:
```python
import math

import jax
import jax.numpy as jnp
from jax import lax
from jax.sharding import PartitionSpec as P


def passed_along(shard, axis, by):
    devices = lax.axis_size(axis)
    pairs = [(i, i + by) for i in range(devices) if 0 <= i + by < devices]
    return lax.ppermute(shard, axis, pairs)


def pass_tx(block, step):
    return passed_along(block, "tx", step)


def pass_ty(block, step):
    return passed_along(block, "ty", step)


def back_tx(block, step):
    return passed_along(block.astype(jnp.bfloat16), "tx", step).astype(block.dtype)


def back_ty(block, step):
    return passed_along(block.astype(jnp.bfloat16), "ty", step).astype(block.dtype)


def on_device(features, conv_weight, classifier, send_rows, neighbour_map, labels):
    rows = features.shape[0]
    chans = features.shape[1]
    width = send_rows.shape[1]
    offsets = conv_weight.shape[0]
    classes = classifier.shape[1]
    span = offsets // 3
    padded = jnp.concatenate([features, jnp.zeros((1, chans), jnp.bfloat16)], axis=0)
    outgoing = padded[send_rows]
    incoming = jnp.concatenate(
        [
            pass_tx(outgoing[0], 1),
            pass_tx(outgoing[1], -1),
            pass_ty(outgoing[2], 1),
            pass_ty(outgoing[3], -1),
        ],
        axis=0,
    )
    extended = jnp.concatenate([padded, incoming], axis=0)
    pre = jnp.zeros((rows, chans), jnp.float32)
    for group in range(3):
        index_block = neighbour_map[group * span : (group + 1) * span]
        pieces = extended[index_block]
        weights = conv_weight[group * span : (group + 1) * span]
        pre = pre + jnp.einsum("kvc,kcd->vd", pieces, weights, preferred_element_type=jnp.float32)
    sig = jax.nn.sigmoid(pre)
    mixed = (features.astype(jnp.float32) + pre * sig).astype(jnp.bfloat16)
    logits = jnp.dot(mixed, classifier, preferred_element_type=jnp.float32)
    probs = jax.nn.softmax(logits, axis=-1)
    onehot = (labels[:, None] == jnp.arange(classes)[None, :]).astype(jnp.float32)
    dlogits = (probs - onehot).astype(jnp.bfloat16)
    head_part = lax.dot_general(
        mixed, dlogits, (((0,), (0,)), ((), ())), preferred_element_type=jnp.float32
    )
    dmixed = lax.dot_general(
        dlogits, classifier, (((1,), (1,)), ((), ())), preferred_element_type=jnp.float32
    )
    dpre = (dmixed * sig * (1.0 + pre * (1.0 - sig))).astype(jnp.bfloat16)
    table = jnp.zeros((rows + 1 + 4 * width, chans), jnp.float32)
    conv_blocks = []
    for group in range(3):
        index_block = neighbour_map[group * span : (group + 1) * span]
        pieces = extended[index_block]
        weights = conv_weight[group * span : (group + 1) * span]
        conv_blocks.append(
            jnp.einsum("kvc,vd->kcd", pieces, dpre, preferred_element_type=jnp.float32)
        )
        dpieces = jnp.einsum("vd,kcd->kvc", dpre, weights, preferred_element_type=jnp.float32)
        table = table.at[index_block.reshape(-1)].add(dpieces.reshape(-1, chans))
    conv_part = jnp.concatenate(conv_blocks, axis=0)
    back = table[rows + 1 :].reshape(4, width, chans)
    returned = jnp.concatenate(
        [back_tx(back[0], -1), back_tx(back[1], 1), back_ty(back[2], -1), back_ty(back[3], 1)],
        axis=0,
    )
    dpad = table[: rows + 1].at[send_rows.reshape(-1)].add(returned)
    grad_input = dpad[:rows] + dmixed
    conv_total, head_total = lax.psum((conv_part, head_part), ("tx", "ty", "rep"))
    count = rows * lax.axis_size("tx") * lax.axis_size("ty") * lax.axis_size("rep")
    scale = 1.0 / math.sqrt(count)
    return (grad_input, conv_total * scale, head_total * scale)


def solution(mesh):
    placed = (
        P(("groups", "tx", "ty", "rep"), None),
        P(),
        P(),
        P(("groups", "tx", "ty", "rep"), None),
        P(None, ("groups", "tx", "ty", "rep")),
        P(("groups", "tx", "ty", "rep")),
    )
    return jax.shard_map(
        on_device,
        mesh=mesh,
        in_specs=placed,
        out_specs=(
            P(("groups", "tx", "ty", "rep"), None),
            P("groups", None, None),
            P("groups", None),
        ),
        check_vma=False,
    )
```

profile of v0, /device:TPU:0, one launch (start us, length us, event | category | flops | bytes accessed | tf_op | source)
XLA Modules:
  0.0 639.7 jit_solution(16679634982872453044)
XLA Ops:
  9.1 1.3 gather_fusion
  10.4 4.9 collective-permute-start
  15.4 1.3 collective-permute-start.1
  16.7 3.4 collective-permute-start.2
  20.1 1.3 collective-permute-start.3
  21.4 1.1 slice_bitcast_fusion
  25.9 1.1 concatenate.17
  27.1 64.9 %gather_fusion.3 = bf16[18432,128]{1,0:T(8,128)(2,1)} fusion(bf16[2561,128]{1,0:T(8,128)(2,1)S(1)} %concatenate.17, s32[18432]{0:T(1024)S(1)} %broadcast_clamp_fusion), kind=kCustom, calls=%fused_computation.3 | custom fusion | bytes 9510912 | tf_op jit(solution)/shard_map/gather | solution.py:53
  92.0 65.0 %gather_fusion.2 = bf16[18432,128]{1,0:T(8,128)(2,1)} fusion(bf16[2561,128]{1,0:T(8,128)(2,1)S(1)} %concatenate.17, s32[18432]{0:T(1024)S(1)} %broadcast_clamp_fusion.1), kind=kCustom, calls=%fused_computation.2 | custom fusion | bytes 9510912 | tf_op jit(solution)/shard_map/gather | solution.py:53
  157.1 3.9 convolution_bitcast_fusion
  161.0 2.4 convolution_bitcast_fusion.1
  163.4 65.0 %gather_fusion.1 = bf16[18432,128]{1,0:T(8,128)(2,1)} fusion(bf16[2561,128]{1,0:T(8,128)(2,1)S(1)} %concatenate.17, s32[18432]{0:T(1024)S(1)} %broadcast_clamp_fusion.2), kind=kCustom, calls=%fused_computation.1 | custom fusion | bytes 9510912 | tf_op jit(solution)/shard_map/gather | solution.py:53
  228.4 4.5 add_convert_fusion
  234.3 1.4 fusion.4
  236.1 1.4 fusion.6
  237.6 1.4 fusion.8
  239.0 5.0 fusion.14
  244.0 5.1 fusion.12
  249.1 5.1 fusion.10
  254.2 1.3 pad_maximum_fusion
  255.5 98.7 %scatter_custom_fusion = f32[2561,128]{1,0:T(8,128)S(1)} fusion(s32[18432]{0:T(1024)} %bitcast.87, f32[18432,128]{1,0:T(8,128)} %bitcast.81, f32[]{:T(128)} %constant.8.clone.1), kind=kCustom, calls=%fused_computation.19 | custom fusion | flops 2359296 | bytes 1311744 | tf_op jit(solution)/shard_map/scatter-add | solution.py:79
  354.3 99.1 %scatter_fusion = f32[2561,128]{1,0:T(8,128)S(1)} fusion(f32[2561,128]{1,0:T(8,128)S(1)} %scatter_custom_fusion, s32[18432]{0:T(1024)S(1)} %bitcast.82, f32[18432,128]{1,0:T(8,128)} %bitcast.76), kind=kCustom, calls=%fused_computation.5 | custom fusion | flops 2359296 | bytes 28385280 | tf_op jit(solution)/shard_map/scatter-add | solution.py:79
  453.4 98.9 %scatter_fusion.1 = f32[2561,128]{1,0:T(8,128)S(1)} fusion(f32[2561,128]{1,0:T(8,128)S(1)} %scatter_fusion, s32[18432]{0:T(1024)S(1)} %bitcast.83, f32[18432,128]{1,0:T(8,128)} %bitcast.75), kind=kCustom, calls=%fused_computation.6 | custom fusion | flops 2359296 | bytes 28385280 | tf_op jit(solution)/shard_map/scatter-add | solution.py:79
  553.1 1.3 collective-permute-start.4
  554.4 5.2 collective-permute-start.5
  559.6 1.3 collective-permute-start.6
  560.9 4.5 collective-permute-start.7
  565.4 1.2 fusion.33
  566.7 57.6 %psum.15 = f32[128,19]{0,1:T(8,128)S(1)} all-reduce(f32[128,19]{0,1:T(8,128)S(1)} %fusion.33), channel_id=1, replica_groups=mesh['groups'=2,'tx'=4,'ty'=2,'rep'=2] {'tx','ty','rep'}, use_global_device_ids=true, to_apply=%region_7.0 | all-reduce | flops 2432 | bytes 19456 | tf_op jit(solution)/shard_map/psum | solution.py:88
  625.0 3.8 scatter_custom_fusion.3
  628.8 1.1 slice_add_fusion
  630.0 2.9 broadcast_multiply_fusion
  (69 shorter events, 8.4 us)
Async XLA Ops:
  7.2 225.7 %copy-start = (bf16[128,19]{0,1:T(8,128)(2,1)S(1)}, bf16[128,19]{0,1:T(8,128)(2,1)}, u32[]{:S(2)}) copy-start(bf16[128,19]{0,1:T(8,128)(2,1)} %param.8) | copy-start | bytes 14596
  7.2 17.2 %copy-start.6 = (s32[4,128]{1,0:T(4,128)S(1)}, s32[4,128]{1,0:T(4,128)}, u32[]{:S(2)}) copy-start(s32[4,128]{1,0:T(4,128)} %param.9) | copy-start | bytes 6148
  7.2 18.7 %copy-start.3 = (bf16[2048,128]{1,0:T(8,128)(2,1)S(1)}, bf16[2048,128]{1,0:T(8,128)(2,1)}, u32[]{:S(2)}) copy-start(bf16[2048,128]{1,0:T(8,128)(2,1)} %param.6) | copy-start | bytes 1572868
  7.2 622.8 %all-reduce.3.cloned.1.call-start = ((), (), s32[]{:S(2)}) async-start(), calls=%async_computation | async-start | bytes 3538944 | tf_op jit(solution)/shard_map/psum | solution.py:88
  10.4 14.5 %collective-permute-start = (bf16[128,128]{1,0:T(8,128)(2,1)S(1)}, bf16[128,128]{1,0:T(8,128)(2,1)S(1)}, u32[]{:S(2)}, u32[]{:S(2)}) collective-permute-start(bf16[128,128]{1,0:T(8,128)(2,1)S(1)} %get-tuple-element.16), channel_id=1, source_target_pairs={{0,4},{4,8},{8,12},{1,5},{5,9},{9,13},{2,6},{6,10},{10,14},{3,7},{... | collective-permute-start | bytes 98312 | tf_op jit(solution)/shard_map/ppermute | solution.py:12
  15.4 9.6 %collective-permute-start.1 = (bf16[128,128]{1,0:T(8,128)(2,1)S(1)}, bf16[128,128]{1,0:T(8,128)(2,1)S(1)}, u32[]{:S(2)}, u32[]{:S(2)}) collective-permute-start(bf16[128,128]{1,0:T(8,128)(2,1)S(1)} %get-tuple-element.15), channel_id=1, source_target_pairs={{4,0},{8,4},{12,8},{5,1},{9,5},{13,9},{6,2},{10,6},{14,10},{7,3},{... | collective-permute-start | bytes 98312 | tf_op jit(solution)/shard_map/ppermute | solution.py:12
  16.7 8.3 %collective-permute-start.2 = (bf16[128,128]{1,0:T(8,128)(2,1)S(1)}, bf16[128,128]{1,0:T(8,128)(2,1)S(1)}, u32[]{:S(2)}, u32[]{:S(2)}) collective-permute-start(bf16[128,128]{1,0:T(8,128)(2,1)S(1)} %get-tuple-element.14), channel_id=1, source_target_pairs={{0,2},{1,3},{4,6},{5,7},{8,10},{9,11},{12,14},{13,15},{16,18},{17,... | collective-permute-start | bytes 98312 | tf_op jit(solution)/shard_map/ppermute | solution.py:12
  20.1 5.8 collective-permute-start.3
  92.0 65.1 %copy-start.2 = (bf16[27,128,128]{2,1,0:T(8,128)(2,1)S(1)}, bf16[27,128,128]{2,1,0:T(8,128)(2,1)}, u32[]{:S(2)}) copy-start(bf16[27,128,128]{2,1,0:T(8,128)(2,1)} %param.7) | copy-start | bytes 2654212
  157.0 3.9 copy-start.1
  228.4 5.9 slice-start
  228.4 5.3 copy-start.7
  228.4 5.9 slice-start.1
  232.9 0.8 copy-start.4
  233.7 2.2 slice-start.2
  234.3 1.8 slice-start.3
  234.3 3.3 slice-start.4
  236.1 1.4 slice-start.5
  354.3 99.1 %copy-start.5 = (s32[18432,1]{0,1:T(1,128)S(1)}, s32[18432,1]{0,1:T(1,128)}, u32[]{:S(2)}) copy-start(s32[18432,1]{0,1:T(1,128)} %compare_select_fusion) | copy-start | bytes 221188
  453.4 112.0 %copy-start.8 = (s32[2048]{0:T(1024)S(1)}, s32[2048]{0:T(1024)}, u32[]{:S(2)}) copy-start(s32[2048]{0:T(1024)} %param.11) | copy-start | bytes 24580
  553.1 71.9 %collective-permute-start.4 = (bf16[128,128]{1,0:T(8,128)(2,1)}, bf16[128,128]{1,0:T(8,128)(2,1)S(1)}, u32[]{:S(2)}, u32[]{:S(2)}) collective-permute-start(bf16[128,128]{1,0:T(8,128)(2,1)} %get-tuple-element.3), channel_id=1, source_target_pairs={{4,0},{8,4},{12,8},{5,1},{9,5},{13,9},{6,2},{10,6},{14,10},{7,3},{... | collective-permute-start | bytes 98312 | tf_op jit(solution)/shard_map/ppermute | solution.py:12
  554.4 70.6 %collective-permute-start.5 = (bf16[128,128]{1,0:T(8,128)(2,1)}, bf16[128,128]{1,0:T(8,128)(2,1)S(1)}, u32[]{:S(2)}, u32[]{:S(2)}) collective-permute-start(bf16[128,128]{1,0:T(8,128)(2,1)} %get-tuple-element.6), channel_id=1, source_target_pairs={{0,4},{4,8},{8,12},{1,5},{5,9},{9,13},{2,6},{6,10},{10,14},{3,7},{... | collective-permute-start | bytes 98312 | tf_op jit(solution)/shard_map/ppermute | solution.py:12
  559.6 65.4 %collective-permute-start.6 = (bf16[128,128]{1,0:T(8,128)(2,1)}, bf16[128,128]{1,0:T(8,128)(2,1)S(1)}, u32[]{:S(2)}, u32[]{:S(2)}) collective-permute-start(bf16[128,128]{1,0:T(8,128)(2,1)} %get-tuple-element.5), channel_id=1, source_target_pairs={{2,0},{3,1},{6,4},{7,5},{10,8},{11,9},{14,12},{15,13},{18,16},{19,... | collective-permute-start | bytes 98312 | tf_op jit(solution)/shard_map/ppermute | solution.py:12
  560.9 64.1 %collective-permute-start.7 = (bf16[128,128]{1,0:T(8,128)(2,1)}, bf16[128,128]{1,0:T(8,128)(2,1)S(1)}, u32[]{:S(2)}, u32[]{:S(2)}) collective-permute-start(bf16[128,128]{1,0:T(8,128)(2,1)} %get-tuple-element.4), channel_id=1, source_target_pairs={{0,2},{1,3},{4,6},{5,7},{8,10},{9,11},{12,14},{13,15},{16,18},{17,... | collective-permute-start | bytes 98312 | tf_op jit(solution)/shard_map/ppermute | solution.py:12
Sparse Core Ops, SparseCore 0:
  255.7 99.1 all-reduce.2
where the time goes:
time: 640 us
  other arithmetic  311 us (49%)
  local copies, waits for them, and re-layouts  200 us (31%)
  blocking collectives  57.6 us (9%)
  matrix products  32.4 us (5%)
  starting transfers between devices  23.2 us (4%)
  between operations  14.5 us (2%)
    scatter-add x3, other arithmetic, on_device(): table = table.at[index_block.reshape(-1)].add(dpieces.reshape(-1, chans))  297 us
    gather x3, local copies, waits for them, and re-layouts, on_device(): pieces = extended[index_block]  195 us
    psum x1, blocking collectives, on_device(): lax.psum((conv_part, head_part), ('tx', 'ty', 'rep'))  57.6 us
    ppermute x8, starting transfers between devices, passed_along(): return lax.ppermute(shard, axis, pairs)  23.2 us
    dot_general x3, matrix products, on_device(): jnp.einsum('vd,kcd->kvc', dpre, weights, preferred_element_type=jnp.float32)  15.2 us
  transfers between devices with their start and end apart: 9, of which 1 were waited for; matrix products, arithmetic and copies ran while one was open for 48% of the time, Pallas kernels for 0%

commit v1 on v0

v1 whole, which is shorter than its diff:
```python
import functools
import math

import jax
import jax.numpy as jnp
from jax import lax
from jax.experimental import pallas as pl
from jax.experimental.pallas import tpu as pltpu
from jax.sharding import PartitionSpec as P

STREAMS = 4
SEGMENT = 64
GAP = 16
CHUNKS = 3
HEAD_ROWS = 32
VMEM = pl.BlockSpec(memory_space=pltpu.VMEM)
HBM = pl.BlockSpec(memory_space=pl.ANY)
NN = (((1,), (0,)), ((), ()))
NT = (((1,), (1,)), ((), ()))
TN = (((0,), (0,)), ((), ()))


def dot(a, b, dims):
    return lax.dot_general(a, b, dims, preferred_element_type=jnp.float32)


def fetch(map_hbm, index, sems, first, length):
    copies = []
    for n, ref in enumerate(index):
        copy = pltpu.make_async_copy(
            map_hbm.at[pl.ds((first + n) * length, length)], ref, sems.at[n]
        )
        copy.start()
        copies.append(copy)
    return copies


def forward_kernel(
    classes, map_hbm, own_ref, halo_refs, weight_ref, class_ref, label_ref,
    dpre_ref, dmixed_ref, conv_ref, table, rows, wide, total, sems, *index,
):
    voxels, chans = dpre_ref.shape
    offsets = len(index) // STREAMS
    stream = voxels // STREAMS
    block = STREAMS * SEGMENT
    copies = fetch(map_hbm, index, sems, 0, stream)
    width = halo_refs[0].shape[0]
    table[:voxels, :] = own_ref[...].astype(jnp.float32)
    table[voxels : voxels + GAP, :] = jnp.zeros((GAP, chans), jnp.float32)
    for n, halo in enumerate(halo_refs):
        start = voxels + GAP + n * width
        table[start : start + width, :] = halo[...].astype(jnp.float32)
    total[...] = jnp.zeros_like(total)
    conv_ref[pl.ds(offsets * chans, conv_ref.shape[0] - offsets * chans), :] = jnp.zeros(
        (conv_ref.shape[0] - offsets * chans, chans), jnp.float32
    )
    for copy in copies:
        copy.wait()

    def block_step(b, carry):
        def gather_step(i, carry):
            at = i - b * SEGMENT
            for u in range(STREAMS):
                for k in range(offsets):
                    rows[k, pl.ds(u * SEGMENT + at, 1), :] = table[
                        pl.ds(index[k * STREAMS + u][i], 1), :
                    ]
            return carry

        lax.fori_loop(b * SEGMENT, (b + 1) * SEGMENT, gather_step, 0)
        for k in range(offsets):
            wide[:, k * chans : (k + 1) * chans] = rows[k].astype(jnp.bfloat16)
        pre = dot(wide[...], weight_ref[...], NN)
        starts = [pl.multiple_of(u * stream + b * SEGMENT, SEGMENT) for u in range(STREAMS)]
        own = jnp.concatenate([table[pl.ds(s, SEGMENT), :] for s in starts], axis=0)
        sig = jax.nn.sigmoid(pre)
        mixed = (own + pre * sig).astype(jnp.bfloat16)
        logits = dot(class_ref[...], mixed, NT)
        which = lax.broadcasted_iota(jnp.int32, logits.shape, 0)
        logits = jnp.where(which < classes, logits, -1e30)
        high = jnp.max(logits, axis=0, keepdims=True)
        expd = jnp.exp(logits - high)
        probs = expd / jnp.sum(expd, axis=0, keepdims=True)
        onehot = (which == label_ref[b]).astype(jnp.float32)
        dlogits = (probs - onehot).astype(jnp.bfloat16)
        conv_ref[pl.ds(offsets * chans, HEAD_ROWS), :] += dot(dlogits, mixed, NN)
        dmixed = dot(dlogits, class_ref[...], TN)
        dpre = (dmixed * sig * (1.0 + pre * (1.0 - sig))).astype(jnp.bfloat16)
        full = dpre.astype(jnp.float32)
        for u, s in enumerate(starts):
            dmixed_ref[pl.ds(s, SEGMENT), :] = dmixed[u * SEGMENT : (u + 1) * SEGMENT]
            dpre_ref[pl.ds(s, SEGMENT), :] = full[u * SEGMENT : (u + 1) * SEGMENT]
        total[...] += dot(full.T.astype(jnp.bfloat16), wide[...], NN)
        return carry

    lax.fori_loop(0, voxels // block, block_step, 0)
    for k in range(offsets):
        conv_ref[k * chans : (k + 1) * chans, :] = total[:, k * chans : (k + 1) * chans].T


def forward(map_flat, features, incoming, weights, class_t, label_blocks, classes, reduce_rows, table_rows):
    voxels, chans = features.shape
    offsets = weights.shape[0] // chans
    stream = voxels // STREAMS
    block = STREAMS * SEGMENT
    return pl.pallas_call(
        functools.partial(forward_kernel, classes),
        out_shape=(
            jax.ShapeDtypeStruct((voxels, chans), jnp.float32),
            jax.ShapeDtypeStruct((voxels, chans), jnp.float32),
            jax.ShapeDtypeStruct((reduce_rows, chans), jnp.float32),
        ),
        in_specs=[HBM, VMEM, [VMEM] * 4, VMEM, VMEM, VMEM],
        out_specs=(VMEM, VMEM, VMEM),
        scratch_shapes=[
            pltpu.VMEM((table_rows, chans), jnp.float32),
            pltpu.VMEM((offsets, block, chans), jnp.float32),
            pltpu.VMEM((block, offsets * chans), jnp.bfloat16),
            pltpu.VMEM((chans, offsets * chans), jnp.float32),
            pltpu.SemaphoreType.DMA((offsets * STREAMS,)),
        ]
        + [pltpu.SMEM((stream,), jnp.int32)] * (offsets * STREAMS),
        compiler_params=pltpu.CompilerParams(vmem_limit_bytes=40 << 20),
        cost_estimate=pl.CostEstimate(
            flops=4 * voxels * offsets * chans * chans, bytes_accessed=150 << 20, transcendentals=0
        ),
        name="forward",
    )(map_flat, features, incoming, weights, class_t, label_blocks)


def scatter_kernel(first, has_before, map_hbm, dpre_ref, weight_ref, *refs):
    refs = list(refs)
    before = refs.pop(0) if has_before else None
    out_ref, sems = refs[0], refs[1]
    offsets = weight_ref.shape[0] // weight_ref.shape[1]
    tables = refs[2 : 2 + offsets]
    index = refs[2 + offsets :]
    voxels, chans = dpre_ref.shape
    stream = voxels // STREAMS
    copies = fetch(map_hbm, index, sems, first * STREAMS, stream)
    for table in tables:
        table[...] = jnp.zeros_like(table)
    for copy in copies:
        copy.wait()

    def step(i, carry):
        for u in range(STREAMS):
            row = dpre_ref[pl.ds(u * stream + i, 1), :]
            for k in range(offsets):
                at = pl.ds(index[k * STREAMS + u][i], 1)
                tables[k][at, :] = tables[k][at, :] + row
        return carry

    lax.fori_loop(0, stream, step, 0)
    tiles = 3
    height = out_ref.shape[0] // tiles

    def finish(t, carry):
        at = pl.ds(pl.multiple_of(t * height, 16), height)
        wide = jnp.concatenate([table[at, :].astype(jnp.bfloat16) for table in tables], axis=1)
        result = dot(wide, weight_ref[...], NN)
        out_ref[at, :] = result + before[at, :] if has_before else result
        return carry

    lax.fori_loop(0, tiles, finish, 0)


def scatter(map_flat, dpre, weights_t, before, first, table_rows):
    voxels, chans = dpre.shape
    offsets = weights_t.shape[0] // chans
    stream = voxels // STREAMS
    has_before = before is not None
    return pl.pallas_call(
        functools.partial(scatter_kernel, first, has_before),
        out_shape=jax.ShapeDtypeStruct((table_rows, chans), jnp.float32),
        in_specs=[HBM, VMEM, VMEM] + ([VMEM] if has_before else []),
        out_specs=VMEM,
        scratch_shapes=[pltpu.SemaphoreType.DMA((offsets * STREAMS,))]
        + [pltpu.VMEM((table_rows, chans), jnp.float32)] * offsets
        + [pltpu.SMEM((stream,), jnp.int32)] * (offsets * STREAMS),
        compiler_params=pltpu.CompilerParams(vmem_limit_bytes=40 << 20),
        cost_estimate=pl.CostEstimate(
            flops=2 * voxels * offsets * chans * chans, bytes_accessed=40 << 20, transcendentals=0
        ),
        name=f"scatter_{first}",
    )(map_flat, dpre, weights_t, *([before] if has_before else []))


def finish_kernel(dmixed_ref, dext_ref, send_ref, back_ref, out_ref):
    voxels, chans = out_ref.shape
    height = voxels // 8

    def step(t, carry):
        at = pl.ds(pl.multiple_of(t * height, height), height)
        row = lax.broadcasted_iota(jnp.int32, (height, send_ref.shape[1]), 0) + t * height
        chosen = (row == send_ref[...]).astype(jnp.float32).astype(jnp.bfloat16)
        out_ref[at, :] = dmixed_ref[at, :] + dext_ref[at, :] + dot(chosen, back_ref[...], NN)
        return carry

    lax.fori_loop(0, voxels // height, step, 0)


def finish(dmixed, dext, send_flat, back):
    return pl.pallas_call(
        finish_kernel,
        out_shape=jax.ShapeDtypeStruct(dmixed.shape, jnp.float32),
        in_specs=[VMEM] * 4,
        out_specs=VMEM,
        compiler_params=pltpu.CompilerParams(vmem_limit_bytes=40 << 20),
        cost_estimate=pl.CostEstimate(flops=1 << 28, bytes_accessed=4 << 20, transcendentals=0),
        name="finish",
    )(dmixed, dext, send_flat, back)


def exchange(shard, axis, distance):
    devices = lax.axis_size(axis)
    return lax.ppermute(shard, axis, [(i, i ^ distance) for i in range(devices)])


def swap_edges(down, up, axis):
    devices = lax.axis_size(axis)
    odd = (lax.axis_index(axis) & 1) != 0
    even_pairs = [(i, i ^ 1) for i in range(devices) if (i ^ 1) < devices]
    odd_pairs = [(i, ((i + 1) ^ 1) - 1) for i in range(1, devices) if ((i + 1) ^ 1) - 1 < devices]
    first = lax.ppermute(jnp.where(odd, down, up), axis, even_pairs)
    if odd_pairs:
        second = lax.ppermute(jnp.where(odd, up, down), axis, odd_pairs)
    else:
        second = jnp.zeros_like(first)
    return jnp.where(odd, first, second), jnp.where(odd, second, first)


def on_device(features, conv_weight, classifier, send_rows, neighbour_map, labels):
    voxels, chans = features.shape
    width = send_rows.shape[1]
    offsets = conv_weight.shape[0]
    classes = classifier.shape[1]
    block = STREAMS * SEGMENT
    table_rows = -(-(voxels + GAP + 4 * width) // 48) * 48
    reduce_rows = -(-(offsets * chans + HEAD_ROWS) // 64) * 64

    outgoing = jnp.where(
        (send_rows < voxels)[..., None], features[jnp.minimum(send_rows, voxels - 1)], 0
    )
    low_y, high_y = swap_edges(outgoing[3], outgoing[2], "ty")
    low_x, high_x = swap_edges(outgoing[1], outgoing[0], "tx")

    map_flat = jnp.where(neighbour_map > voxels, neighbour_map + (GAP - 1), neighbour_map).reshape(-1)
    weights = conv_weight.reshape(offsets * chans, chans)
    weights_t = conv_weight.transpose(0, 2, 1).reshape(offsets * chans, chans)
    class_t = jnp.pad(classifier.T, ((0, HEAD_ROWS - classes), (0, 0)))
    label_blocks = (
        labels.reshape(STREAMS, voxels // block, SEGMENT).transpose(1, 0, 2)
        .reshape(voxels // block, 1, block)
    )
    dpre, dmixed, part = forward(
        map_flat, features, [low_x, high_x, low_y, high_y], weights, class_t, label_blocks,
        classes, reduce_rows, table_rows,
    )

    chunks = [
        (c * offsets // CHUNKS, (c + 1) * offsets // CHUNKS) for c in range(CHUNKS)
    ]
    dext = None

    def scatter_beside(sent, before):
        if not chunks:
            return sent, before
        first, last = chunks.pop(0)
        held = (sent, dpre) if before is None else (sent, dpre, before)
        held = lax.optimization_barrier(held)
        return held[0], scatter(
            map_flat, held[1], weights_t[first * chans : last * chans],
            None if before is None else held[2], first, table_rows,
        )

    halved = []
    for axis, kind in (("rep", jnp.float32), ("ty", jnp.bfloat16)):
        distance = lax.axis_size(axis) // 2
        while distance:
            halved.append((axis, distance))
            upper = (lax.axis_index(axis) & distance) != 0
            half = part.shape[0] // 2
            low, high = part[:half], part[half:]
            sent = jnp.where(upper, low, high).astype(kind)
            if axis != "rep":
                sent, dext = scatter_beside(sent, dext)
            got = exchange(sent, axis, distance)
            if dext is not None:
                got, dext = lax.optimization_barrier((got, dext))
            part = jnp.where(upper, high, low) + got.astype(jnp.float32)
            distance //= 2
    distance = lax.axis_size("tx") // 2
    kind = jnp.bfloat16
    while distance:
        sent, dext = scatter_beside(part.astype(kind), dext)
        got, dext = lax.optimization_barrier((exchange(sent, "tx", distance), dext))
        part = sent.astype(jnp.float32) + got.astype(jnp.float32)
        distance //= 2
        kind = jnp.float32
    while chunks:
        part, dext = scatter_beside(part, dext)
    total = part.astype(jnp.bfloat16)
    for axis, distance in reversed(halved):
        upper = (lax.axis_index(axis) & distance) != 0
        got = exchange(total, axis, distance)
        total = jnp.where(
            upper, jnp.concatenate([got, total], axis=0), jnp.concatenate([total, got], axis=0)
        )

    start = voxels + GAP
    halo = dext[start : start + 4 * width].astype(jnp.bfloat16).reshape(4, width, chans)
    back_3, back_2 = swap_edges(halo[2], halo[3], "ty")
    back_1, back_0 = swap_edges(halo[0], halo[1], "tx")
    back = jnp.concatenate([back_0, back_1, back_2, back_3], axis=0)
    grad_input = finish(dmixed, dext, send_rows.reshape(1, -1), back)

    count = voxels * lax.axis_size("tx") * lax.axis_size("ty") * lax.axis_size("rep")
    scale = 1.0 / math.sqrt(count)
    total = total.astype(jnp.float32) * scale
    grad_conv = total[: offsets * chans].reshape(offsets, chans, chans)
    grad_head = total[offsets * chans : offsets * chans + classes].T
    return grad_input, grad_conv, grad_head


def solution(mesh):
    placed = (
        P(("groups", "tx", "ty", "rep"), None),
        P(),
        P(),
        P(("groups", "tx", "ty", "rep"), None),
        P(None, ("groups", "tx", "ty", "rep")),
        P(("groups", "tx", "ty", "rep")),
    )
    return jax.shard_map(
        on_device,
        mesh=mesh,
        in_specs=placed,
        out_specs=(
            P(("groups", "tx", "ty", "rep"), None),
            P("groups", None, None),
            P("groups", None),
        ),
        check_vma=False,
    )
```

time: 640 us -> 149 us (0.23)
  other arithmetic: 311 us -> 6.3 us
  local copies, waits for them, and re-layouts: 200 us -> 10.2 us
  Pallas kernels: 0 us -> 105 us
  blocking collectives: 57.6 us -> 0 us
  matrix products: 32.4 us -> 0 us
  between operations: 14.5 us -> 1.02 us
    scatter-add x4 -> x0, other arithmetic: 301 us -> none  [the longest x3 297 us: on_device(): table = table.at[index_block.reshape(-1)].add(dpieces.reshape(-1, chans))]
    gather x4 -> x1, local copies, waits for them, and re-layouts: 196 us -> 2.17 us  [on_device(): features[jnp.minimum(send_rows, voxels - 1)]]
    pallas_call x0 -> x5, Pallas kernels: none -> 105 us  [the longest x3 52.8 us: scatter(): pl.pallas_call(functools.partial(scatter_kernel, first, has_before), out_...]
    psum x1 -> x0, blocking collectives: 57.6 us -> none  [on_device(): lax.psum((conv_part, head_part), ('tx', 'ty', 'rep'))]
    dot_general x12 -> x0, matrix products: 32.4 us -> none  [the longest x3 15.2 us: on_device(): jnp.einsum('vd,kcd->kvc', dpre, weights, preferred_element_type=jnp.float32)]
    ppermute x8 -> x12, starting transfers between devices: 23.2 us -> 19 us  [the longest x4 11 us: swap_edges(): first = lax.ppermute(jnp.where(odd, down, up), axis, even_pairs)]
  transfers between devices with their start and end apart: 9 -> 12, of which waited for: 1 -> 3; matrix products, arithmetic and copies ran while one was open for 48% -> 3% of each run, Pallas kernels for 0% -> 37%
where the time goes in v1:
time: 149 us; the launch traced here: 148 us
  Pallas kernels  105 us (70%)
  starting transfers between devices  19 us (13%)
  local copies, waits for them, and re-layouts  10.2 us (7%)
  waiting for transfers between devices  6.78 us (5%)
  other arithmetic  6.3 us (4%)
    pallas_call x3, Pallas kernels, scatter(): pl.pallas_call(functools.partial(scatter_kernel, first, has_before), out_...  52.8 us
    pallas_call x1, Pallas kernels, forward(): pl.pallas_call(functools.partial(forward_kernel, classes), out_shape=(jax...  49.6 us
    ppermute x4, starting transfers between devices, swap_edges(): first = lax.ppermute(jnp.where(odd, down, up), axis, even_pairs)  11 us
    ppermute x6, starting transfers between devices, exchange(): lax.ppermute(shard, axis, [(i, i ^ distance) for i in range(devices)])  6.75 us
    ppermute x4, waiting for transfers between devices, swap_edges(): first = lax.ppermute(jnp.where(odd, down, up), axis, even_pairs)  4.33 us
    slice x4, local copies, waits for them, and re-layouts, scatter_beside(): weights_t[first * chans:last * chans]  3.49 us
  transfers between devices with their start and end apart: 12, of which 3 were waited for; matrix products, arithmetic and copies ran while one was open for 3% of the time, Pallas kernels for 37%

profile of v1, /device:TPU:0, one launch (start us, length us, event | category | flops | bytes accessed | tf_op | source)
XLA Modules:
  0.0 148.5 jit_solution(14702521469809295760)
XLA Ops:
  0.7 0.8 fusion.1
  1.5 0.7 broadcast_compare_fusion
  2.2 2.2 %gather_fusion = bf16[512,128]{1,0:T(8,128)(2,1)S(1)} fusion(bf16[2048,128]{1,0:T(8,128)(2,1)} %own_ref.1, s32[1024]{0:T(1024)S(1)} %pad_clamp_fusion), kind=kCustom, calls=%fused_computation | custom fusion | bytes 264192 | tf_op jit(solution)/shard_map/gather | solution.py:243
  4.5 3.1 %collective-permute-start = (bf16[128,128]{1,0:T(8,128)(2,1)S(1)}, bf16[128,128]{1,0:T(8,128)(2,1)S(1)}, u32[]{:S(2)}, u32[]{:S(2)}) collective-permute-start(bf16[128,128]{1,0:T(8,128)(2,1)S(1)} %get-tuple-element.44), channel_id=1, source_target_pairs={{0,4},{4,0},{8,12},{12,8},{1,5},{5,1},{9,13},{13,9},{2,6},{6,2},{1... | collective-permute-start | bytes 98312 | tf_op jit(solution)/shard_map/ppermute | solution.py:225
  7.6 0.7 collective-permute-start.1
  8.3 1.6 %collective-permute-start.2 = (bf16[128,128]{1,0:T(8,128)(2,1)S(1)}, bf16[128,128]{1,0:T(8,128)(2,1)S(1)}, u32[]{:S(2)}, u32[]{:S(2)}) collective-permute-start(bf16[128,128]{1,0:T(8,128)(2,1)S(1)} %get-tuple-element.43), channel_id=1, source_target_pairs={{0,2},{2,0},{1,3},{3,1},{4,6},{6,4},{5,7},{7,5},{8,10},{10,8},{9,1... | collective-permute-start | bytes 98312 | tf_op jit(solution)/shard_map/ppermute | solution.py:225
  10.1 2.1 %collective-permute-done.2 = bf16[128,128]{1,0:T(8,128)(2,1)S(1)} collective-permute-done((bf16[128,128]{1,0:T(8,128)(2,1)S(1)}, bf16[128,128]{1,0:T(8,128)(2,1)S(1)}, u32[]{:S(2)}, u32[]{:S(2)}) %collective-permute-start.2) | collective-permute-done | bytes 32800 | tf_op jit(solution)/shard_map/ppermute | solution.py:225
  12.3 49.6 %forward.1 = (f32[2048,128]{1,0:T(8,128)S(1)}, f32[2048,128]{1,0:T(8,128)S(1)}, f32[3520,128]{1,0:T(8,128)S(1)}) custom-call(s32[55296]{0:T(1024)S(1)} %reshape.44.map_hbm, bf16[2048,128]{1,0:T(8,128)(2,1)S(1)} %copy-done.2, bf16[128,128]{1,0:T(8,128)(2,1)S(1)} %get-tuple-element.49.halo_refs_0_, bf16[128,128]{1,0:T(8,128)(2,1)S(1)} %get-tuple-element.48.halo_refs_1_, ...), custom_call_target="tpu_custom_call" | custom-call | flops 3623878656 | bytes 157286400 | tf_op jit(solution)/shard_map/forward/pallas_call | solution.py:106
  62.1 2.4 %collective-permute-done.3 = f32[1760,128]{1,0:T(8,128)S(1)} collective-permute-done((f32[1760,128]{1,0:T(8,128)S(1)}, f32[1760,128]{1,0:T(8,128)S(1)}, u32[]{:S(2)}, u32[]{:S(2)}) %collective-permute-start.3) | collective-permute-done | bytes 901152 | tf_op jit(solution)/shard_map/ppermute | solution.py:217
  64.7 0.7 select_convert_fusion
  65.4 1.5 collective-permute-start.4
  66.9 0.9 fusion.2
  67.8 1.2 copy.13
  69.0 17.6 %scatter_0.1.refs_0_ = f32[2592,128]{1,0:T(8,128)S(1)} custom-call(s32[55296]{0:T(1024)S(1)} %reshape.44.map_hbm, f32[2048,128]{1,0:T(8,128)S(1)} %get-tuple-element.33.dpre_ref, bf16[1152,128]{1,0:T(8,128)(2,1)S(1)} %bitcast.22), custom_call_target="tpu_custom_call" | custom-call | flops 603979776 | bytes 41943040 | tf_op jit(solution)/shard_map/scatter_0/pallas_call | solution.py:173
  86.6 1.1 copy-done
  87.7 1.0 add_convert_fusion.1
  88.7 3.9 %collective-permute-start.5 = (bf16[880,128]{1,0:T(8,128)(2,1)S(1)}, bf16[880,128]{1,0:T(8,128)(2,1)}, u32[]{:S(2)}, u32[]{:S(2)}) collective-permute-start(bf16[880,128]{1,0:T(8,128)(2,1)S(1)} %add_convert_fusion.1), channel_id=1, source_target_pairs={{0,8},{4,12},{8,0},{12,4},{1,9},{5,13},{9,1},{13,5},{2,10},{6,14},... | collective-permute-start | bytes 675848 | tf_op jit(solution)/shard_map/ppermute | solution.py:217
  92.8 1.3 copy-done.1
  94.1 17.6 %scatter_9.1.refs_0_ = f32[2592,128]{1,0:T(8,128)S(1)} custom-call(s32[55296]{0:T(1024)S(1)} %reshape.44.map_hbm, f32[2048,128]{1,0:T(8,128)S(1)} %get-tuple-element.33.dpre_ref, bf16[1152,128]{1,0:T(8,128)(2,1)S(1)} %bitcast.21, f32[2592,128]{1,0:T(8,128)S(1)} %copy-done.1), custom_call_target="tpu_custom_call" | custom-call | flops 603979776 | bytes 41943040 | tf_op jit(solution)/shard_map/scatter_9/pallas_call | solution.py:173
  111.8 1.1 convert_add_fusion
  112.9 0.7 collective-permute-start.6
  113.6 1.2 copy.15
  114.7 17.6 %scatter_18.1.dext_ref = f32[2592,128]{1,0:T(8,128)S(1)} custom-call(s32[55296]{0:T(1024)S(1)} %reshape.44.map_hbm, f32[2048,128]{1,0:T(8,128)S(1)} %get-tuple-element.33.dpre_ref, bf16[1152,128]{1,0:T(8,128)(2,1)S(1)} %bitcast.20, f32[2592,128]{1,0:T(8,128)S(1)} %scatter_9.1.refs_0_), custom_call_target="tpu_custom_call" | custom-call | flops 603979776 | bytes 41943040 | tf_op jit(solution)/shard_map/scatter_18/pallas_call | solution.py:173
  132.4 1.1 add_convert_fusion
  133.5 0.6 collective-permute-start.10
  134.1 0.7 collective-permute-start.7
  134.8 4.8 %collective-permute-start.8 = (bf16[128,128]{1,0:T(8,128)(2,1)S(1)}, bf16[128,128]{1,0:T(8,128)(2,1)S(1)}, u32[]{:S(2)}, u32[]{:S(2)}) collective-permute-start(bf16[128,128]{1,0:T(8,128)(2,1)S(1)} %get-tuple-element.42), channel_id=1, source_target_pairs={{0,4},{4,0},{8,12},{12,8},{1,5},{5,1},{9,13},{13,9},{2,6},{6,2},{1... | collective-permute-start | bytes 98312 | tf_op jit(solution)/shard_map/ppermute | solution.py:225
  139.6 1.5 %collective-permute-start.9 = (bf16[128,128]{1,0:T(8,128)(2,1)S(1)}, bf16[128,128]{1,0:T(8,128)(2,1)S(1)}, u32[]{:S(2)}, u32[]{:S(2)}) collective-permute-start(bf16[128,128]{1,0:T(8,128)(2,1)S(1)} %get-tuple-element.41), channel_id=1, source_target_pairs={{0,2},{2,0},{1,3},{3,1},{4,6},{6,4},{5,7},{7,5},{8,10},{10,8},{9,1... | collective-permute-start | bytes 98312 | tf_op jit(solution)/shard_map/ppermute | solution.py:225
  141.3 2.2 %collective-permute-done.9 = bf16[128,128]{1,0:T(8,128)(2,1)S(1)} collective-permute-done((bf16[128,128]{1,0:T(8,128)(2,1)S(1)}, bf16[128,128]{1,0:T(8,128)(2,1)S(1)}, u32[]{:S(2)}, u32[]{:S(2)}) %collective-permute-start.9) | collective-permute-done | bytes 32800 | tf_op jit(solution)/shard_map/ppermute | solution.py:225
  143.6 2.7 %finish.1 = f32[2048,128]{1,0:T(8,128)} custom-call(f32[2048,128]{1,0:T(8,128)S(1)} %copy-done.4, f32[2592,128]{1,0:T(8,128)S(1)} %scatter_18.1.dext_ref, s32[1,512]{1,0:T(1,128)S(1)} %bitcast.25, bf16[512,128]{1,0:T(8,128)(2,1)S(1)} %pad_maximum_fusion.back_ref), custom_call_target="tpu_custom_call" | custom-call | flops 268435456 | bytes 4194304 | tf_op jit(solution)/shard_map/finish/pallas_call | solution.py:204
  146.6 1.3 slice.105
  147.9 0.6 slice_bitcast_fusion
  (54 shorter events, 1.5 us)
Async XLA Ops:
  0.6 11.7 %copy-start.2 = (bf16[2048,128]{1,0:T(8,128)(2,1)S(1)}, bf16[2048,128]{1,0:T(8,128)(2,1)}, u32[]{:S(2)}) copy-start(bf16[2048,128]{1,0:T(8,128)(2,1)} %own_ref.1) | copy-start | bytes 1572868
  0.6 9.2 %copy-start.9 = (s32[27,2048]{1,0:T(8,128)S(1)}, s32[27,2048]{1,0:T(8,128)}, u32[]{:S(2)}) copy-start(s32[27,2048]{1,0:T(8,128)} %param.10) | copy-start | bytes 663556
  0.7 9.3 %copy-start.10 = (s32[2048]{0:T(1024)S(1)}, s32[2048]{0:T(1024)}, u32[]{:S(2)}) copy-start(s32[2048]{0:T(1024)} %param.11) | copy-start | bytes 24580
  0.7 9.4 %copy-start.11 = (bf16[128,19]{0,1:T(8,128)(2,1)S(1)}, bf16[128,19]{0,1:T(8,128)(2,1)}, u32[]{:S(2)}) copy-start(bf16[128,19]{0,1:T(8,128)(2,1)} %param.8) | copy-start | bytes 14596
  0.7 11.6 %copy-start.5 = (bf16[27,128,128]{2,1,0:T(8,128)(2,1)S(1)}, bf16[27,128,128]{2,1,0:T(8,128)(2,1)}, u32[]{:S(2)}) copy-start(bf16[27,128,128]{2,1,0:T(8,128)(2,1)} %param.7) | copy-start | bytes 2654212
  4.5 7.7 %collective-permute-start = (bf16[128,128]{1,0:T(8,128)(2,1)S(1)}, bf16[128,128]{1,0:T(8,128)(2,1)S(1)}, u32[]{:S(2)}, u32[]{:S(2)}) collective-permute-start(bf16[128,128]{1,0:T(8,128)(2,1)S(1)} %get-tuple-element.44), channel_id=1, source_target_pairs={{0,4},{4,0},{8,12},{12,8},{1,5},{5,1},{9,13},{13,9},{2,6},{6,2},{1... | collective-permute-start | bytes 98312 | tf_op jit(solution)/shard_map/ppermute | solution.py:225
  7.6 4.7 %collective-permute-start.1 = (bf16[128,128]{1,0:T(8,128)(2,1)S(1)}, bf16[128,128]{1,0:T(8,128)(2,1)S(1)}, u32[]{:S(2)}, u32[]{:S(2)}) collective-permute-start(bf16[128,128]{1,0:T(8,128)(2,1)S(1)} %get-tuple-element.45), channel_id=1, source_target_pairs={{4,8},{8,4},{5,9},{9,5},{6,10},{10,6},{7,11},{11,7},{20,24},{24,20... | collective-permute-start | bytes 98312 | tf_op jit(solution)/shard_map/ppermute | solution.py:227
  8.3 4.0 %collective-permute-start.2 = (bf16[128,128]{1,0:T(8,128)(2,1)S(1)}, bf16[128,128]{1,0:T(8,128)(2,1)S(1)}, u32[]{:S(2)}, u32[]{:S(2)}) collective-permute-start(bf16[128,128]{1,0:T(8,128)(2,1)S(1)} %get-tuple-element.43), channel_id=1, source_target_pairs={{0,2},{2,0},{1,3},{3,1},{4,6},{6,4},{5,7},{7,5},{8,10},{10,8},{9,1... | collective-permute-start | bytes 98312 | tf_op jit(solution)/shard_map/ppermute | solution.py:225
  61.9 2.8 %copy-start.3 = (f32[2048,128]{1,0:T(8,128)}, f32[2048,128]{1,0:T(8,128)S(1)}, u32[]{:S(2)}) copy-start(f32[2048,128]{1,0:T(8,128)S(1)} %get-tuple-element.20.dmixed_ref) | copy-start | bytes 3145732
  62.0 2.5 %collective-permute-start.3 = (f32[1760,128]{1,0:T(8,128)S(1)}, f32[1760,128]{1,0:T(8,128)S(1)}, u32[]{:S(2)}, u32[]{:S(2)}) collective-permute-start(f32[1760,128]{1,0:T(8,128)S(1)} %slice_select_fusion), channel_id=1, source_target_pairs={{0,1},{1,0},{2,3},{3,2},{4,5},{5,4},{6,7},{7,6},{8,9},{9,8},{10,11... | collective-permute-start | bytes 2703368 | tf_op jit(solution)/shard_map/ppermute | solution.py:217
  65.4 22.2 %collective-permute-start.4 = (bf16[880,128]{1,0:T(8,128)(2,1)}, bf16[880,128]{1,0:T(8,128)(2,1)}, u32[]{:S(2)}, u32[]{:S(2)}) collective-permute-start(bf16[880,128]{1,0:T(8,128)(2,1)} %select_convert_fusion), channel_id=1, source_target_pairs={{0,2},{2,0},{1,3},{3,1},{4,6},{6,4},{5,7},{7,5},{8,10},{10,8},{9,1... | collective-permute-start | bytes 675848 | tf_op jit(solution)/shard_map/ppermute | solution.py:217
  69.0 23.6 %copy-start.7 = (bf16[9,128,128]{1,2,0:T(8,128)(2,1)S(1)}, bf16[9,128,128]{1,2,0:T(8,128)(2,1)}, u32[]{:S(2)}) copy-start(bf16[9,128,128]{1,2,0:T(8,128)(2,1)} %get-tuple-element.38) | copy-start | bytes 884740
  86.6 1.1 copy-start
  88.7 23.1 %copy-start.8 = (bf16[880,128]{1,0:T(8,128)(2,1)}, bf16[880,128]{1,0:T(8,128)(2,1)S(1)}, u32[]{:S(2)}) copy-start(bf16[880,128]{1,0:T(8,128)(2,1)S(1)} %add_convert_fusion.1) | copy-start | bytes 675844
  88.7 23.1 %collective-permute-start.5 = (bf16[880,128]{1,0:T(8,128)(2,1)S(1)}, bf16[880,128]{1,0:T(8,128)(2,1)}, u32[]{:S(2)}, u32[]{:S(2)}) collective-permute-start(bf16[880,128]{1,0:T(8,128)(2,1)S(1)} %add_convert_fusion.1), channel_id=1, source_target_pairs={{0,8},{4,12},{8,0},{12,4},{1,9},{5,13},{9,1},{13,5},{2,10},{6,14},... | collective-permute-start | bytes 675848 | tf_op jit(solution)/shard_map/ppermute | solution.py:217
  92.8 1.3 copy-start.1
  112.9 19.5 %collective-permute-start.6 = (f32[880,128]{1,0:T(8,128)S(1)}, f32[880,128]{1,0:T(8,128)}, u32[]{:S(2)}, u32[]{:S(2)}) collective-permute-start(f32[880,128]{1,0:T(8,128)S(1)} %convert_add_fusion), channel_id=1, source_target_pairs={{0,4},{4,0},{8,12},{12,8},{1,5},{5,1},{9,13},{13,9},{2,6},{6,2},{1... | collective-permute-start | bytes 1351688 | tf_op jit(solution)/shard_map/ppermute | solution.py:217
  133.5 10.1 %copy-start.4 = (f32[2048,128]{1,0:T(8,128)S(1)}, f32[2048,128]{1,0:T(8,128)}, u32[]{:S(2)}) copy-start(f32[2048,128]{1,0:T(8,128)} %copy-done.3) | copy-start | bytes 3145732
  133.5 10.1 %copy-start.6 = (s32[4,128]{1,0:T(4,128)S(1)}, s32[4,128]{1,0:T(4,128)}, u32[]{:S(2)}) copy-start(s32[4,128]{1,0:T(4,128)} %param.9) | copy-start | bytes 6148
  133.5 7.6 %collective-permute-start.10 = (bf16[880,128]{1,0:T(8,128)(2,1)S(1)}, bf16[880,128]{1,0:T(8,128)(2,1)S(1)}, u32[]{:S(2)}, u32[]{:S(2)}) collective-permute-start(bf16[880,128]{1,0:T(8,128)(2,1)S(1)} %add_convert_fusion), channel_id=1, source_target_pairs={{0,2},{2,0},{1,3},{3,1},{4,6},{6,4},{5,7},{7,5},{8,10},{10,8},{9,1... | collective-permute-start | bytes 675848 | tf_op jit(solution)/shard_map/ppermute | solution.py:217
  134.1 9.4 %collective-permute-start.7 = (bf16[128,128]{1,0:T(8,128)(2,1)S(1)}, bf16[128,128]{1,0:T(8,128)(2,1)S(1)}, u32[]{:S(2)}, u32[]{:S(2)}) collective-permute-start(bf16[128,128]{1,0:T(8,128)(2,1)S(1)} %get-tuple-element.40), channel_id=1, source_target_pairs={{4,8},{8,4},{5,9},{9,5},{6,10},{10,6},{7,11},{11,7},{20,24},{24,20... | collective-permute-start | bytes 98312 | tf_op jit(solution)/shard_map/ppermute | solution.py:227
  134.8 8.7 %collective-permute-start.8 = (bf16[128,128]{1,0:T(8,128)(2,1)S(1)}, bf16[128,128]{1,0:T(8,128)(2,1)S(1)}, u32[]{:S(2)}, u32[]{:S(2)}) collective-permute-start(bf16[128,128]{1,0:T(8,128)(2,1)S(1)} %get-tuple-element.42), channel_id=1, source_target_pairs={{0,4},{4,0},{8,12},{12,8},{1,5},{5,1},{9,13},{13,9},{2,6},{6,2},{1... | collective-permute-start | bytes 98312 | tf_op jit(solution)/shard_map/ppermute | solution.py:225
  139.6 3.9 %collective-permute-start.9 = (bf16[128,128]{1,0:T(8,128)(2,1)S(1)}, bf16[128,128]{1,0:T(8,128)(2,1)S(1)}, u32[]{:S(2)}, u32[]{:S(2)}) collective-permute-start(bf16[128,128]{1,0:T(8,128)(2,1)S(1)} %get-tuple-element.41), channel_id=1, source_target_pairs={{0,2},{2,0},{1,3},{3,1},{4,6},{6,4},{5,7},{7,5},{8,10},{10,8},{9,1... | collective-permute-start | bytes 98312 | tf_op jit(solution)/shard_map/ppermute | solution.py:225
  141.3 5.1 %collective-permute-start.11 = (bf16[1760,128]{1,0:T(8,128)(2,1)S(1)}, bf16[1760,128]{1,0:T(8,128)(2,1)S(1)}, u32[]{:S(2)}, u32[]{:S(2)}) collective-permute-start(bf16[1760,128]{1,0:T(8,128)(2,1)S(1)} %maximum_select_fusion.1), channel_id=1, source_target_pairs={{0,1},{1,0},{2,3},{3,2},{4,5},{5,4},{6,7},{7,6},{8,9},{9,8},{10,11... | collective-permute-start | bytes 1351688 | tf_op jit(solution)/shard_map/ppermute | solution.py:217

commit v2 on v1

--- a/solution.py
+++ b/solution.py
@@ -9,6 +9,7 @@
 from jax.sharding import PartitionSpec as P
 
 STREAMS = 4
+SCATTER_STREAMS = 8
 SEGMENT = 64
 GAP = 16
 CHUNKS = 3
@@ -24,26 +25,33 @@
     return lax.dot_general(a, b, dims, preferred_element_type=jnp.float32)
 
 
-def fetch(map_hbm, index, sems, first, length):
-    copies = []
-    for n, ref in enumerate(index):
-        copy = pltpu.make_async_copy(
-            map_hbm.at[pl.ds((first + n) * length, length)], ref, sems.at[n]
-        )
-        copy.start()
-        copies.append(copy)
-    return copies
+def fetch(map_hbm, index, sems, first, length, parts):
+    stages = []
+    for part, (start, stop) in enumerate(zip(parts[:-1], parts[1:])):
+        stage = []
+        for n, ref in enumerate(index):
+            at = (first + n) * length + start
+            stage.append(
+                pltpu.make_async_copy(
+                    map_hbm.at[pl.ds(at, stop - start)], ref.at[pl.ds(start, stop - start)],
+                    sems.at[part, n],
+                )
+            )
+        for copy in stage:
+            copy.start()
+        stages.append(stage)
+    return stages
 
 
 def forward_kernel(
     classes, map_hbm, own_ref, halo_refs, weight_ref, class_ref, label_ref,
-    dpre_ref, dmixed_ref, conv_ref, table, rows, wide, total, sems, *index,
+    dpre_ref, dmixed_ref, conv_ref, flipped_ref, table, rows, wide, total, sems, *index,
 ):
     voxels, chans = dpre_ref.shape
     offsets = len(index) // STREAMS
     stream = voxels // STREAMS
     block = STREAMS * SEGMENT
-    copies = fetch(map_hbm, index, sems, 0, stream)
+    ready, later = fetch(map_hbm, index, sems, 0, stream, (0, 128, stream))
     width = halo_refs[0].shape[0]
     table[:voxels, :] = own_ref[...].astype(jnp.float32)
     table[voxels : voxels + GAP, :] = jnp.zeros((GAP, chans), jnp.float32)
@@ -54,10 +62,18 @@
     conv_ref[pl.ds(offsets * chans, conv_ref.shape[0] - offsets * chans), :] = jnp.zeros(
         (conv_ref.shape[0] - offsets * chans, chans), jnp.float32
     )
-    for copy in copies:
+    for k in range(offsets):
+        at = slice(k * chans, (k + 1) * chans)
+        flipped_ref[at, :] = weight_ref[at, :].T
+    for copy in ready:
         copy.wait()
 
     def block_step(b, carry):
+        @pl.when(b == 128 // SEGMENT)
+        def _():
+            for copy in later:
+                copy.wait()
+
         def gather_step(i, carry):
             at = i - b * SEGMENT
             for u in range(STREAMS):
@@ -109,15 +125,16 @@
             jax.ShapeDtypeStruct((voxels, chans), jnp.float32),
             jax.ShapeDtypeStruct((voxels, chans), jnp.float32),
             jax.ShapeDtypeStruct((reduce_rows, chans), jnp.float32),
+            jax.ShapeDtypeStruct(weights.shape, jnp.bfloat16),
         ),
         in_specs=[HBM, VMEM, [VMEM] * 4, VMEM, VMEM, VMEM],
-        out_specs=(VMEM, VMEM, VMEM),
+        out_specs=(VMEM, VMEM, VMEM, VMEM),
         scratch_shapes=[
             pltpu.VMEM((table_rows, chans), jnp.float32),
             pltpu.VMEM((offsets, block, chans), jnp.float32),
             pltpu.VMEM((block, offsets * chans), jnp.bfloat16),
             pltpu.VMEM((chans, offsets * chans), jnp.float32),
-            pltpu.SemaphoreType.DMA((offsets * STREAMS,)),
+            pltpu.SemaphoreType.DMA((2, offsets * STREAMS)),
         ]
         + [pltpu.SMEM((stream,), jnp.int32)] * (offsets * STREAMS),
         compiler_params=pltpu.CompilerParams(vmem_limit_bytes=40 << 20),
@@ -128,62 +145,63 @@
     )(map_flat, features, incoming, weights, class_t, label_blocks)
 
 
-def scatter_kernel(first, has_before, map_hbm, dpre_ref, weight_ref, *refs):
+def scatter_kernel(first, offsets, has_before, map_hbm, dpre_ref, weight_ref, *refs):
     refs = list(refs)
     before = refs.pop(0) if has_before else None
     out_ref, sems = refs[0], refs[1]
-    offsets = weight_ref.shape[0] // weight_ref.shape[1]
     tables = refs[2 : 2 + offsets]
     index = refs[2 + offsets :]
     voxels, chans = dpre_ref.shape
-    stream = voxels // STREAMS
-    copies = fetch(map_hbm, index, sems, first * STREAMS, stream)
+    stream = voxels // SCATTER_STREAMS
+    ready, later = fetch(map_hbm, index, sems, first * SCATTER_STREAMS, stream, (0, 128, stream))
     for table in tables:
         table[...] = jnp.zeros_like(table)
-    for copy in copies:
+    for copy in ready:
         copy.wait()
 
     def step(i, carry):
-        for u in range(STREAMS):
+        for u in range(SCATTER_STREAMS):
             row = dpre_ref[pl.ds(u * stream + i, 1), :]
             for k in range(offsets):
-                at = pl.ds(index[k * STREAMS + u][i], 1)
+                at = pl.ds(index[k * SCATTER_STREAMS + u][i], 1)
                 tables[k][at, :] = tables[k][at, :] + row
         return carry
 
-    lax.fori_loop(0, stream, step, 0)
+    lax.fori_loop(0, 128, step, 0)
+    for copy in later:
+        copy.wait()
+    lax.fori_loop(128, stream, step, 0)
     tiles = 3
     height = out_ref.shape[0] // tiles
 
     def finish(t, carry):
         at = pl.ds(pl.multiple_of(t * height, 16), height)
         wide = jnp.concatenate([table[at, :].astype(jnp.bfloat16) for table in tables], axis=1)
-        result = dot(wide, weight_ref[...], NN)
+        result = dot(wide, weight_ref[first * chans : (first + offsets) * chans, :], NN)
         out_ref[at, :] = result + before[at, :] if has_before else result
         return carry
 
     lax.fori_loop(0, tiles, finish, 0)
 
 
-def scatter(map_flat, dpre, weights_t, before, first, table_rows):
+def scatter(map_flat, dpre, flipped, before, first, offsets, table_rows):
     voxels, chans = dpre.shape
-    offsets = weights_t.shape[0] // chans
-    stream = voxels // STREAMS
+    stream = voxels // SCATTER_STREAMS
     has_before = before is not None
     return pl.pallas_call(
-        functools.partial(scatter_kernel, first, has_before),
+        functools.partial(scatter_kernel, first, offsets, has_before),
         out_shape=jax.ShapeDtypeStruct((table_rows, chans), jnp.float32),
         in_specs=[HBM, VMEM, VMEM] + ([VMEM] if has_before else []),
         out_specs=VMEM,
-        scratch_shapes=[pltpu.SemaphoreType.DMA((offsets * STREAMS,))]
+        scratch_shapes=[pltpu.SemaphoreType.DMA((2, offsets * SCATTER_STREAMS))]
         + [pltpu.VMEM((table_rows, chans), jnp.float32)] * offsets
-        + [pltpu.SMEM((stream,), jnp.int32)] * (offsets * STREAMS),
+        + [pltpu.SMEM((stream,), jnp.int32)] * (offsets * SCATTER_STREAMS),
         compiler_params=pltpu.CompilerParams(vmem_limit_bytes=40 << 20),
         cost_estimate=pl.CostEstimate(
             flops=2 * voxels * offsets * chans * chans, bytes_accessed=40 << 20, transcendentals=0
         ),
         name=f"scatter_{first}",
-    )(map_flat, dpre, weights_t, *([before] if has_before else []))
+    )(map_flat, dpre, flipped, *([before] if has_before else []))
 
 
 def finish_kernel(dmixed_ref, dext_ref, send_ref, back_ref, out_ref):
@@ -247,13 +265,12 @@
 
     map_flat = jnp.where(neighbour_map > voxels, neighbour_map + (GAP - 1), neighbour_map).reshape(-1)
     weights = conv_weight.reshape(offsets * chans, chans)
-    weights_t = conv_weight.transpose(0, 2, 1).reshape(offsets * chans, chans)
     class_t = jnp.pad(classifier.T, ((0, HEAD_ROWS - classes), (0, 0)))
     label_blocks = (
         labels.reshape(STREAMS, voxels // block, SEGMENT).transpose(1, 0, 2)
         .reshape(voxels // block, 1, block)
     )
-    dpre, dmixed, part = forward(
+    dpre, dmixed, part, flipped = forward(
         map_flat, features, [low_x, high_x, low_y, high_y], weights, class_t, label_blocks,
         classes, reduce_rows, table_rows,
     )
@@ -270,8 +287,8 @@
         held = (sent, dpre) if before is None else (sent, dpre, before)
         held = lax.optimization_barrier(held)
         return held[0], scatter(
-            map_flat, held[1], weights_t[first * chans : last * chans],
-            None if before is None else held[2], first, table_rows,
+            map_flat, held[1], flipped, None if before is None else held[2],
+            first, last - first, table_rows,
         )
 
     halved = []
@@ -303,10 +320,9 @@
     total = part.astype(jnp.bfloat16)
     for axis, distance in reversed(halved):
         upper = (lax.axis_index(axis) & distance) != 0
-        got = exchange(total, axis, distance)
-        total = jnp.where(
-            upper, jnp.concatenate([got, total], axis=0), jnp.concatenate([total, got], axis=0)
-        )
+        total_before, got = total, exchange(total, axis, distance)
+        low, high = jnp.where(upper, got, total), jnp.where(upper, total, got)
+        total = jnp.concatenate([low, high], axis=0)
 
     start = voxels + GAP
     halo = dext[start : start + 4 * width].astype(jnp.bfloat16).reshape(4, width, chans)
@@ -317,9 +333,12 @@
 
     count = voxels * lax.axis_size("tx") * lax.axis_size("ty") * lax.axis_size("rep")
     scale = 1.0 / math.sqrt(count)
-    total = total.astype(jnp.float32) * scale
-    grad_conv = total[: offsets * chans].reshape(offsets, chans, chans)
-    grad_head = total[offsets * chans : offsets * chans + classes].T
+    split = offsets * chans - low.shape[0]
+    grad_conv = jnp.concatenate([low, high[:split]], axis=0).astype(jnp.float32) * scale
+    grad_conv = grad_conv.reshape(offsets, chans, chans)
+    grad_head = jnp.where(
+        upper, total_before[split : split + classes], got[split : split + classes]
+    ).T.astype(jnp.float32) * scale
     return grad_input, grad_conv, grad_head
 
 

time: 149 us -> 135 us (0.906)
  local copies, waits for them, and re-layouts: 10.2 us -> 2.41 us
  Pallas kernels: 105 us -> 103 us
  other arithmetic: 6.3 us -> 4.49 us
    slice x5 -> x0, local copies, waits for them, and re-layouts: 4.81 us -> none  [the longest x4 3.49 us: scatter_beside(): weights_t[first * chans:last * chans]]
    ppermute x4, starting transfers between devices: 11 us -> 8.45 us  [swap_edges(): first = lax.ppermute(jnp.where(odd, down, up), axis, even_pairs)]
    ppermute x4, waiting for transfers between devices: 4.33 us -> 1.85 us  [swap_edges(): first = lax.ppermute(jnp.where(odd, down, up), axis, even_pairs)]
    unnamed x24 -> x12, local copies, waits for them, and re-layouts: 2.43 us -> 0.03 us
    ppermute x6, starting transfers between devices: 6.75 us -> 8.47 us  [exchange(): lax.ppermute(shard, axis, [(i, i ^ distance) for i in range(devices)])]
    mul x1 -> x2, other arithmetic: 0.23 us -> 1.95 us  [the longest x1 1.34 us: on_device(): jnp.concatenate([low, high[:split]], axis=0).astype(jnp.float32) * scale]
  transfers between devices with their start and end apart: 12 -> 12, of which waited for: 3 -> 5; matrix products, arithmetic and copies ran while one was open for 3% -> 0% of each run, Pallas kernels for 37% -> 41%
where the time goes in v2:
time: 135 us
  Pallas kernels  103 us (76%)
  starting transfers between devices  18.2 us (13%)
  waiting for transfers between devices  5.52 us (4%)
  other arithmetic  4.49 us (3%)
  local copies, waits for them, and re-layouts  2.41 us (2%)
    pallas_call x3, Pallas kernels, scatter(): pl.pallas_call(functools.partial(scatter_kernel, first, offsets, has_befo...  52.3 us
    pallas_call x1, Pallas kernels, forward(): pl.pallas_call(functools.partial(forward_kernel, classes), out_shape=(jax...  48.5 us
    ppermute x6, starting transfers between devices, exchange(): lax.ppermute(shard, axis, [(i, i ^ distance) for i in range(devices)])  8.47 us
    ppermute x4, starting transfers between devices, swap_edges(): first = lax.ppermute(jnp.where(odd, down, up), axis, even_pairs)  8.45 us
    ppermute x6, waiting for transfers between devices, exchange(): lax.ppermute(shard, axis, [(i, i ^ distance) for i in range(devices)])  3.66 us
    pallas_call x1, Pallas kernels, finish(): pl.pallas_call(finish_kernel, out_shape=jax.ShapeDtypeStruct(dmixed.shape...  2.72 us
  transfers between devices with their start and end apart: 12, of which 5 were waited for; matrix products, arithmetic and copies ran while one was open for 0% of the time, Pallas kernels for 41%

profile of v2, /device:TPU:0, one launch (start us, length us, event | category | flops | bytes accessed | tf_op | source)
XLA Modules:
  0.0 135.1 jit_solution(16825855714676558445)
XLA Ops:
  0.7 0.8 broadcast_compare_fusion
  1.5 0.7 fusion.3
  2.2 2.2 %gather_fusion = bf16[512,128]{1,0:T(8,128)(2,1)S(1)} fusion(bf16[2048,128]{1,0:T(8,128)(2,1)} %own_ref.1, s32[1024]{0:T(1024)S(1)} %pad_clamp_fusion), kind=kCustom, calls=%fused_computation | custom fusion | bytes 264192 | tf_op jit(solution)/shard_map/gather | solution.py:261
  4.4 0.1 broadcast_select_fusion.3
  4.5 3.0 %collective-permute-start.2 = (bf16[128,128]{1,0:T(8,128)(2,1)S(1)}, bf16[128,128]{1,0:T(8,128)(2,1)S(1)}, u32[]{:S(2)}, u32[]{:S(2)}) collective-permute-start(bf16[128,128]{1,0:T(8,128)(2,1)S(1)} %get-tuple-element.44), channel_id=1, source_target_pairs={{0,2},{2,0},{1,3},{3,1},{4,6},{6,4},{5,7},{7,5},{8,10},{10,8},{9,1... | collective-permute-start | bytes 98312 | tf_op jit(solution)/shard_map/ppermute | solution.py:243
  7.5 1.6 %collective-permute-start = (bf16[128,128]{1,0:T(8,128)(2,1)S(1)}, bf16[128,128]{1,0:T(8,128)(2,1)S(1)}, u32[]{:S(2)}, u32[]{:S(2)}) collective-permute-start(bf16[128,128]{1,0:T(8,128)(2,1)S(1)} %get-tuple-element.45), channel_id=1, source_target_pairs={{0,4},{4,0},{8,12},{12,8},{1,5},{5,1},{9,13},{13,9},{2,6},{6,2},{1... | collective-permute-start | bytes 98312 | tf_op jit(solution)/shard_map/ppermute | solution.py:243
  9.1 0.7 collective-permute-start.1
  9.9 0.1 reshape.45.label_ref
  10.1 1.4 %collective-permute-done = bf16[128,128]{1,0:T(8,128)(2,1)S(1)} collective-permute-done((bf16[128,128]{1,0:T(8,128)(2,1)S(1)}, bf16[128,128]{1,0:T(8,128)(2,1)S(1)}, u32[]{:S(2)}, u32[]{:S(2)}) %collective-permute-start) | collective-permute-done | bytes 32800 | tf_op jit(solution)/shard_map/ppermute | solution.py:243
  11.5 48.5 %forward.1 = (f32[2048,128]{1,0:T(8,128)S(1)}, f32[2048,128]{1,0:T(8,128)S(1)}, f32[3520,128]{1,0:T(8,128)S(1)}, bf16[3456,128]{1,0:T(8,128)(2,1)S(1)}) custom-call(s32[55296]{0:T(1024)S(1)} %reshape.42.map_hbm, bf16[2048,128]{1,0:T(8,128)(2,1)S(1)} %copy-done, bf16[128,128]{1,0:T(8,128)(2,1)S(1)} %get-tuple-element.50.halo_refs_0_, ...), custom_call_target="tpu_custom_call" | custom-call | flops 3623878656 | bytes 157286400 | tf_op jit(solution)/shard_map/forward/pallas_call | solution.py:122
  60.0 0.1 slice_select_fusion
  60.1 0.1 collective-permute-start.3
  60.2 2.4 %collective-permute-done.3 = f32[1760,128]{1,0:T(8,128)S(1)} collective-permute-done((f32[1760,128]{1,0:T(8,128)S(1)}, f32[1760,128]{1,0:T(8,128)S(1)}, u32[]{:S(2)}, u32[]{:S(2)}) %collective-permute-start.3) | collective-permute-done | bytes 901152 | tf_op jit(solution)/shard_map/ppermute | solution.py:235
  62.6 0.1 select_add_fusion
  62.8 0.1 collective-permute-start.4
  62.9 17.4 %scatter_0.1.refs_0_ = f32[2592,128]{1,0:T(8,128)S(1)} custom-call(s32[55296]{0:T(1024)S(1)} %reshape.42.map_hbm, f32[2048,128]{1,0:T(8,128)S(1)} %get-tuple-element.35.dpre_ref, bf16[3456,128]{1,0:T(8,128)(2,1)S(1)} %get-tuple-element.26.weight_ref), custom_call_target="tpu_custom_call" | custom-call | flops 603979776 | bytes 41943040 | tf_op jit(solution)/shard_map/scatter_0/pallas_call | solution.py:191
  80.4 6.6 %collective-permute-start.5 = (bf16[880,128]{1,0:T(8,128)(2,1)S(1)}, bf16[880,128]{1,0:T(8,128)(2,1)S(1)}, u32[]{:S(2)}, u32[]{:S(2)}) collective-permute-start(bf16[880,128]{1,0:T(8,128)(2,1)S(1)} %add_convert_fusion.1), channel_id=1, source_target_pairs={{0,8},{4,12},{8,0},{12,4},{1,9},{5,13},{9,1},{13,5},{2,10},{6,14},... | collective-permute-start | bytes 675848 | tf_op jit(solution)/shard_map/ppermute | solution.py:235
  87.0 17.4 %scatter_9.1.refs_0_ = f32[2592,128]{1,0:T(8,128)S(1)} custom-call(s32[55296]{0:T(1024)S(1)} %reshape.42.map_hbm, f32[2048,128]{1,0:T(8,128)S(1)} %get-tuple-element.35.dpre_ref, bf16[3456,128]{1,0:T(8,128)(2,1)S(1)} %get-tuple-element.26.weight_ref, f32[2592,128]{1,0:T(8,128)S(1)} %scatter_0.1.refs_0_), custom_call_target="tpu_custom_call" | custom-call | flops 603979776 | bytes 41943040 | tf_op jit(solution)/shard_map/scatter_9/pallas_call | solution.py:191
  104.5 0.1 collective-permute-start.6
  104.6 17.4 %scatter_18.1.dext_ref = f32[2592,128]{1,0:T(8,128)S(1)} custom-call(s32[55296]{0:T(1024)S(1)} %reshape.42.map_hbm, f32[2048,128]{1,0:T(8,128)S(1)} %get-tuple-element.35.dpre_ref, bf16[3456,128]{1,0:T(8,128)(2,1)S(1)} %get-tuple-element.26.weight_ref, f32[2592,128]{1,0:T(8,128)S(1)} %scatter_9.1.refs_0_), custom_call_target="tpu_custom_call" | custom-call | flops 603979776 | bytes 41943040 | tf_op jit(solution)/shard_map/scatter_18/pallas_call | solution.py:191
  122.1 1.6 %collective-permute-start.10 = (bf16[880,128]{1,0:T(8,128)(2,1)S(1)}, bf16[880,128]{1,0:T(8,128)(2,1)S(1)}, u32[]{:S(2)}, u32[]{:S(2)}) collective-permute-start(bf16[880,128]{1,0:T(8,128)(2,1)S(1)} %add_convert_fusion), channel_id=1, source_target_pairs={{0,2},{2,0},{1,3},{3,1},{4,6},{6,4},{5,7},{7,5},{8,10},{10,8},{9,1... | collective-permute-start | bytes 675848 | tf_op jit(solution)/shard_map/ppermute | solution.py:235
  123.7 0.7 collective-permute-start.7
  124.4 0.6 collective-permute-start.9
  125.0 3.3 %collective-permute-start.8 = (bf16[128,128]{1,0:T(8,128)(2,1)S(1)}, bf16[128,128]{1,0:T(8,128)(2,1)S(1)}, u32[]{:S(2)}, u32[]{:S(2)}) collective-permute-start(bf16[128,128]{1,0:T(8,128)(2,1)S(1)} %get-tuple-element.41), channel_id=1, source_target_pairs={{0,4},{4,0},{8,12},{12,8},{1,5},{5,1},{9,13},{13,9},{2,6},{6,2},{1... | collective-permute-start | bytes 98312 | tf_op jit(solution)/shard_map/ppermute | solution.py:243
  128.3 1.2 collective-permute-done.10
  129.6 0.2 collective-permute-done.9
  129.9 0.3 collective-permute-done.8
  130.2 2.7 %finish.1 = f32[2048,128]{1,0:T(8,128)} custom-call(f32[2048,128]{1,0:T(8,128)S(1)} %get-tuple-element.21.dmixed_ref, f32[2592,128]{1,0:T(8,128)S(1)} %scatter_18.1.dext_ref, s32[1,512]{1,0:T(1,128)S(1)} %bitcast.16, bf16[512,128]{1,0:T(8,128)(2,1)S(1)} %pad_maximum_fusion.1.back_ref), custom_call_target="tpu_custom_call" | custom-call | flops 268435456 | bytes 4194304 | tf_op jit(solution)/shard_map/finish/pallas_call | solution.py:222
  132.9 0.1 fusion.1
  133.1 0.1 broadcast_select_fusion
  133.2 1.3 convert_multiply_fusion
  134.5 0.6 multiply_bitcast_fusion
  (40 shorter events, 0.7 us)
Async XLA Ops:
  0.6 10.8 %copy-start = (bf16[2048,128]{1,0:T(8,128)(2,1)S(1)}, bf16[2048,128]{1,0:T(8,128)(2,1)}, u32[]{:S(2)}) copy-start(bf16[2048,128]{1,0:T(8,128)(2,1)} %own_ref.1) | copy-start | bytes 1572868
  0.6 9.1 %copy-start.3 = (s32[27,2048]{1,0:T(8,128)S(1)}, s32[27,2048]{1,0:T(8,128)}, u32[]{:S(2)}) copy-start(s32[27,2048]{1,0:T(8,128)} %param.10) | copy-start | bytes 663556
  0.7 9.2 %copy-start.4 = (s32[2048]{0:T(1024)S(1)}, s32[2048]{0:T(1024)}, u32[]{:S(2)}) copy-start(s32[2048]{0:T(1024)} %param.11) | copy-start | bytes 24580
  0.7 9.4 %copy-start.5 = (bf16[128,19]{0,1:T(8,128)(2,1)S(1)}, bf16[128,19]{0,1:T(8,128)(2,1)}, u32[]{:S(2)}) copy-start(bf16[128,19]{0,1:T(8,128)(2,1)} %param.8) | copy-start | bytes 14596
  0.7 10.8 %copy-start.2 = (bf16[27,128,128]{2,1,0:T(8,128)(2,1)S(1)}, bf16[27,128,128]{2,1,0:T(8,128)(2,1)}, u32[]{:S(2)}) copy-start(bf16[27,128,128]{2,1,0:T(8,128)(2,1)} %param.7) | copy-start | bytes 2654212
  4.5 5.5 %collective-permute-start.2 = (bf16[128,128]{1,0:T(8,128)(2,1)S(1)}, bf16[128,128]{1,0:T(8,128)(2,1)S(1)}, u32[]{:S(2)}, u32[]{:S(2)}) collective-permute-start(bf16[128,128]{1,0:T(8,128)(2,1)S(1)} %get-tuple-element.44), channel_id=1, source_target_pairs={{0,2},{2,0},{1,3},{3,1},{4,6},{6,4},{5,7},{7,5},{8,10},{10,8},{9,1... | collective-permute-start | bytes 98312 | tf_op jit(solution)/shard_map/ppermute | solution.py:243
  7.5 3.9 %collective-permute-start = (bf16[128,128]{1,0:T(8,128)(2,1)S(1)}, bf16[128,128]{1,0:T(8,128)(2,1)S(1)}, u32[]{:S(2)}, u32[]{:S(2)}) collective-permute-start(bf16[128,128]{1,0:T(8,128)(2,1)S(1)} %get-tuple-element.45), channel_id=1, source_target_pairs={{0,4},{4,0},{8,12},{12,8},{1,5},{5,1},{9,13},{13,9},{2,6},{6,2},{1... | collective-permute-start | bytes 98312 | tf_op jit(solution)/shard_map/ppermute | solution.py:243
  9.1 2.3 %collective-permute-start.1 = (bf16[128,128]{1,0:T(8,128)(2,1)S(1)}, bf16[128,128]{1,0:T(8,128)(2,1)S(1)}, u32[]{:S(2)}, u32[]{:S(2)}) collective-permute-start(bf16[128,128]{1,0:T(8,128)(2,1)S(1)} %get-tuple-element.46), channel_id=1, source_target_pairs={{4,8},{8,4},{5,9},{9,5},{6,10},{10,6},{7,11},{11,7},{20,24},{24,20... | collective-permute-start | bytes 98312 | tf_op jit(solution)/shard_map/ppermute | solution.py:245
  60.1 2.5 %collective-permute-start.3 = (f32[1760,128]{1,0:T(8,128)S(1)}, f32[1760,128]{1,0:T(8,128)S(1)}, u32[]{:S(2)}, u32[]{:S(2)}) collective-permute-start(f32[1760,128]{1,0:T(8,128)S(1)} %slice_select_fusion), channel_id=1, source_target_pairs={{0,1},{1,0},{2,3},{3,2},{4,5},{5,4},{6,7},{7,6},{8,9},{9,8},{10,11... | collective-permute-start | bytes 2703368 | tf_op jit(solution)/shard_map/ppermute | solution.py:235
  62.8 17.6 %collective-permute-start.4 = (bf16[880,128]{1,0:T(8,128)(2,1)S(1)}, bf16[880,128]{1,0:T(8,128)(2,1)S(1)}, u32[]{:S(2)}, u32[]{:S(2)}) collective-permute-start(bf16[880,128]{1,0:T(8,128)(2,1)S(1)} %select_convert_fusion), channel_id=1, source_target_pairs={{0,2},{2,0},{1,3},{3,1},{4,6},{6,4},{5,7},{7,5},{8,10},{10,8},{9,1... | collective-permute-start | bytes 675848 | tf_op jit(solution)/shard_map/ppermute | solution.py:235
  80.4 24.0 %collective-permute-start.5 = (bf16[880,128]{1,0:T(8,128)(2,1)S(1)}, bf16[880,128]{1,0:T(8,128)(2,1)S(1)}, u32[]{:S(2)}, u32[]{:S(2)}) collective-permute-start(bf16[880,128]{1,0:T(8,128)(2,1)S(1)} %add_convert_fusion.1), channel_id=1, source_target_pairs={{0,8},{4,12},{8,0},{12,4},{1,9},{5,13},{9,1},{13,5},{2,10},{6,14},... | collective-permute-start | bytes 675848 | tf_op jit(solution)/shard_map/ppermute | solution.py:235
  104.5 17.5 %collective-permute-start.6 = (f32[880,128]{1,0:T(8,128)S(1)}, f32[880,128]{1,0:T(8,128)S(1)}, u32[]{:S(2)}, u32[]{:S(2)}) collective-permute-start(f32[880,128]{1,0:T(8,128)S(1)} %convert_add_fusion), channel_id=1, source_target_pairs={{0,4},{4,0},{8,12},{12,8},{1,5},{5,1},{9,13},{13,9},{2,6},{6,2},{1... | collective-permute-start | bytes 1351688 | tf_op jit(solution)/shard_map/ppermute | solution.py:235
  122.1 7.4 %collective-permute-start.10 = (bf16[880,128]{1,0:T(8,128)(2,1)S(1)}, bf16[880,128]{1,0:T(8,128)(2,1)S(1)}, u32[]{:S(2)}, u32[]{:S(2)}) collective-permute-start(bf16[880,128]{1,0:T(8,128)(2,1)S(1)} %add_convert_fusion), channel_id=1, source_target_pairs={{0,2},{2,0},{1,3},{3,1},{4,6},{6,4},{5,7},{7,5},{8,10},{10,8},{9,1... | collective-permute-start | bytes 675848 | tf_op jit(solution)/shard_map/ppermute | solution.py:235
  123.7 6.5 %copy-start.1 = (s32[4,128]{1,0:T(4,128)S(1)}, s32[4,128]{1,0:T(4,128)}, u32[]{:S(2)}) copy-start(s32[4,128]{1,0:T(4,128)} %param.9) | copy-start | bytes 6148
  123.7 6.1 %collective-permute-start.7 = (bf16[128,128]{1,0:T(8,128)(2,1)S(1)}, bf16[128,128]{1,0:T(8,128)(2,1)S(1)}, u32[]{:S(2)}, u32[]{:S(2)}) collective-permute-start(bf16[128,128]{1,0:T(8,128)(2,1)S(1)} %get-tuple-element.39), channel_id=1, source_target_pairs={{4,8},{8,4},{5,9},{9,5},{6,10},{10,6},{7,11},{11,7},{20,24},{24,20... | collective-permute-start | bytes 98312 | tf_op jit(solution)/shard_map/ppermute | solution.py:245
  124.4 5.4 %collective-permute-start.9 = (bf16[128,128]{1,0:T(8,128)(2,1)S(1)}, bf16[128,128]{1,0:T(8,128)(2,1)S(1)}, u32[]{:S(2)}, u32[]{:S(2)}) collective-permute-start(bf16[128,128]{1,0:T(8,128)(2,1)S(1)} %get-tuple-element.40), channel_id=1, source_target_pairs={{0,2},{2,0},{1,3},{3,1},{4,6},{6,4},{5,7},{7,5},{8,10},{10,8},{9,1... | collective-permute-start | bytes 98312 | tf_op jit(solution)/shard_map/ppermute | solution.py:243
  125.0 5.2 %collective-permute-start.8 = (bf16[128,128]{1,0:T(8,128)(2,1)S(1)}, bf16[128,128]{1,0:T(8,128)(2,1)S(1)}, u32[]{:S(2)}, u32[]{:S(2)}) collective-permute-start(bf16[128,128]{1,0:T(8,128)(2,1)S(1)} %get-tuple-element.41), channel_id=1, source_target_pairs={{0,4},{4,0},{8,12},{12,8},{1,5},{5,1},{9,13},{13,9},{2,6},{6,2},{1... | collective-permute-start | bytes 98312 | tf_op jit(solution)/shard_map/ppermute | solution.py:243
  129.6 3.4 %collective-permute-start.11 = (bf16[1760,128]{1,0:T(8,128)(2,1)S(1)}, bf16[1760,128]{1,0:T(8,128)(2,1)S(1)}, u32[]{:S(2)}, u32[]{:S(2)}) collective-permute-start(bf16[1760,128]{1,0:T(8,128)(2,1)S(1)} %pad_maximum_fusion), channel_id=1, source_target_pairs={{0,1},{1,0},{2,3},{3,2},{4,5},{5,4},{6,7},{7,6},{8,9},{9,8},{10,11... | collective-permute-start | bytes 1351688 | tf_op jit(solution)/shard_map/ppermute | solution.py:235

commit v3 on v2

--- a/solution.py
+++ b/solution.py
@@ -11,6 +11,7 @@
 STREAMS = 4
 SCATTER_STREAMS = 8
 SEGMENT = 64
+BY_MATMUL = 8
 GAP = 16
 CHUNKS = 3
 HEAD_ROWS = 32
@@ -44,27 +45,37 @@
 
 
 def forward_kernel(
-    classes, map_hbm, own_ref, halo_refs, weight_ref, class_ref, label_ref,
-    dpre_ref, dmixed_ref, conv_ref, flipped_ref, table, rows, wide, total, sems, *index,
+    classes, map_hbm, sparse_ref, own_ref, halo_refs, weight_ref, class_ref, label_ref,
+    dpre_ref, dmixed_ref, conv_ref, flipped_ref,
+    table, turned, rows, wide, columns, side, total, sems, *index,
 ):
     voxels, chans = dpre_ref.shape
-    offsets = len(index) // STREAMS
+    looped = len(index) // STREAMS
+    offsets = looped + BY_MATMUL
     stream = voxels // STREAMS
     block = STREAMS * SEGMENT
+    share = SEGMENT // BY_MATMUL
     ready, later = fetch(map_hbm, index, sems, 0, stream, (0, 128, stream))
     width = halo_refs[0].shape[0]
     table[:voxels, :] = own_ref[...].astype(jnp.float32)
-    table[voxels : voxels + GAP, :] = jnp.zeros((GAP, chans), jnp.float32)
     for n, halo in enumerate(halo_refs):
-        start = voxels + GAP + n * width
+        start = voxels + n * width
         table[start : start + width, :] = halo[...].astype(jnp.float32)
+    filled = voxels + 4 * width
+    table[filled:, :] = jnp.zeros((table.shape[0] - filled, chans), jnp.float32)
+    for n in range(filled // chans):
+        at = slice(n * chans, (n + 1) * chans)
+        turned[:, at] = table[at, :].T.astype(jnp.bfloat16)
     total[...] = jnp.zeros_like(total)
     conv_ref[pl.ds(offsets * chans, conv_ref.shape[0] - offsets * chans), :] = jnp.zeros(
         (conv_ref.shape[0] - offsets * chans, chans), jnp.float32
     )
     for k in range(offsets):
         at = slice(k * chans, (k + 1) * chans)
-        flipped_ref[at, :] = weight_ref[at, :].T
+        turned_weight = weight_ref[at, :].T
+        flipped_ref[at, :] = turned_weight
+        if k >= looped:
+            side[:, (k - looped) * chans : (k - looped + 1) * chans] = turned_weight
     for copy in ready:
         copy.wait()
 
@@ -74,19 +85,26 @@
             for copy in later:
                 copy.wait()
 
-        def gather_step(i, carry):
-            at = i - b * SEGMENT
-            for u in range(STREAMS):
-                for k in range(offsets):
-                    rows[k, pl.ds(u * SEGMENT + at, 1), :] = table[
-                        pl.ds(index[k * STREAMS + u][i], 1), :
-                    ]
+        def gather_step(j, carry):
+            row = lax.broadcasted_iota(jnp.int32, (filled, block), 0)
+            chosen = (row == sparse_ref[b, pl.ds(j, 1), :]).astype(jnp.float32)
+            at = pl.ds(pl.multiple_of(j * chans, chans), chans)
+            columns[at, :] = dot(turned[...], chosen.astype(jnp.bfloat16), NN).astype(jnp.bfloat16)
+            for n in range(share):
+                to = j * share + n
+                i = b * SEGMENT + to
+                for u in range(STREAMS):
+                    for k in range(looped):
+                        rows[k, pl.ds(u * SEGMENT + to, 1), :] = table[
+                            pl.ds(index[k * STREAMS + u][i], 1), :
+                        ]
             return carry
 
-        lax.fori_loop(b * SEGMENT, (b + 1) * SEGMENT, gather_step, 0)
-        for k in range(offsets):
+        lax.fori_loop(0, BY_MATMUL, gather_step, 0)
+        for k in range(looped):
             wide[:, k * chans : (k + 1) * chans] = rows[k].astype(jnp.bfloat16)
-        pre = dot(wide[...], weight_ref[...], NN)
+        pre = dot(wide[...], weight_ref[: looped * chans, :], NN)
+        pre = pre + dot(side[...], columns[...], NN).T
         starts = [pl.multiple_of(u * stream + b * SEGMENT, SEGMENT) for u in range(STREAMS)]
         own = jnp.concatenate([table[pl.ds(s, SEGMENT), :] for s in starts], axis=0)
         sig = jax.nn.sigmoid(pre)
@@ -106,7 +124,9 @@
         for u, s in enumerate(starts):
             dmixed_ref[pl.ds(s, SEGMENT), :] = dmixed[u * SEGMENT : (u + 1) * SEGMENT]
             dpre_ref[pl.ds(s, SEGMENT), :] = full[u * SEGMENT : (u + 1) * SEGMENT]
-        total[...] += dot(full.T.astype(jnp.bfloat16), wide[...], NN)
+        full_t = full.T.astype(jnp.bfloat16)
+        total[:, : looped * chans] += dot(full_t, wide[...], NN)
+        total[:, looped * chans :] += dot(full_t, columns[...], NT)
         return carry
 
     lax.fori_loop(0, voxels // block, block_step, 0)
@@ -114,11 +134,13 @@
         conv_ref[k * chans : (k + 1) * chans, :] = total[:, k * chans : (k + 1) * chans].T
 
 
-def forward(map_flat, features, incoming, weights, class_t, label_blocks, classes, reduce_rows, table_rows):
+def forward(map_flat, sparse, features, incoming, weights, class_t, label_blocks, classes, reduce_rows, table_rows):
     voxels, chans = features.shape
     offsets = weights.shape[0] // chans
+    looped = offsets - BY_MATMUL
     stream = voxels // STREAMS
     block = STREAMS * SEGMENT
+    filled = voxels + sum(halo.shape[0] for halo in incoming)
     return pl.pallas_call(
         functools.partial(forward_kernel, classes),
         out_shape=(
@@ -127,22 +149,25 @@
             jax.ShapeDtypeStruct((reduce_rows, chans), jnp.float32),
             jax.ShapeDtypeStruct(weights.shape, jnp.bfloat16),
         ),
-        in_specs=[HBM, VMEM, [VMEM] * 4, VMEM, VMEM, VMEM],
+        in_specs=[HBM, VMEM, VMEM, [VMEM] * 4, VMEM, VMEM, VMEM],
         out_specs=(VMEM, VMEM, VMEM, VMEM),
         scratch_shapes=[
             pltpu.VMEM((table_rows, chans), jnp.float32),
-            pltpu.VMEM((offsets, block, chans), jnp.float32),
-            pltpu.VMEM((block, offsets * chans), jnp.bfloat16),
+            pltpu.VMEM((chans, filled), jnp.bfloat16),
+            pltpu.VMEM((looped, block, chans), jnp.float32),
+            pltpu.VMEM((block, looped * chans), jnp.bfloat16),
+            pltpu.VMEM((BY_MATMUL * chans, block), jnp.bfloat16),
+            pltpu.VMEM((chans, BY_MATMUL * chans), jnp.bfloat16),
             pltpu.VMEM((chans, offsets * chans), jnp.float32),
-            pltpu.SemaphoreType.DMA((2, offsets * STREAMS)),
+            pltpu.SemaphoreType.DMA((2, looped * STREAMS)),
         ]
-        + [pltpu.SMEM((stream,), jnp.int32)] * (offsets * STREAMS),
+        + [pltpu.SMEM((stream,), jnp.int32)] * (looped * STREAMS),
         compiler_params=pltpu.CompilerParams(vmem_limit_bytes=40 << 20),
         cost_estimate=pl.CostEstimate(
             flops=4 * voxels * offsets * chans * chans, bytes_accessed=150 << 20, transcendentals=0
         ),
         name="forward",
-    )(map_flat, features, incoming, weights, class_t, label_blocks)
+    )(map_flat, sparse, features, incoming, weights, class_t, label_blocks)
 
 
 def scatter_kernel(first, offsets, has_before, map_hbm, dpre_ref, weight_ref, *refs):
@@ -263,7 +288,14 @@
     low_y, high_y = swap_edges(outgoing[3], outgoing[2], "ty")
     low_x, high_x = swap_edges(outgoing[1], outgoing[0], "tx")
 
-    map_flat = jnp.where(neighbour_map > voxels, neighbour_map + (GAP - 1), neighbour_map).reshape(-1)
+    zero_row = voxels + 4 * width
+    moved = jnp.where(neighbour_map > voxels, neighbour_map - 1, neighbour_map)
+    moved = jnp.where(neighbour_map == voxels, zero_row, moved)
+    map_flat = moved.reshape(-1)
+    sparse = (
+        moved[offsets - BY_MATMUL :].reshape(BY_MATMUL, STREAMS, voxels // block, SEGMENT)
+        .transpose(2, 0, 1, 3).reshape(voxels // block, BY_MATMUL, block)
+    )
     weights = conv_weight.reshape(offsets * chans, chans)
     class_t = jnp.pad(classifier.T, ((0, HEAD_ROWS - classes), (0, 0)))
     label_blocks = (
@@ -271,7 +303,7 @@
         .reshape(voxels // block, 1, block)
     )
     dpre, dmixed, part, flipped = forward(
-        map_flat, features, [low_x, high_x, low_y, high_y], weights, class_t, label_blocks,
+        map_flat, sparse, features, [low_x, high_x, low_y, high_y], weights, class_t, label_blocks,
         classes, reduce_rows, table_rows,
     )
 
@@ -324,8 +356,7 @@
         low, high = jnp.where(upper, got, total), jnp.where(upper, total, got)
         total = jnp.concatenate([low, high], axis=0)
 
-    start = voxels + GAP
-    halo = dext[start : start + 4 * width].astype(jnp.bfloat16).reshape(4, width, chans)
+    halo = dext[voxels : voxels + 4 * width].astype(jnp.bfloat16).reshape(4, width, chans)
     back_3, back_2 = swap_edges(halo[2], halo[3], "ty")
     back_1, back_0 = swap_edges(halo[0], halo[1], "tx")
     back = jnp.concatenate([back_0, back_1, back_2, back_3], axis=0)

time: 135 us -> 129 us (0.956)
  Pallas kernels: 103 us -> 97.6 us
    pallas_call x1, Pallas kernels: 48.5 us -> 42.6 us  [forward(): pl.pallas_call(functools.partial(forward_kernel, classes), out_shape=(jax...]
  transfers between devices with their start and end apart: 12 -> 12, of which waited for: 5 -> 5; matrix products, arithmetic and copies ran while one was open for 0% -> 1% of each run, Pallas kernels for 41% -> 43%
where the time goes in v3:
time: 129 us
  Pallas kernels  97.6 us (76%)
  starting transfers between devices  18.2 us (14%)
  waiting for transfers between devices  5.23 us (4%)
  other arithmetic  4.48 us (3%)
  local copies, waits for them, and re-layouts  2.78 us (2%)
    pallas_call x3, Pallas kernels, scatter(): pl.pallas_call(functools.partial(scatter_kernel, first, offsets, has_befo...  52.3 us
    pallas_call x1, Pallas kernels, forward(): pl.pallas_call(functools.partial(forward_kernel, classes), out_shape=(jax...  42.6 us
    ppermute x4, starting transfers between devices, swap_edges(): first = lax.ppermute(jnp.where(odd, down, up), axis, even_pairs)  8.46 us
    ppermute x6, starting transfers between devices, exchange(): lax.ppermute(shard, axis, [(i, i ^ distance) for i in range(devices)])  8.42 us
    ppermute x6, waiting for transfers between devices, exchange(): lax.ppermute(shard, axis, [(i, i ^ distance) for i in range(devices)])  3.66 us
    pallas_call x1, Pallas kernels, finish(): pl.pallas_call(finish_kernel, out_shape=jax.ShapeDtypeStruct(dmixed.shape...  2.71 us
  transfers between devices with their start and end apart: 12, of which 5 were waited for; matrix products, arithmetic and copies ran while one was open for 1% of the time, Pallas kernels for 43%

profile of v3, /device:TPU:0, one launch (start us, length us, event | category | flops | bytes accessed | tf_op | source)
XLA Modules:
  0.0 129.3 jit_solution(11012019166824736557)
XLA Ops:
  0.7 0.7 broadcast_compare_fusion
  1.4 0.7 fusion.4
  2.1 2.3 %gather_fusion = bf16[512,128]{1,0:T(8,128)(2,1)S(1)} fusion(bf16[2048,128]{1,0:T(8,128)(2,1)} %own_ref.1, s32[1024]{0:T(1024)S(1)} %pad_clamp_fusion), kind=kCustom, calls=%fused_computation | custom fusion | bytes 264192 | tf_op jit(solution)/shard_map/gather | solution.py:286
  4.4 0.1 broadcast_select_fusion.3
  4.6 3.0 %collective-permute-start.2 = (bf16[128,128]{1,0:T(8,128)(2,1)S(1)}, bf16[128,128]{1,0:T(8,128)(2,1)S(1)}, u32[]{:S(2)}, u32[]{:S(2)}) collective-permute-start(bf16[128,128]{1,0:T(8,128)(2,1)S(1)} %get-tuple-element.44), channel_id=1, source_target_pairs={{0,2},{2,0},{1,3},{3,1},{4,6},{6,4},{5,7},{7,5},{8,10},{10,8},{9,1... | collective-permute-start | bytes 98312 | tf_op jit(solution)/shard_map/ppermute | solution.py:268
  7.6 1.6 %collective-permute-start = (bf16[128,128]{1,0:T(8,128)(2,1)S(1)}, bf16[128,128]{1,0:T(8,128)(2,1)S(1)}, u32[]{:S(2)}, u32[]{:S(2)}) collective-permute-start(bf16[128,128]{1,0:T(8,128)(2,1)S(1)} %get-tuple-element.45), channel_id=1, source_target_pairs={{0,4},{4,0},{8,12},{12,8},{1,5},{5,1},{9,13},{13,9},{2,6},{6,2},{1... | collective-permute-start | bytes 98312 | tf_op jit(solution)/shard_map/ppermute | solution.py:268
  9.1 0.7 collective-permute-start.1
  10.0 0.1 reshape.53.label_ref
  10.2 0.1 reshape.50.sparse_ref
  10.4 1.1 collective-permute-done
  11.5 42.6 %forward.1 = (f32[2048,128]{1,0:T(8,128)S(1)}, f32[2048,128]{1,0:T(8,128)S(1)}, f32[3520,128]{1,0:T(8,128)S(1)}, bf16[3456,128]{1,0:T(8,128)(2,1)S(1)}) custom-call(s32[55296]{0:T(1024)S(1)} %reshape.48.map_hbm, s32[8,8,256]{2,1,0:T(8,128)S(1)} %reshape.50.sparse_ref, bf16[2048,128]{1,0:T(8,128)(2,1)S(1)} %copy-done, ...), custom_call_target="tpu_custom_call" | custom-call | flops 3623878656 | bytes 157286400 | tf_op jit(solution)/shard_map/forward/pallas_call | solution.py:144
  54.1 0.1 slice_select_fusion
  54.3 2.4 %collective-permute-done.3 = f32[1760,128]{1,0:T(8,128)S(1)} collective-permute-done((f32[1760,128]{1,0:T(8,128)S(1)}, f32[1760,128]{1,0:T(8,128)S(1)}, u32[]{:S(2)}, u32[]{:S(2)}) %collective-permute-start.3) | collective-permute-done | bytes 901152 | tf_op jit(solution)/shard_map/ppermute | solution.py:260
  56.8 0.1 select_add_fusion
  56.9 0.1 collective-permute-start.4
  57.1 17.4 %scatter_0.1.refs_0_ = f32[2592,128]{1,0:T(8,128)S(1)} custom-call(s32[55296]{0:T(1024)S(1)} %reshape.48.map_hbm, f32[2048,128]{1,0:T(8,128)S(1)} %get-tuple-element.35.dpre_ref, bf16[3456,128]{1,0:T(8,128)(2,1)S(1)} %get-tuple-element.26.weight_ref), custom_call_target="tpu_custom_call" | custom-call | flops 603979776 | bytes 41943040 | tf_op jit(solution)/shard_map/scatter_0/pallas_call | solution.py:216
  74.5 0.1 add_convert_fusion.1
  74.6 6.5 %collective-permute-start.5 = (bf16[880,128]{1,0:T(8,128)(2,1)S(1)}, bf16[880,128]{1,0:T(8,128)(2,1)S(1)}, u32[]{:S(2)}, u32[]{:S(2)}) collective-permute-start(bf16[880,128]{1,0:T(8,128)(2,1)S(1)} %add_convert_fusion.1), channel_id=1, source_target_pairs={{0,8},{4,12},{8,0},{12,4},{1,9},{5,13},{9,1},{13,5},{2,10},{6,14},... | collective-permute-start | bytes 675848 | tf_op jit(solution)/shard_map/ppermute | solution.py:260
  81.1 17.4 %scatter_9.1.refs_0_ = f32[2592,128]{1,0:T(8,128)S(1)} custom-call(s32[55296]{0:T(1024)S(1)} %reshape.48.map_hbm, f32[2048,128]{1,0:T(8,128)S(1)} %get-tuple-element.35.dpre_ref, bf16[3456,128]{1,0:T(8,128)(2,1)S(1)} %get-tuple-element.26.weight_ref, f32[2592,128]{1,0:T(8,128)S(1)} %scatter_0.1.refs_0_), custom_call_target="tpu_custom_call" | custom-call | flops 603979776 | bytes 41943040 | tf_op jit(solution)/shard_map/scatter_9/pallas_call | solution.py:216
  98.7 17.4 %scatter_18.1.dext_ref = f32[2592,128]{1,0:T(8,128)S(1)} custom-call(s32[55296]{0:T(1024)S(1)} %reshape.48.map_hbm, f32[2048,128]{1,0:T(8,128)S(1)} %get-tuple-element.35.dpre_ref, bf16[3456,128]{1,0:T(8,128)(2,1)S(1)} %get-tuple-element.26.weight_ref, f32[2592,128]{1,0:T(8,128)S(1)} %scatter_9.1.refs_0_), custom_call_target="tpu_custom_call" | custom-call | flops 603979776 | bytes 41943040 | tf_op jit(solution)/shard_map/scatter_18/pallas_call | solution.py:216
  116.2 1.5 %collective-permute-start.10 = (bf16[880,128]{1,0:T(8,128)(2,1)S(1)}, bf16[880,128]{1,0:T(8,128)(2,1)S(1)}, u32[]{:S(2)}, u32[]{:S(2)}) collective-permute-start(bf16[880,128]{1,0:T(8,128)(2,1)S(1)} %add_convert_fusion), channel_id=1, source_target_pairs={{0,2},{2,0},{1,3},{3,1},{4,6},{6,4},{5,7},{7,5},{8,10},{10,8},{9,1... | collective-permute-start | bytes 675848 | tf_op jit(solution)/shard_map/ppermute | solution.py:260
  117.9 0.7 collective-permute-start.7
  118.5 0.6 collective-permute-start.9
  119.1 3.3 %collective-permute-start.8 = (bf16[128,128]{1,0:T(8,128)(2,1)S(1)}, bf16[128,128]{1,0:T(8,128)(2,1)S(1)}, u32[]{:S(2)}, u32[]{:S(2)}) collective-permute-start(bf16[128,128]{1,0:T(8,128)(2,1)S(1)} %get-tuple-element.41), channel_id=1, source_target_pairs={{0,4},{4,0},{8,12},{12,8},{1,5},{5,1},{9,13},{13,9},{2,6},{6,2},{1... | collective-permute-start | bytes 98312 | tf_op jit(solution)/shard_map/ppermute | solution.py:268
  122.4 1.2 collective-permute-done.10
  123.8 0.2 collective-permute-done.9
  124.0 0.3 collective-permute-done.8
  124.3 2.7 %finish.1 = f32[2048,128]{1,0:T(8,128)} custom-call(f32[2048,128]{1,0:T(8,128)S(1)} %get-tuple-element.21.dmixed_ref, f32[2592,128]{1,0:T(8,128)S(1)} %scatter_18.1.dext_ref, s32[1,512]{1,0:T(1,128)S(1)} %bitcast.19, bf16[512,128]{1,0:T(8,128)(2,1)S(1)} %pad_maximum_fusion.1.back_ref), custom_call_target="tpu_custom_call" | custom-call | flops 268435456 | bytes 4194304 | tf_op jit(solution)/shard_map/finish/pallas_call | solution.py:247
  127.1 0.1 fusion.1
  127.2 0.1 broadcast_select_fusion
  127.3 1.3 %convert_multiply_fusion = f32[3456,128]{1,0:T(8,128)} fusion(bf16[1696,128]{1,0:T(8,128)(2,1)S(1)} %fusion.1, bf16[1760,128]{1,0:T(8,128)(2,1)S(1)} %broadcast_select_fusion), kind=kLoop, calls=%fused_computation.1 | loop fusion | flops 2211840 | bytes 2654208 | tf_op jit(solution)/shard_map/mul | solution.py:368
  128.7 0.6 multiply_bitcast_fusion
  (44 shorter events, 0.9 us)
Async XLA Ops:
  0.6 9.2 %copy-start.3 = (s32[27,2048]{1,0:T(8,128)S(1)}, s32[27,2048]{1,0:T(8,128)}, u32[]{:S(2)}) copy-start(s32[27,2048]{1,0:T(8,128)} %param.10) | copy-start | bytes 663556
  0.6 9.3 %copy-start.4 = (s32[2048]{0:T(1024)S(1)}, s32[2048]{0:T(1024)}, u32[]{:S(2)}) copy-start(s32[2048]{0:T(1024)} %param.11) | copy-start | bytes 24580
  2.1 8.3 %copy-start.5 = (bf16[128,19]{0,1:T(8,128)(2,1)S(1)}, bf16[128,19]{0,1:T(8,128)(2,1)}, u32[]{:S(2)}) copy-start(bf16[128,19]{0,1:T(8,128)(2,1)} %param.8) | copy-start | bytes 14596
  2.1 9.4 %copy-start = (bf16[2048,128]{1,0:T(8,128)(2,1)S(1)}, bf16[2048,128]{1,0:T(8,128)(2,1)}, u32[]{:S(2)}) copy-start(bf16[2048,128]{1,0:T(8,128)(2,1)} %own_ref.1) | copy-start | bytes 1572868
  2.1 9.4 %copy-start.2 = (bf16[27,128,128]{2,1,0:T(8,128)(2,1)S(1)}, bf16[27,128,128]{2,1,0:T(8,128)(2,1)}, u32[]{:S(2)}) copy-start(bf16[27,128,128]{2,1,0:T(8,128)(2,1)} %param.7) | copy-start | bytes 2654212
  4.6 5.8 %collective-permute-start.2 = (bf16[128,128]{1,0:T(8,128)(2,1)S(1)}, bf16[128,128]{1,0:T(8,128)(2,1)S(1)}, u32[]{:S(2)}, u32[]{:S(2)}) collective-permute-start(bf16[128,128]{1,0:T(8,128)(2,1)S(1)} %get-tuple-element.44), channel_id=1, source_target_pairs={{0,2},{2,0},{1,3},{3,1},{4,6},{6,4},{5,7},{7,5},{8,10},{10,8},{9,1... | collective-permute-start | bytes 98312 | tf_op jit(solution)/shard_map/ppermute | solution.py:268
  7.6 3.9 %collective-permute-start = (bf16[128,128]{1,0:T(8,128)(2,1)S(1)}, bf16[128,128]{1,0:T(8,128)(2,1)S(1)}, u32[]{:S(2)}, u32[]{:S(2)}) collective-permute-start(bf16[128,128]{1,0:T(8,128)(2,1)S(1)} %get-tuple-element.45), channel_id=1, source_target_pairs={{0,4},{4,0},{8,12},{12,8},{1,5},{5,1},{9,13},{13,9},{2,6},{6,2},{1... | collective-permute-start | bytes 98312 | tf_op jit(solution)/shard_map/ppermute | solution.py:268
  9.1 2.3 %collective-permute-start.1 = (bf16[128,128]{1,0:T(8,128)(2,1)S(1)}, bf16[128,128]{1,0:T(8,128)(2,1)S(1)}, u32[]{:S(2)}, u32[]{:S(2)}) collective-permute-start(bf16[128,128]{1,0:T(8,128)(2,1)S(1)} %get-tuple-element.46), channel_id=1, source_target_pairs={{4,8},{8,4},{5,9},{9,5},{6,10},{10,6},{7,11},{11,7},{20,24},{24,20... | collective-permute-start | bytes 98312 | tf_op jit(solution)/shard_map/ppermute | solution.py:270
  54.2 2.5 %collective-permute-start.3 = (f32[1760,128]{1,0:T(8,128)S(1)}, f32[1760,128]{1,0:T(8,128)S(1)}, u32[]{:S(2)}, u32[]{:S(2)}) collective-permute-start(f32[1760,128]{1,0:T(8,128)S(1)} %slice_select_fusion), channel_id=1, source_target_pairs={{0,1},{1,0},{2,3},{3,2},{4,5},{5,4},{6,7},{7,6},{8,9},{9,8},{10,11... | collective-permute-start | bytes 2703368 | tf_op jit(solution)/shard_map/ppermute | solution.py:260
  56.9 17.5 %collective-permute-start.4 = (bf16[880,128]{1,0:T(8,128)(2,1)S(1)}, bf16[880,128]{1,0:T(8,128)(2,1)S(1)}, u32[]{:S(2)}, u32[]{:S(2)}) collective-permute-start(bf16[880,128]{1,0:T(8,128)(2,1)S(1)} %select_convert_fusion), channel_id=1, source_target_pairs={{0,2},{2,0},{1,3},{3,1},{4,6},{6,4},{5,7},{7,5},{8,10},{10,8},{9,1... | collective-permute-start | bytes 675848 | tf_op jit(solution)/shard_map/ppermute | solution.py:260
  74.6 24.0 %collective-permute-start.5 = (bf16[880,128]{1,0:T(8,128)(2,1)S(1)}, bf16[880,128]{1,0:T(8,128)(2,1)S(1)}, u32[]{:S(2)}, u32[]{:S(2)}) collective-permute-start(bf16[880,128]{1,0:T(8,128)(2,1)S(1)} %add_convert_fusion.1), channel_id=1, source_target_pairs={{0,8},{4,12},{8,0},{12,4},{1,9},{5,13},{9,1},{13,5},{2,10},{6,14},... | collective-permute-start | bytes 675848 | tf_op jit(solution)/shard_map/ppermute | solution.py:260
  98.6 17.5 %collective-permute-start.6 = (f32[880,128]{1,0:T(8,128)S(1)}, f32[880,128]{1,0:T(8,128)S(1)}, u32[]{:S(2)}, u32[]{:S(2)}) collective-permute-start(f32[880,128]{1,0:T(8,128)S(1)} %convert_add_fusion), channel_id=1, source_target_pairs={{0,4},{4,0},{8,12},{12,8},{1,5},{5,1},{9,13},{13,9},{2,6},{6,2},{1... | collective-permute-start | bytes 1351688 | tf_op jit(solution)/shard_map/ppermute | solution.py:260
  116.2 7.4 %collective-permute-start.10 = (bf16[880,128]{1,0:T(8,128)(2,1)S(1)}, bf16[880,128]{1,0:T(8,128)(2,1)S(1)}, u32[]{:S(2)}, u32[]{:S(2)}) collective-permute-start(bf16[880,128]{1,0:T(8,128)(2,1)S(1)} %add_convert_fusion), channel_id=1, source_target_pairs={{0,2},{2,0},{1,3},{3,1},{4,6},{6,4},{5,7},{7,5},{8,10},{10,8},{9,1... | collective-permute-start | bytes 675848 | tf_op jit(solution)/shard_map/ppermute | solution.py:260
  117.8 6.5 %copy-start.1 = (s32[4,128]{1,0:T(4,128)S(1)}, s32[4,128]{1,0:T(4,128)}, u32[]{:S(2)}) copy-start(s32[4,128]{1,0:T(4,128)} %param.9) | copy-start | bytes 6148
  117.9 6.1 %collective-permute-start.7 = (bf16[128,128]{1,0:T(8,128)(2,1)S(1)}, bf16[128,128]{1,0:T(8,128)(2,1)S(1)}, u32[]{:S(2)}, u32[]{:S(2)}) collective-permute-start(bf16[128,128]{1,0:T(8,128)(2,1)S(1)} %get-tuple-element.39), channel_id=1, source_target_pairs={{4,8},{8,4},{5,9},{9,5},{6,10},{10,6},{7,11},{11,7},{20,24},{24,20... | collective-permute-start | bytes 98312 | tf_op jit(solution)/shard_map/ppermute | solution.py:270
  118.5 5.4 %collective-permute-start.9 = (bf16[128,128]{1,0:T(8,128)(2,1)S(1)}, bf16[128,128]{1,0:T(8,128)(2,1)S(1)}, u32[]{:S(2)}, u32[]{:S(2)}) collective-permute-start(bf16[128,128]{1,0:T(8,128)(2,1)S(1)} %get-tuple-element.40), channel_id=1, source_target_pairs={{0,2},{2,0},{1,3},{3,1},{4,6},{6,4},{5,7},{7,5},{8,10},{10,8},{9,1... | collective-permute-start | bytes 98312 | tf_op jit(solution)/shard_map/ppermute | solution.py:268
  119.1 5.2 %collective-permute-start.8 = (bf16[128,128]{1,0:T(8,128)(2,1)S(1)}, bf16[128,128]{1,0:T(8,128)(2,1)S(1)}, u32[]{:S(2)}, u32[]{:S(2)}) collective-permute-start(bf16[128,128]{1,0:T(8,128)(2,1)S(1)} %get-tuple-element.41), channel_id=1, source_target_pairs={{0,4},{4,0},{8,12},{12,8},{1,5},{5,1},{9,13},{13,9},{2,6},{6,2},{1... | collective-permute-start | bytes 98312 | tf_op jit(solution)/shard_map/ppermute | solution.py:268
  123.7 3.4 %collective-permute-start.11 = (bf16[1760,128]{1,0:T(8,128)(2,1)S(1)}, bf16[1760,128]{1,0:T(8,128)(2,1)S(1)}, u32[]{:S(2)}, u32[]{:S(2)}) collective-permute-start(bf16[1760,128]{1,0:T(8,128)(2,1)S(1)} %pad_maximum_fusion), channel_id=1, source_target_pairs={{0,1},{1,0},{2,3},{3,2},{4,5},{5,4},{6,7},{7,6},{8,9},{9,8},{10,11... | collective-permute-start | bytes 1351688 | tf_op jit(solution)/shard_map/ppermute | solution.py:260

commit v4 on v3

--- a/solution.py
+++ b/solution.py
@@ -8,12 +8,13 @@
 from jax.experimental.pallas import tpu as pltpu
 from jax.sharding import PartitionSpec as P
 
-STREAMS = 4
-SCATTER_STREAMS = 8
-SEGMENT = 64
+STREAMS = 1
+SCATTER_STREAMS = 2
+SEGMENT = 256
 BY_MATMUL = 8
-GAP = 16
-CHUNKS = 3
+SCATTER_STEPS = 64
+FIRST_PART = 512
+CHUNKS = 2
 HEAD_ROWS = 32
 VMEM = pl.BlockSpec(memory_space=pltpu.VMEM)
 HBM = pl.BlockSpec(memory_space=pl.ANY)
@@ -55,7 +56,7 @@
     stream = voxels // STREAMS
     block = STREAMS * SEGMENT
     share = SEGMENT // BY_MATMUL
-    ready, later = fetch(map_hbm, index, sems, 0, stream, (0, 128, stream))
+    ready, later = fetch(map_hbm, index, sems, 0, stream, (0, FIRST_PART, stream))
     width = halo_refs[0].shape[0]
     table[:voxels, :] = own_ref[...].astype(jnp.float32)
     for n, halo in enumerate(halo_refs):
@@ -80,7 +81,7 @@
         copy.wait()
 
     def block_step(b, carry):
-        @pl.when(b == 128 // SEGMENT)
+        @pl.when(b == FIRST_PART // SEGMENT)
         def _():
             for copy in later:
                 copy.wait()
@@ -173,29 +174,28 @@
 def scatter_kernel(first, offsets, has_before, map_hbm, dpre_ref, weight_ref, *refs):
     refs = list(refs)
     before = refs.pop(0) if has_before else None
-    out_ref, sems = refs[0], refs[1]
+    out_ref, sems = refs[:2]
     tables = refs[2 : 2 + offsets]
     index = refs[2 + offsets :]
-    voxels, chans = dpre_ref.shape
-    stream = voxels // SCATTER_STREAMS
-    ready, later = fetch(map_hbm, index, sems, first * SCATTER_STREAMS, stream, (0, 128, stream))
+    streams, stream, chans = dpre_ref.shape
+    share = stream // SCATTER_STEPS
+    copies, = fetch(map_hbm, index, sems, first * streams, stream, (0, stream))
     for table in tables:
         table[...] = jnp.zeros_like(table)
-    for copy in ready:
+    for copy in copies:
         copy.wait()
 
-    def step(i, carry):
-        for u in range(SCATTER_STREAMS):
-            row = dpre_ref[pl.ds(u * stream + i, 1), :]
-            for k in range(offsets):
-                at = pl.ds(index[k * SCATTER_STREAMS + u][i], 1)
-                tables[k][at, :] = tables[k][at, :] + row
+    def step(j, carry):
+        for n in range(share):
+            i = j * share + n
+            for u in range(streams):
+                value = dpre_ref[u, pl.ds(i, 1), :]
+                for k in range(offsets):
+                    where = pl.ds(index[k * streams + u][i], 1)
+                    tables[k][where, :] = tables[k][where, :] + value
         return carry
 
-    lax.fori_loop(0, 128, step, 0)
-    for copy in later:
-        copy.wait()
-    lax.fori_loop(128, stream, step, 0)
+    lax.fori_loop(0, SCATTER_STEPS, step, 0)
     tiles = 3
     height = out_ref.shape[0] // tiles
 
@@ -218,7 +218,9 @@
         out_shape=jax.ShapeDtypeStruct((table_rows, chans), jnp.float32),
         in_specs=[HBM, VMEM, VMEM] + ([VMEM] if has_before else []),
         out_specs=VMEM,
-        scratch_shapes=[pltpu.SemaphoreType.DMA((2, offsets * SCATTER_STREAMS))]
+        scratch_shapes=[
+            pltpu.SemaphoreType.DMA((1, offsets * SCATTER_STREAMS)),
+        ]
         + [pltpu.VMEM((table_rows, chans), jnp.float32)] * offsets
         + [pltpu.SMEM((stream,), jnp.int32)] * (offsets * SCATTER_STREAMS),
         compiler_params=pltpu.CompilerParams(vmem_limit_bytes=40 << 20),
@@ -226,7 +228,10 @@
             flops=2 * voxels * offsets * chans * chans, bytes_accessed=40 << 20, transcendentals=0
         ),
         name=f"scatter_{first}",
-    )(map_flat, dpre, flipped, *([before] if has_before else []))
+    )(
+        map_flat, dpre.reshape(SCATTER_STREAMS, stream, chans), flipped,
+        *([before] if has_before else []),
+    )
 
 
 def finish_kernel(dmixed_ref, dext_ref, send_ref, back_ref, out_ref):
@@ -255,22 +260,120 @@
     )(dmixed, dext, send_flat, back)
 
 
-def exchange(shard, axis, distance):
+def outgoing_kernel(axes, send_ref, own_ref, *refs):
+    *out_refs, table, sent = refs
+    voxels, chans = own_ref.shape
+    width = send_ref.shape[1]
+    table[:voxels, :] = own_ref[...].astype(jnp.float32)
+    table[voxels:, :] = jnp.zeros((table.shape[0] - voxels, chans), jnp.float32)
+    for s in range(4):
+
+        def step(t, carry, s=s):
+            for n in range(32):
+                i = t * 32 + n
+                sent[pl.ds(s * width + i, 1), :] = table[pl.ds(send_ref[s, i], 1), :]
+            return carry
+
+        lax.fori_loop(0, width // 32, step, 0)
+    lists = [sent[s * width : (s + 1) * width, :] for s in range(4)]
+    picked = []
+    for axis, (up, down) in zip(axes, ((2, 3), (0, 1))):
+        odd = (lax.axis_index(axis) & 1) != 0
+        picked.append(jnp.where(odd, lists[down], lists[up]))
+        picked.append(jnp.where(odd, lists[up], lists[down]))
+    for out_ref, value in zip(out_refs, picked):
+        out_ref[...] = value.astype(jnp.bfloat16)
+
+
+def outgoing(send_rows, features):
+    voxels, chans = features.shape
+    width = send_rows.shape[1]
+    return pl.pallas_call(
+        functools.partial(outgoing_kernel, ("ty", "tx")),
+        out_shape=[jax.ShapeDtypeStruct((width, chans), jnp.bfloat16)] * 4,
+        in_specs=[pl.BlockSpec(memory_space=pltpu.SMEM), VMEM],
+        out_specs=[VMEM] * 4,
+        scratch_shapes=[
+            pltpu.VMEM((voxels + 8, chans), jnp.float32),
+            pltpu.VMEM((4 * width, chans), jnp.float32),
+        ],
+        compiler_params=pltpu.CompilerParams(vmem_limit_bytes=16 << 20),
+        name="outgoing",
+    )(send_rows, features)
+
+
+def assemble_kernel(axes, scale, conv_rows, *refs):
+    *piece_refs, conv_ref, head_ref = refs
+    pieces = len(piece_refs)
+    height = piece_refs[0].shape[0]
+    mine = group_index(axes)
+    for d, piece_ref in enumerate(piece_refs):
+        for p in range(pieces):
+
+            @pl.when((mine ^ d) == p)
+            def _(p=p, piece_ref=piece_ref):
+                start = p * height
+                inside = max(0, min(height, conv_rows - start))
+                if inside:
+                    value = piece_ref[:inside, :].astype(jnp.float32) * scale
+                    conv_ref[start : start + inside, :] = value
+                if start <= conv_rows < start + height:
+                    at = conv_rows - start
+                    value = piece_ref[at : at + HEAD_ROWS, :].astype(jnp.float32) * scale
+                    head_ref[...] = value
+
+
+def assemble(pieces, axes, scale, conv_rows):
+    chans = pieces[0].shape[1]
+    return pl.pallas_call(
+        functools.partial(assemble_kernel, axes, scale, conv_rows),
+        out_shape=(
+            jax.ShapeDtypeStruct((conv_rows, chans), jnp.float32),
+            jax.ShapeDtypeStruct((HEAD_ROWS, chans), jnp.float32),
+        ),
+        in_specs=[VMEM] * len(pieces),
+        out_specs=(VMEM, VMEM),
+        compiler_params=pltpu.CompilerParams(vmem_limit_bytes=16 << 20),
+        name="assemble",
+    )(*pieces)
+
+
+def group_index(axes):
+    at = 0
+    for axis in axes:
+        at = at * lax.axis_size(axis) + lax.axis_index(axis)
+    return at
+
+
+def group_size(axes):
+    return math.prod(lax.axis_size(axis) for axis in axes)
+
+
+def exchange(shard, axes, distance):
+    return lax.ppermute(shard, axes, [(i, i ^ distance) for i in range(group_size(axes))])
+
+
+def edge_pairs(axis):
     devices = lax.axis_size(axis)
-    return lax.ppermute(shard, axis, [(i, i ^ distance) for i in range(devices)])
-
-
-def swap_edges(down, up, axis):
-    devices = lax.axis_size(axis)
+    even = [(i, i ^ 1) for i in range(devices) if (i ^ 1) < devices]
+    odd = [(i, ((i + 1) ^ 1) - 1) for i in range(1, devices) if ((i + 1) ^ 1) - 1 < devices]
+    return even, odd
+
+
+def swap_edges(over_even, over_odd, axis):
+    even_pairs, odd_pairs = edge_pairs(axis)
     odd = (lax.axis_index(axis) & 1) != 0
-    even_pairs = [(i, i ^ 1) for i in range(devices) if (i ^ 1) < devices]
-    odd_pairs = [(i, ((i + 1) ^ 1) - 1) for i in range(1, devices) if ((i + 1) ^ 1) - 1 < devices]
-    first = lax.ppermute(jnp.where(odd, down, up), axis, even_pairs)
+    first = lax.ppermute(over_even, axis, even_pairs)
     if odd_pairs:
-        second = lax.ppermute(jnp.where(odd, up, down), axis, odd_pairs)
+        second = lax.ppermute(over_odd, axis, odd_pairs)
     else:
         second = jnp.zeros_like(first)
     return jnp.where(odd, first, second), jnp.where(odd, second, first)
+
+
+def by_parity(down, up, axis):
+    odd = (lax.axis_index(axis) & 1) != 0
+    return jnp.where(odd, down, up), jnp.where(odd, up, down)
 
 
 def on_device(features, conv_weight, classifier, send_rows, neighbour_map, labels):
@@ -279,14 +382,16 @@
     offsets = conv_weight.shape[0]
     classes = classifier.shape[1]
     block = STREAMS * SEGMENT
-    table_rows = -(-(voxels + GAP + 4 * width) // 48) * 48
-    reduce_rows = -(-(offsets * chans + HEAD_ROWS) // 64) * 64
-
-    outgoing = jnp.where(
-        (send_rows < voxels)[..., None], features[jnp.minimum(send_rows, voxels - 1)], 0
-    )
-    low_y, high_y = swap_edges(outgoing[3], outgoing[2], "ty")
-    low_x, high_x = swap_edges(outgoing[1], outgoing[0], "tx")
+    table_rows = -(-(voxels + 4 * width + 1) // 48) * 48
+    square = ("ty", "rep")
+    pieces = group_size(square)
+    unit = 16 * pieces
+    reduce_rows = -(-(offsets * chans + HEAD_ROWS) // unit) * unit
+    height = reduce_rows // pieces
+
+    even_y, odd_y, even_x, odd_x = outgoing(send_rows, features)
+    low_y, high_y = swap_edges(even_y, odd_y, "ty")
+    low_x, high_x = swap_edges(even_x, odd_x, "tx")
 
     zero_row = voxels + 4 * width
     moved = jnp.where(neighbour_map > voxels, neighbour_map - 1, neighbour_map)
@@ -307,14 +412,9 @@
         classes, reduce_rows, table_rows,
     )
 
-    chunks = [
-        (c * offsets // CHUNKS, (c + 1) * offsets // CHUNKS) for c in range(CHUNKS)
-    ]
-    dext = None
+    chunks = [(c * offsets // CHUNKS, (c + 1) * offsets // CHUNKS) for c in range(CHUNKS)]
 
     def scatter_beside(sent, before):
-        if not chunks:
-            return sent, before
         first, last = chunks.pop(0)
         held = (sent, dpre) if before is None else (sent, dpre, before)
         held = lax.optimization_barrier(held)
@@ -323,54 +423,44 @@
             first, last - first, table_rows,
         )
 
-    halved = []
-    for axis, kind in (("rep", jnp.float32), ("ty", jnp.bfloat16)):
-        distance = lax.axis_size(axis) // 2
-        while distance:
-            halved.append((axis, distance))
-            upper = (lax.axis_index(axis) & distance) != 0
-            half = part.shape[0] // 2
-            low, high = part[:half], part[half:]
-            sent = jnp.where(upper, low, high).astype(kind)
-            if axis != "rep":
-                sent, dext = scatter_beside(sent, dext)
-            got = exchange(sent, axis, distance)
-            if dext is not None:
-                got, dext = lax.optimization_barrier((got, dext))
-            part = jnp.where(upper, high, low) + got.astype(jnp.float32)
-            distance //= 2
-    distance = lax.axis_size("tx") // 2
-    kind = jnp.bfloat16
-    while distance:
-        sent, dext = scatter_beside(part.astype(kind), dext)
-        got, dext = lax.optimization_barrier((exchange(sent, "tx", distance), dext))
-        part = sent.astype(jnp.float32) + got.astype(jnp.float32)
-        distance //= 2
-        kind = jnp.float32
+    mine = group_index(square)
+    sent = []
+    for d in range(1, pieces):
+        piece = lax.dynamic_slice_in_dim(part, (mine ^ d) * height, height, axis=0)
+        sent.append(piece.astype(jnp.bfloat16))
+    own = lax.dynamic_slice_in_dim(part, mine * height, height, axis=0)
+    sent, dext = scatter_beside(sent, None)
+    got = [exchange(piece, square, d + 1) for d, piece in enumerate(sent)]
+    got, dext = lax.optimization_barrier((got, dext))
+    own = own + sum(piece.astype(jnp.float32) for piece in got)
+
+    stride = 1
+    while stride < lax.axis_size("tx"):
+        radix = min(4, lax.axis_size("tx") // stride)
+        own = own.astype(jnp.bfloat16)
+        if chunks:
+            own, dext = scatter_beside(own, dext)
+        got = [own] + [exchange(own, ("tx",), m * stride) for m in range(1, radix)]
+        got, dext = lax.optimization_barrier((got, dext))
+        got = [piece.astype(jnp.float32) for piece in got]
+        while len(got) > 1:
+            got = [a + b for a, b in zip(got[::2], got[1::2])]
+        own = got[0]
+        stride *= radix
     while chunks:
-        part, dext = scatter_beside(part, dext)
-    total = part.astype(jnp.bfloat16)
-    for axis, distance in reversed(halved):
-        upper = (lax.axis_index(axis) & distance) != 0
-        total_before, got = total, exchange(total, axis, distance)
-        low, high = jnp.where(upper, got, total), jnp.where(upper, total, got)
-        total = jnp.concatenate([low, high], axis=0)
+        own, dext = scatter_beside(own, dext)
 
     halo = dext[voxels : voxels + 4 * width].astype(jnp.bfloat16).reshape(4, width, chans)
-    back_3, back_2 = swap_edges(halo[2], halo[3], "ty")
-    back_1, back_0 = swap_edges(halo[0], halo[1], "tx")
+    back_3, back_2 = swap_edges(*by_parity(halo[2], halo[3], "ty"), "ty")
+    back_1, back_0 = swap_edges(*by_parity(halo[0], halo[1], "tx"), "tx")
     back = jnp.concatenate([back_0, back_1, back_2, back_3], axis=0)
     grad_input = finish(dmixed, dext, send_rows.reshape(1, -1), back)
 
+    own = own.astype(jnp.bfloat16)
+    everywhere = [own] + [exchange(own, square, d) for d in range(1, pieces)]
     count = voxels * lax.axis_size("tx") * lax.axis_size("ty") * lax.axis_size("rep")
-    scale = 1.0 / math.sqrt(count)
-    split = offsets * chans - low.shape[0]
-    grad_conv = jnp.concatenate([low, high[:split]], axis=0).astype(jnp.float32) * scale
-    grad_conv = grad_conv.reshape(offsets, chans, chans)
-    grad_head = jnp.where(
-        upper, total_before[split : split + classes], got[split : split + classes]
-    ).T.astype(jnp.float32) * scale
-    return grad_input, grad_conv, grad_head
+    conv, head = assemble(everywhere, square, 1.0 / math.sqrt(count), offsets * chans)
+    return grad_input, conv.reshape(offsets, chans, chans), head[:classes].T
 
 
 def solution(mesh):

time: 129 us -> 132 us (1.023)
  Pallas kernels: 97.6 us -> 90 us
  waiting for transfers between devices: 5.23 us -> 10.6 us
  local copies, waits for them, and re-layouts: 2.78 us -> 7.38 us
  starting transfers between devices: 18.2 us -> 20.5 us
  other arithmetic: 4.48 us -> 2.61 us
    pallas_call x3 -> x2, Pallas kernels: 52.3 us -> 41.8 us  [scatter(): pl.pallas_call(functools.partial(scatter_kernel, first, offsets, has_befo...]
    ppermute x12 -> x15, waiting for transfers between devices: 5.23 us -> 10.6 us  [the longest x4 10.6 us: swap_edges(): first = lax.ppermute(over_even, axis, even_pairs)]
    unnamed x12 -> x14, local copies, waits for them, and re-layouts: 0.03 us -> 5.17 us
    pallas_call x0 -> x2, Pallas kernels: none -> 3.67 us  [the longest x1 2.25 us: outgoing(): pl.pallas_call(functools.partial(outgoing_kernel, ('ty', 'tx')), out_shap...]
    ppermute x12 -> x15, starting transfers between devices: 18.2 us -> 20.5 us  [the longest x9 9.71 us: exchange(): lax.ppermute(shard, axes, [(i, i ^ distance) for i in range(group_size(ax...]
    gather x1 -> x0, local copies, waits for them, and re-layouts: 2.27 us -> none  [on_device(): features[jnp.minimum(send_rows, voxels - 1)]]
    mul x2 -> x0, other arithmetic: 1.95 us -> none  [the longest x1 1.34 us: on_device(): jnp.concatenate([low, high[:split]], axis=0).astype(jnp.float32) * scale]
  transfers between devices with their start and end apart: 12 -> 15, of which waited for: 5 -> 2; matrix products, arithmetic and copies ran while one was open for 1% -> 1% of each run, Pallas kernels for 43% -> 34%
where the time goes in v4:
time: 132 us
  Pallas kernels  90 us (68%)
  starting transfers between devices  20.5 us (16%)
  waiting for transfers between devices  10.6 us (8%)
  local copies, waits for them, and re-layouts  7.38 us (6%)
  other arithmetic  2.61 us (2%)
    pallas_call x1, Pallas kernels, forward(): pl.pallas_call(functools.partial(forward_kernel, classes), out_shape=(jax...  41.8 us
    pallas_call x2, Pallas kernels, scatter(): pl.pallas_call(functools.partial(scatter_kernel, first, offsets, has_befo...  41.8 us
    ppermute x4, waiting for transfers between devices, swap_edges(): first = lax.ppermute(over_even, axis, even_pairs)  10.6 us
    ppermute x9, starting transfers between devices, exchange(): lax.ppermute(shard, axes, [(i, i ^ distance) for i in range(group_size(ax...  9.71 us
    ppermute x4, starting transfers between devices, swap_edges(): first = lax.ppermute(over_even, axis, even_pairs)  9.5 us
    unnamed x14, local copies, waits for them, and re-layouts  5.17 us
    pallas_call x1, Pallas kernels, finish(): pl.pallas_call(finish_kernel, out_shape=jax.ShapeDtypeStruct(dmixed.shape...  2.71 us
  transfers between devices with their start and end apart: 15, of which 2 were waited for; matrix products, arithmetic and copies ran while one was open for 1% of the time, Pallas kernels for 34%

profile of v4, /device:TPU:0, one launch (start us, length us, event | category | flops | bytes accessed | tf_op | source)
XLA Modules:
  0.0 132.0 jit_solution(13680179044838695594)
XLA Ops:
  0.6 1.0 copy-done.1
  1.7 0.7 copy-done.3
  2.4 2.3 %outgoing.1 = (bf16[128,128]{1,0:T(8,128)(2,1)S(1)}, bf16[128,128]{1,0:T(8,128)(2,1)}, bf16[128,128]{1,0:T(8,128)(2,1)S(1)}, bf16[128,128]{1,0:T(8,128)(2,1)S(1)}) custom-call(s32[4,128]{1,0:T(4,128)S(1)} %copy-done.3, bf16[2048,128]{1,0:T(8,128)(2,1)S(1)} %copy-done.1), custom_call_target="tpu_custom_call" | custom-call | tf_op jit(solution)/shard_map/outgoing/pallas_call | solution.py:291
  4.6 3.0 %collective-permute-start = (bf16[128,128]{1,0:T(8,128)(2,1)S(1)}, bf16[128,128]{1,0:T(8,128)(2,1)S(1)}, u32[]{:S(2)}, u32[]{:S(2)}) collective-permute-start(bf16[128,128]{1,0:T(8,128)(2,1)S(1)} %get-tuple-element.28), channel_id=1, source_target_pairs={{0,4},{4,0},{8,12},{12,8},{1,5},{5,1},{9,13},{13,9},{2,6},{6,2},{1... | collective-permute-start | bytes 98312 | tf_op jit(solution)/shard_map/ppermute | solution.py:366
  7.6 0.7 collective-permute-start.1
  8.3 1.6 %collective-permute-start.2 = (bf16[128,128]{1,0:T(8,128)(2,1)S(1)}, bf16[128,128]{1,0:T(8,128)(2,1)S(1)}, u32[]{:S(2)}, u32[]{:S(2)}) collective-permute-start(bf16[128,128]{1,0:T(8,128)(2,1)S(1)} %get-tuple-element.30), channel_id=1, source_target_pairs={{0,2},{2,0},{1,3},{3,1},{4,6},{6,4},{5,7},{7,5},{8,10},{10,8},{9,1... | collective-permute-start | bytes 98312 | tf_op jit(solution)/shard_map/ppermute | solution.py:366
  9.9 1.0 fusion
  11.0 0.7 pad.4.class_ref
  11.7 0.6 collective-permute-done.2
  12.3 1.0 copy-done.2
  13.4 1.2 copy-done.5
  14.6 41.8 %forward.1 = (f32[2048,128]{1,0:T(8,128)S(1)}, f32[2048,128]{1,0:T(8,128)S(1)}, f32[3520,128]{1,0:T(8,128)S(1)}, bf16[3456,128]{1,0:T(8,128)(2,1)S(1)}) custom-call(s32[55296]{0:T(1024)S(1)} %reshape.39.map_hbm, s32[8,8,256]{2,1,0:T(8,128)S(1)} %bitcast.16, bf16[2048,128]{1,0:T(8,128)(2,1)S(1)} %copy-done.2, ...), custom_call_target="tpu_custom_call" | custom-call | flops 3623878656 | bytes 157286400 | tf_op jit(solution)/shard_map/forward/pallas_call | solution.py:145
  56.4 1.2 copy-done
  57.6 0.9 dynamic-slice_convert_fusion
  58.5 1.5 %collective-permute-start.4 = (bf16[880,128]{1,0:T(8,128)(2,1)}, bf16[880,128]{1,0:T(8,128)(2,1)}, u32[]{:S(2)}, u32[]{:S(2)}) collective-permute-start(bf16[880,128]{1,0:T(8,128)(2,1)} %get-tuple-element.35), channel_id=1, source_target_pairs={{0,2},{1,3},{2,0},{3,1},{4,6},{5,7},{6,4},{7,5},{8,10},{9,11},{10,... | collective-permute-start | bytes 675848 | tf_op jit(solution)/shard_map/ppermute | solution.py:353
  59.9 0.4 collective-permute-start.5
  60.3 20.2 %scatter_0.1.refs_0_ = f32[2592,128]{1,0:T(8,128)S(1)} custom-call(s32[55296]{0:T(1024)S(1)} %reshape.39.map_hbm, f32[2,1024,128]{2,1,0:T(8,128)S(1)} %bitcast.14, bf16[3456,128]{1,0:T(8,128)(2,1)S(1)} %get-tuple-element.38.weight_ref), custom_call_target="tpu_custom_call" | custom-call | flops 872415232 | bytes 41943040 | tf_op jit(solution)/shard_map/scatter_0/pallas_call | solution.py:216
  80.5 1.4 %add_convert_fusion.1 = bf16[880,128]{1,0:T(8,128)(2,1)S(1)} fusion(bf16[880,128]{1,0:T(8,128)(2,1)} %collective-permute-done.5, bf16[880,128]{1,0:T(8,128)(2,1)} %collective-permute-done.4, bf16[880,128]{1,0:T(8,128)(2,1)S(1)} %collective-permute-done.3, f32[3520,128]{1,0:T(8,128)} %copy-done, s32[]{:T(128)S(6)} %select_n.78), kind=kLoop, calls=%fused_computation.2 | loop fusion | flops 788480 | bytes 1351684 | tf_op jit(solution)/shard_map/convert_element_type | solution.py:440
  81.9 2.5 %collective-permute-start.8 = (bf16[880,128]{1,0:T(8,128)(2,1)S(1)}, bf16[880,128]{1,0:T(8,128)(2,1)S(1)}, u32[]{:S(2)}, u32[]{:S(2)}) collective-permute-start(bf16[880,128]{1,0:T(8,128)(2,1)S(1)} %add_convert_fusion.1), channel_id=1, source_target_pairs={{0,12},{4,8},{8,4},{12,0},{1,13},{5,9},{9,5},{13,1},{2,14},{6,10},... | collective-permute-start | bytes 675848 | tf_op jit(solution)/shard_map/ppermute | solution.py:353
  84.4 3.4 %collective-permute-start.7 = (bf16[880,128]{1,0:T(8,128)(2,1)S(1)}, bf16[880,128]{1,0:T(8,128)(2,1)S(1)}, u32[]{:S(2)}, u32[]{:S(2)}) collective-permute-start(bf16[880,128]{1,0:T(8,128)(2,1)S(1)} %add_convert_fusion.1), channel_id=1, source_target_pairs={{0,8},{4,12},{8,0},{12,4},{1,9},{5,13},{9,1},{13,5},{2,10},{6,14},... | collective-permute-start | bytes 675848 | tf_op jit(solution)/shard_map/ppermute | solution.py:353
  87.8 21.6 %scatter_13.1.dext_ref = f32[2592,128]{1,0:T(8,128)S(1)} custom-call(s32[55296]{0:T(1024)S(1)} %reshape.39.map_hbm, f32[2,1024,128]{2,1,0:T(8,128)S(1)} %bitcast.15, bf16[3456,128]{1,0:T(8,128)(2,1)S(1)} %get-tuple-element.38.weight_ref, f32[2592,128]{1,0:T(8,128)S(1)} %scatter_0.1.refs_0_), custom_call_target="tpu_custom_call" | custom-call | flops 939524096 | bytes 41943040 | tf_op jit(solution)/shard_map/scatter_13/pallas_call | solution.py:216
  109.6 0.7 collective-permute-start.9
  110.2 3.4 %collective-permute-start.10 = (bf16[128,128]{1,0:T(8,128)(2,1)S(1)}, bf16[128,128]{1,0:T(8,128)(2,1)S(1)}, u32[]{:S(2)}, u32[]{:S(2)}) collective-permute-start(bf16[128,128]{1,0:T(8,128)(2,1)S(1)} %get-tuple-element.58), channel_id=1, source_target_pairs={{0,4},{4,0},{8,12},{12,8},{1,5},{5,1},{9,13},{13,9},{2,6},{6,2},{1... | collective-permute-start | bytes 98312 | tf_op jit(solution)/shard_map/ppermute | solution.py:366
  113.7 0.1 add_convert_fusion.refs_0_
  113.8 0.3 collective-permute-start.14
  114.1 1.3 collective-permute-start.13
  115.4 0.3 collective-permute-start.12
  115.7 1.5 %collective-permute-start.11 = (bf16[128,128]{1,0:T(8,128)(2,1)S(1)}, bf16[128,128]{1,0:T(8,128)(2,1)S(1)}, u32[]{:S(2)}, u32[]{:S(2)}) collective-permute-start(bf16[128,128]{1,0:T(8,128)(2,1)S(1)} %get-tuple-element.57), channel_id=1, source_target_pairs={{0,2},{2,0},{1,3},{3,1},{4,6},{6,4},{5,7},{7,5},{8,10},{10,8},{9,1... | collective-permute-start | bytes 98312 | tf_op jit(solution)/shard_map/ppermute | solution.py:366
  117.2 10.0 %collective-permute-done.11 = bf16[128,128]{1,0:T(8,128)(2,1)S(1)} collective-permute-done((bf16[128,128]{1,0:T(8,128)(2,1)S(1)}, bf16[128,128]{1,0:T(8,128)(2,1)S(1)}, u32[]{:S(2)}, u32[]{:S(2)}) %collective-permute-start.11) | collective-permute-done | bytes 32800 | tf_op jit(solution)/shard_map/ppermute | solution.py:366
  127.2 2.7 %finish.1 = f32[2048,128]{1,0:T(8,128)} custom-call(f32[2048,128]{1,0:T(8,128)S(1)} %get-tuple-element.31.dmixed_ref, f32[2592,128]{1,0:T(8,128)S(1)} %scatter_13.1.dext_ref, s32[1,512]{1,0:T(1,128)S(1)} %bitcast.17, bf16[512,128]{1,0:T(8,128)(2,1)S(1)} %pad_maximum_fusion.back_ref), custom_call_target="tpu_custom_call" | custom-call | flops 268435456 | bytes 4194304 | tf_op jit(solution)/shard_map/finish/pallas_call | solution.py:252
  130.0 1.4 %assemble.1 = (f32[3456,128]{1,0:T(8,128)}, f32[32,128]{1,0:T(8,128)S(1)}) custom-call(bf16[880,128]{1,0:T(8,128)(2,1)S(1)} %add_convert_fusion.refs_0_, bf16[880,128]{1,0:T(8,128)(2,1)S(1)} %collective-permute-done.12.refs_1_, bf16[880,128]{1,0:T(8,128)(2,1)S(1)} %collective-permute-done.13.refs_2_, bf16[880,128]{1,0:T(8,128)(2,1)S(1)} %collective-permute-done.14.refs_3_), custom_call_target="tpu_custom_call" | custom-call | tf_op jit(solution)/shard_map/assemble/pallas_call | solution.py:328
  131.4 0.6 slice_bitcast_fusion
  (33 shorter events, 0.2 us)
Async XLA Ops:
  0.6 1.0 copy-start.1
  1.7 0.7 copy-start.3
  2.4 10.0 %copy-start.6 = (s32[2048]{0:T(1024)S(1)}, s32[2048]{0:T(1024)}, u32[]{:S(2)}) copy-start(s32[2048]{0:T(1024)} %param.11) | copy-start | bytes 24580
  4.6 7.7 %collective-permute-start = (bf16[128,128]{1,0:T(8,128)(2,1)S(1)}, bf16[128,128]{1,0:T(8,128)(2,1)S(1)}, u32[]{:S(2)}, u32[]{:S(2)}) collective-permute-start(bf16[128,128]{1,0:T(8,128)(2,1)S(1)} %get-tuple-element.28), channel_id=1, source_target_pairs={{0,4},{4,0},{8,12},{12,8},{1,5},{5,1},{9,13},{13,9},{2,6},{6,2},{1... | collective-permute-start | bytes 98312 | tf_op jit(solution)/shard_map/ppermute | solution.py:366
  7.6 4.7 %collective-permute-start.1 = (bf16[128,128]{1,0:T(8,128)(2,1)S(1)}, bf16[128,128]{1,0:T(8,128)(2,1)S(1)}, u32[]{:S(2)}, u32[]{:S(2)}) collective-permute-start(bf16[128,128]{1,0:T(8,128)(2,1)S(1)} %get-tuple-element.29), channel_id=1, source_target_pairs={{4,8},{8,4},{5,9},{9,5},{6,10},{10,6},{7,11},{11,7},{20,24},{24,20... | collective-permute-start | bytes 98312 | tf_op jit(solution)/shard_map/ppermute | solution.py:368
  8.3 4.0 %collective-permute-start.2 = (bf16[128,128]{1,0:T(8,128)(2,1)S(1)}, bf16[128,128]{1,0:T(8,128)(2,1)S(1)}, u32[]{:S(2)}, u32[]{:S(2)}) collective-permute-start(bf16[128,128]{1,0:T(8,128)(2,1)S(1)} %get-tuple-element.30), channel_id=1, source_target_pairs={{0,2},{2,0},{1,3},{3,1},{4,6},{6,4},{5,7},{7,5},{8,10},{10,8},{9,1... | collective-permute-start | bytes 98312 | tf_op jit(solution)/shard_map/ppermute | solution.py:366
  12.3 1.0 copy-start.2
  13.4 1.2 copy-start.5
  56.4 1.2 copy-start
  58.5 22.1 %collective-permute-start.3 = (bf16[880,128]{1,0:T(8,128)(2,1)}, bf16[880,128]{1,0:T(8,128)(2,1)S(1)}, u32[]{:S(2)}, u32[]{:S(2)}) collective-permute-start(bf16[880,128]{1,0:T(8,128)(2,1)} %get-tuple-element.34), channel_id=1, source_target_pairs={{0,1},{1,0},{2,3},{3,2},{4,5},{5,4},{6,7},{7,6},{8,9},{9,8},{10,11... | collective-permute-start | bytes 675848 | tf_op jit(solution)/shard_map/ppermute | solution.py:353
  58.5 22.1 %collective-permute-start.4 = (bf16[880,128]{1,0:T(8,128)(2,1)}, bf16[880,128]{1,0:T(8,128)(2,1)}, u32[]{:S(2)}, u32[]{:S(2)}) collective-permute-start(bf16[880,128]{1,0:T(8,128)(2,1)} %get-tuple-element.35), channel_id=1, source_target_pairs={{0,2},{1,3},{2,0},{3,1},{4,6},{5,7},{6,4},{7,5},{8,10},{9,11},{10,... | collective-permute-start | bytes 675848 | tf_op jit(solution)/shard_map/ppermute | solution.py:353
  59.9 20.6 %collective-permute-start.5 = (bf16[880,128]{1,0:T(8,128)(2,1)}, bf16[880,128]{1,0:T(8,128)(2,1)}, u32[]{:S(2)}, u32[]{:S(2)}) collective-permute-start(bf16[880,128]{1,0:T(8,128)(2,1)} %get-tuple-element.36), channel_id=1, source_target_pairs={{0,3},{1,2},{2,1},{3,0},{4,7},{5,6},{6,5},{7,4},{8,11},{9,10},{10,... | collective-permute-start | bytes 675848 | tf_op jit(solution)/shard_map/ppermute | solution.py:353
  81.9 27.5 %collective-permute-start.8 = (bf16[880,128]{1,0:T(8,128)(2,1)S(1)}, bf16[880,128]{1,0:T(8,128)(2,1)S(1)}, u32[]{:S(2)}, u32[]{:S(2)}) collective-permute-start(bf16[880,128]{1,0:T(8,128)(2,1)S(1)} %add_convert_fusion.1), channel_id=1, source_target_pairs={{0,12},{4,8},{8,4},{12,0},{1,13},{5,9},{9,5},{13,1},{2,14},{6,10},... | collective-permute-start | bytes 675848 | tf_op jit(solution)/shard_map/ppermute | solution.py:353
  84.4 25.0 %collective-permute-start.7 = (bf16[880,128]{1,0:T(8,128)(2,1)S(1)}, bf16[880,128]{1,0:T(8,128)(2,1)S(1)}, u32[]{:S(2)}, u32[]{:S(2)}) collective-permute-start(bf16[880,128]{1,0:T(8,128)(2,1)S(1)} %add_convert_fusion.1), channel_id=1, source_target_pairs={{0,8},{4,12},{8,0},{12,4},{1,9},{5,13},{9,1},{13,5},{2,10},{6,14},... | collective-permute-start | bytes 675848 | tf_op jit(solution)/shard_map/ppermute | solution.py:353
  87.8 21.6 %collective-permute-start.6 = (bf16[880,128]{1,0:T(8,128)(2,1)S(1)}, bf16[880,128]{1,0:T(8,128)(2,1)S(1)}, u32[]{:S(2)}, u32[]{:S(2)}) collective-permute-start(bf16[880,128]{1,0:T(8,128)(2,1)S(1)} %add_convert_fusion.1), channel_id=1, source_target_pairs={{0,4},{4,0},{8,12},{12,8},{1,5},{5,1},{9,13},{13,9},{2,6},{6,2},{1... | collective-permute-start | bytes 675848 | tf_op jit(solution)/shard_map/ppermute | solution.py:353
  109.4 17.8 %copy-start.4 = (s32[4,128]{1,0:T(4,128)S(1)}, s32[4,128]{1,0:T(4,128)}, u32[]{:S(2)}) copy-start(s32[4,128]{1,0:T(4,128)} %send_ref.1) | copy-start | bytes 6148
  109.6 6.1 %collective-permute-start.9 = (bf16[128,128]{1,0:T(8,128)(2,1)S(1)}, bf16[128,128]{1,0:T(8,128)(2,1)S(1)}, u32[]{:S(2)}, u32[]{:S(2)}) collective-permute-start(bf16[128,128]{1,0:T(8,128)(2,1)S(1)} %get-tuple-element.56), channel_id=1, source_target_pairs={{4,8},{8,4},{5,9},{9,5},{6,10},{10,6},{7,11},{11,7},{20,24},{24,20... | collective-permute-start | bytes 98312 | tf_op jit(solution)/shard_map/ppermute | solution.py:368
  110.2 7.0 %collective-permute-start.10 = (bf16[128,128]{1,0:T(8,128)(2,1)S(1)}, bf16[128,128]{1,0:T(8,128)(2,1)S(1)}, u32[]{:S(2)}, u32[]{:S(2)}) collective-permute-start(bf16[128,128]{1,0:T(8,128)(2,1)S(1)} %get-tuple-element.58), channel_id=1, source_target_pairs={{0,4},{4,0},{8,12},{12,8},{1,5},{5,1},{9,13},{13,9},{2,6},{6,2},{1... | collective-permute-start | bytes 98312 | tf_op jit(solution)/shard_map/ppermute | solution.py:366
  113.8 16.2 %collective-permute-start.14 = (bf16[880,128]{1,0:T(8,128)(2,1)S(1)}, bf16[880,128]{1,0:T(8,128)(2,1)S(1)}, u32[]{:S(2)}, u32[]{:S(2)}) collective-permute-start(bf16[880,128]{1,0:T(8,128)(2,1)S(1)} %add_convert_fusion.refs_0_), channel_id=1, source_target_pairs={{0,3},{1,2},{2,1},{3,0},{4,7},{5,6},{6,5},{7,4},{8,11},{9,10},{10,... | collective-permute-start | bytes 675848 | tf_op jit(solution)/shard_map/ppermute | solution.py:353
  114.1 15.8 %collective-permute-start.13 = (bf16[880,128]{1,0:T(8,128)(2,1)S(1)}, bf16[880,128]{1,0:T(8,128)(2,1)S(1)}, u32[]{:S(2)}, u32[]{:S(2)}) collective-permute-start(bf16[880,128]{1,0:T(8,128)(2,1)S(1)} %add_convert_fusion.refs_0_), channel_id=1, source_target_pairs={{0,2},{1,3},{2,0},{3,1},{4,6},{5,7},{6,4},{7,5},{8,10},{9,11},{10,... | collective-permute-start | bytes 675848 | tf_op jit(solution)/shard_map/ppermute | solution.py:353
  115.4 14.5 %collective-permute-start.12 = (bf16[880,128]{1,0:T(8,128)(2,1)S(1)}, bf16[880,128]{1,0:T(8,128)(2,1)S(1)}, u32[]{:S(2)}, u32[]{:S(2)}) collective-permute-start(bf16[880,128]{1,0:T(8,128)(2,1)S(1)} %add_convert_fusion.refs_0_), channel_id=1, source_target_pairs={{0,1},{1,0},{2,3},{3,2},{4,5},{5,4},{6,7},{7,6},{8,9},{9,8},{10,11... | collective-permute-start | bytes 675848 | tf_op jit(solution)/shard_map/ppermute | solution.py:353
  115.7 11.5 %collective-permute-start.11 = (bf16[128,128]{1,0:T(8,128)(2,1)S(1)}, bf16[128,128]{1,0:T(8,128)(2,1)S(1)}, u32[]{:S(2)}, u32[]{:S(2)}) collective-permute-start(bf16[128,128]{1,0:T(8,128)(2,1)S(1)} %get-tuple-element.57), channel_id=1, source_target_pairs={{0,2},{2,0},{1,3},{3,1},{4,6},{6,4},{5,7},{7,5},{8,10},{10,8},{9,1... | collective-permute-start | bytes 98312 | tf_op jit(solution)/shard_map/ppermute | solution.py:366

commit v5 on v4

--- a/solution.py
+++ b/solution.py
@@ -25,6 +25,18 @@
 
 def dot(a, b, dims):
     return lax.dot_general(a, b, dims, preferred_element_type=jnp.float32)
+
+
+def from_neighbours(refs, axis):
+    odd = (lax.axis_index(axis) & 1) != 0
+    first = refs[0][...].astype(jnp.float32)
+    second = refs[1][...].astype(jnp.float32) if len(refs) > 1 else jnp.zeros_like(first)
+    return jnp.where(odd, first, second), jnp.where(odd, second, first)
+
+
+def over_edges(down, up, axis):
+    odd = (lax.axis_index(axis) & 1) != 0
+    return jnp.where(odd, down, up), jnp.where(odd, up, down)
 
 
 def fetch(map_hbm, index, sems, first, length, parts):
@@ -46,9 +58,9 @@
 
 
 def forward_kernel(
-    classes, map_hbm, sparse_ref, own_ref, halo_refs, weight_ref, class_ref, label_ref,
+    classes, map_hbm, sparse_ref, own_hbm, x_refs, y_refs, weight_hbm, class_ref, label_ref,
     dpre_ref, dmixed_ref, conv_ref, flipped_ref,
-    table, turned, rows, wide, columns, side, total, sems, *index,
+    own_ref, weight_ref, load_sems, table, turned, rows, wide, columns, side, total, sems, *index,
 ):
     voxels, chans = dpre_ref.shape
     looped = len(index) // STREAMS
@@ -56,12 +68,18 @@
     stream = voxels // STREAMS
     block = STREAMS * SEGMENT
     share = SEGMENT // BY_MATMUL
+    own_copy = pltpu.make_async_copy(own_hbm, own_ref, load_sems.at[0])
+    own_copy.start()
+    weight_copy = pltpu.make_async_copy(weight_hbm, weight_ref, load_sems.at[1])
+    weight_copy.start()
     ready, later = fetch(map_hbm, index, sems, 0, stream, (0, FIRST_PART, stream))
-    width = halo_refs[0].shape[0]
+    own_copy.wait()
+    width = x_refs[0].shape[0]
     table[:voxels, :] = own_ref[...].astype(jnp.float32)
-    for n, halo in enumerate(halo_refs):
+    halos = from_neighbours(x_refs, "tx") + from_neighbours(y_refs, "ty")
+    for n, halo in enumerate(halos):
         start = voxels + n * width
-        table[start : start + width, :] = halo[...].astype(jnp.float32)
+        table[start : start + width, :] = halo
     filled = voxels + 4 * width
     table[filled:, :] = jnp.zeros((table.shape[0] - filled, chans), jnp.float32)
     for n in range(filled // chans):
@@ -71,6 +89,7 @@
     conv_ref[pl.ds(offsets * chans, conv_ref.shape[0] - offsets * chans), :] = jnp.zeros(
         (conv_ref.shape[0] - offsets * chans, chans), jnp.float32
     )
+    weight_copy.wait()
     for k in range(offsets):
         at = slice(k * chans, (k + 1) * chans)
         turned_weight = weight_ref[at, :].T
@@ -135,13 +154,13 @@
         conv_ref[k * chans : (k + 1) * chans, :] = total[:, k * chans : (k + 1) * chans].T
 
 
-def forward(map_flat, sparse, features, incoming, weights, class_t, label_blocks, classes, reduce_rows, table_rows):
+def forward(map_flat, sparse, features, from_x, from_y, weights, class_t, label_blocks, classes, reduce_rows, table_rows):
     voxels, chans = features.shape
     offsets = weights.shape[0] // chans
     looped = offsets - BY_MATMUL
     stream = voxels // STREAMS
     block = STREAMS * SEGMENT
-    filled = voxels + sum(halo.shape[0] for halo in incoming)
+    filled = voxels + 4 * from_x[0].shape[0]
     return pl.pallas_call(
         functools.partial(forward_kernel, classes),
         out_shape=(
@@ -150,9 +169,12 @@
             jax.ShapeDtypeStruct((reduce_rows, chans), jnp.float32),
             jax.ShapeDtypeStruct(weights.shape, jnp.bfloat16),
         ),
-        in_specs=[HBM, VMEM, VMEM, [VMEM] * 4, VMEM, VMEM, VMEM],
+        in_specs=[HBM, VMEM, HBM, [VMEM] * len(from_x), [VMEM] * len(from_y), HBM, VMEM, VMEM],
         out_specs=(VMEM, VMEM, VMEM, VMEM),
         scratch_shapes=[
+            pltpu.VMEM(features.shape, jnp.bfloat16),
+            pltpu.VMEM(weights.shape, jnp.bfloat16),
+            pltpu.SemaphoreType.DMA((2,)),
             pltpu.VMEM((table_rows, chans), jnp.float32),
             pltpu.VMEM((chans, filled), jnp.bfloat16),
             pltpu.VMEM((looped, block, chans), jnp.float32),
@@ -163,20 +185,22 @@
             pltpu.SemaphoreType.DMA((2, looped * STREAMS)),
         ]
         + [pltpu.SMEM((stream,), jnp.int32)] * (looped * STREAMS),
-        compiler_params=pltpu.CompilerParams(vmem_limit_bytes=40 << 20),
+        compiler_params=pltpu.CompilerParams(vmem_limit_bytes=20 << 20),
         cost_estimate=pl.CostEstimate(
             flops=4 * voxels * offsets * chans * chans, bytes_accessed=150 << 20, transcendentals=0
         ),
         name="forward",
-    )(map_flat, sparse, features, incoming, weights, class_t, label_blocks)
+    )(map_flat, sparse, features, from_x, from_y, weights, class_t, label_blocks)
 
 
 def scatter_kernel(first, offsets, has_before, map_hbm, dpre_ref, weight_ref, *refs):
     refs = list(refs)
     before = refs.pop(0) if has_before else None
-    out_ref, sems = refs[:2]
-    tables = refs[2 : 2 + offsets]
-    index = refs[2 + offsets :]
+    out_ref = refs.pop(0)
+    back_refs = [refs.pop(0) for _ in range(4)] if has_before else []
+    sems = refs.pop(0)
+    tables = refs[:offsets]
+    index = refs[offsets:]
     streams, stream, chans = dpre_ref.shape
     share = stream // SCATTER_STEPS
     copies, = fetch(map_hbm, index, sems, first * streams, stream, (0, stream))
@@ -207,23 +231,31 @@
         return carry
 
     lax.fori_loop(0, tiles, finish, 0)
-
-
-def scatter(map_flat, dpre, flipped, before, first, offsets, table_rows):
+    if back_refs:
+        width = back_refs[0].shape[0]
+        voxels = streams * stream
+        halos = [out_ref[voxels + n * width : voxels + (n + 1) * width, :] for n in range(4)]
+        picked = over_edges(halos[2], halos[3], "ty") + over_edges(halos[0], halos[1], "tx")
+        for back_ref, value in zip(back_refs, picked):
+            back_ref[...] = value.astype(jnp.bfloat16)
+
+
+def scatter(map_flat, dpre, flipped, before, first, offsets, table_rows, width):
     voxels, chans = dpre.shape
     stream = voxels // SCATTER_STREAMS
     has_before = before is not None
     return pl.pallas_call(
         functools.partial(scatter_kernel, first, offsets, has_before),
-        out_shape=jax.ShapeDtypeStruct((table_rows, chans), jnp.float32),
+        out_shape=[jax.ShapeDtypeStruct((table_rows, chans), jnp.float32)]
+        + [jax.ShapeDtypeStruct((width, chans), jnp.bfloat16)] * (4 if has_before else 0),
         in_specs=[HBM, VMEM, VMEM] + ([VMEM] if has_before else []),
-        out_specs=VMEM,
+        out_specs=[VMEM] * (5 if has_before else 1),
         scratch_shapes=[
             pltpu.SemaphoreType.DMA((1, offsets * SCATTER_STREAMS)),
         ]
         + [pltpu.VMEM((table_rows, chans), jnp.float32)] * offsets
         + [pltpu.SMEM((stream,), jnp.int32)] * (offsets * SCATTER_STREAMS),
-        compiler_params=pltpu.CompilerParams(vmem_limit_bytes=40 << 20),
+        compiler_params=pltpu.CompilerParams(vmem_limit_bytes=28 << 20),
         cost_estimate=pl.CostEstimate(
             flops=2 * voxels * offsets * chans * chans, bytes_accessed=40 << 20, transcendentals=0
         ),
@@ -234,8 +266,13 @@
     )
 
 
-def finish_kernel(dmixed_ref, dext_ref, send_ref, back_ref, out_ref):
+def finish_kernel(dmixed_ref, dext_ref, send_ref, x_refs, y_refs, out_ref, back_ref):
     voxels, chans = out_ref.shape
+    width = x_refs[0].shape[0]
+    low_x, high_x = from_neighbours(x_refs, "tx")
+    low_y, high_y = from_neighbours(y_refs, "ty")
+    for n, value in enumerate((high_x, low_x, high_y, low_y)):
+        back_ref[n * width : (n + 1) * width, :] = value.astype(jnp.bfloat16)
     height = voxels // 8
 
     def step(t, carry):
@@ -248,24 +285,31 @@
     lax.fori_loop(0, voxels // height, step, 0)
 
 
-def finish(dmixed, dext, send_flat, back):
+def finish(dmixed, dext, send_flat, from_x, from_y):
     return pl.pallas_call(
         finish_kernel,
         out_shape=jax.ShapeDtypeStruct(dmixed.shape, jnp.float32),
-        in_specs=[VMEM] * 4,
+        in_specs=[VMEM, VMEM, VMEM, [VMEM] * len(from_x), [VMEM] * len(from_y)],
         out_specs=VMEM,
-        compiler_params=pltpu.CompilerParams(vmem_limit_bytes=40 << 20),
+        scratch_shapes=[pltpu.VMEM((send_flat.shape[1], dmixed.shape[1]), jnp.bfloat16)],
+        compiler_params=pltpu.CompilerParams(vmem_limit_bytes=12 << 20),
         cost_estimate=pl.CostEstimate(flops=1 << 28, bytes_accessed=4 << 20, transcendentals=0),
         name="finish",
-    )(dmixed, dext, send_flat, back)
-
-
-def outgoing_kernel(axes, send_ref, own_ref, *refs):
-    *out_refs, table, sent = refs
+    )(dmixed, dext, send_flat, from_x, from_y)
+
+
+def outgoing_kernel(axes, send_hbm, own_hbm, *refs):
+    *out_refs, send_ref, own_ref, sems, table, sent = refs
     voxels, chans = own_ref.shape
+    send_copy = pltpu.make_async_copy(send_hbm, send_ref, sems.at[0])
+    send_copy.start()
+    own_copy = pltpu.make_async_copy(own_hbm, own_ref, sems.at[1])
+    own_copy.start()
+    own_copy.wait()
     width = send_ref.shape[1]
     table[:voxels, :] = own_ref[...].astype(jnp.float32)
     table[voxels:, :] = jnp.zeros((table.shape[0] - voxels, chans), jnp.float32)
+    send_copy.wait()
     for s in range(4):
 
         def step(t, carry, s=s):
@@ -278,9 +322,7 @@
     lists = [sent[s * width : (s + 1) * width, :] for s in range(4)]
     picked = []
     for axis, (up, down) in zip(axes, ((2, 3), (0, 1))):
-        odd = (lax.axis_index(axis) & 1) != 0
-        picked.append(jnp.where(odd, lists[down], lists[up]))
-        picked.append(jnp.where(odd, lists[up], lists[down]))
+        picked.extend(over_edges(lists[down], lists[up], axis))
     for out_ref, value in zip(out_refs, picked):
         out_ref[...] = value.astype(jnp.bfloat16)
 
@@ -291,13 +333,17 @@
     return pl.pallas_call(
         functools.partial(outgoing_kernel, ("ty", "tx")),
         out_shape=[jax.ShapeDtypeStruct((width, chans), jnp.bfloat16)] * 4,
-        in_specs=[pl.BlockSpec(memory_space=pltpu.SMEM), VMEM],
+        in_specs=[HBM, HBM],
         out_specs=[VMEM] * 4,
         scratch_shapes=[
+            pltpu.SMEM(send_rows.shape, jnp.int32),
+            pltpu.VMEM(features.shape, jnp.bfloat16),
+            pltpu.SemaphoreType.DMA((2,)),
             pltpu.VMEM((voxels + 8, chans), jnp.float32),
             pltpu.VMEM((4 * width, chans), jnp.float32),
         ],
-        compiler_params=pltpu.CompilerParams(vmem_limit_bytes=16 << 20),
+        compiler_params=pltpu.CompilerParams(vmem_limit_bytes=60 << 20),
+        cost_estimate=pl.CostEstimate(flops=0, bytes_accessed=8 << 20, transcendentals=0),
         name="outgoing",
     )(send_rows, features)
 
@@ -320,20 +366,20 @@
                 if start <= conv_rows < start + height:
                     at = conv_rows - start
                     value = piece_ref[at : at + HEAD_ROWS, :].astype(jnp.float32) * scale
-                    head_ref[...] = value
-
-
-def assemble(pieces, axes, scale, conv_rows):
+                    head_ref[...] = value[: head_ref.shape[0], :]
+
+
+def assemble(pieces, axes, scale, conv_rows, classes):
     chans = pieces[0].shape[1]
     return pl.pallas_call(
         functools.partial(assemble_kernel, axes, scale, conv_rows),
         out_shape=(
             jax.ShapeDtypeStruct((conv_rows, chans), jnp.float32),
-            jax.ShapeDtypeStruct((HEAD_ROWS, chans), jnp.float32),
+            jax.ShapeDtypeStruct((classes, chans), jnp.float32),
         ),
         in_specs=[VMEM] * len(pieces),
         out_specs=(VMEM, VMEM),
-        compiler_params=pltpu.CompilerParams(vmem_limit_bytes=16 << 20),
+        compiler_params=pltpu.CompilerParams(vmem_limit_bytes=12 << 20),
         name="assemble",
     )(*pieces)
 
@@ -362,18 +408,10 @@
 
 def swap_edges(over_even, over_odd, axis):
     even_pairs, odd_pairs = edge_pairs(axis)
-    odd = (lax.axis_index(axis) & 1) != 0
-    first = lax.ppermute(over_even, axis, even_pairs)
+    got = [lax.ppermute(over_even, axis, even_pairs)]
     if odd_pairs:
-        second = lax.ppermute(over_odd, axis, odd_pairs)
-    else:
-        second = jnp.zeros_like(first)
-    return jnp.where(odd, first, second), jnp.where(odd, second, first)
-
-
-def by_parity(down, up, axis):
-    odd = (lax.axis_index(axis) & 1) != 0
-    return jnp.where(odd, down, up), jnp.where(odd, up, down)
+        got.append(lax.ppermute(over_odd, axis, odd_pairs))
+    return got
 
 
 def on_device(features, conv_weight, classifier, send_rows, neighbour_map, labels):
@@ -390,8 +428,8 @@
     height = reduce_rows // pieces
 
     even_y, odd_y, even_x, odd_x = outgoing(send_rows, features)
-    low_y, high_y = swap_edges(even_y, odd_y, "ty")
-    low_x, high_x = swap_edges(even_x, odd_x, "tx")
+    from_y = swap_edges(even_y, odd_y, "ty")
+    from_x = swap_edges(even_x, odd_x, "tx")
 
     zero_row = voxels + 4 * width
     moved = jnp.where(neighbour_map > voxels, neighbour_map - 1, neighbour_map)
@@ -408,20 +446,24 @@
         .reshape(voxels // block, 1, block)
     )
     dpre, dmixed, part, flipped = forward(
-        map_flat, sparse, features, [low_x, high_x, low_y, high_y], weights, class_t, label_blocks,
+        map_flat, sparse, features, from_x, from_y, weights, class_t, label_blocks,
         classes, reduce_rows, table_rows,
     )
 
     chunks = [(c * offsets // CHUNKS, (c + 1) * offsets // CHUNKS) for c in range(CHUNKS)]
+
+    halo = []
 
     def scatter_beside(sent, before):
         first, last = chunks.pop(0)
         held = (sent, dpre) if before is None else (sent, dpre, before)
         held = lax.optimization_barrier(held)
-        return held[0], scatter(
+        dext, *blocks = scatter(
             map_flat, held[1], flipped, None if before is None else held[2],
-            first, last - first, table_rows,
+            first, last - first, table_rows, width,
         )
+        halo.extend(blocks)
+        return held[0], dext
 
     mine = group_index(square)
     sent = []
@@ -441,7 +483,7 @@
         if chunks:
             own, dext = scatter_beside(own, dext)
         got = [own] + [exchange(own, ("tx",), m * stride) for m in range(1, radix)]
-        got, dext = lax.optimization_barrier((got, dext))
+        got, dext, halo = lax.optimization_barrier((got, dext, halo))
         got = [piece.astype(jnp.float32) for piece in got]
         while len(got) > 1:
             got = [a + b for a, b in zip(got[::2], got[1::2])]
@@ -450,17 +492,21 @@
     while chunks:
         own, dext = scatter_beside(own, dext)
 
-    halo = dext[voxels : voxels + 4 * width].astype(jnp.bfloat16).reshape(4, width, chans)
-    back_3, back_2 = swap_edges(*by_parity(halo[2], halo[3], "ty"), "ty")
-    back_1, back_0 = swap_edges(*by_parity(halo[0], halo[1], "tx"), "tx")
-    back = jnp.concatenate([back_0, back_1, back_2, back_3], axis=0)
-    grad_input = finish(dmixed, dext, send_rows.reshape(1, -1), back)
-
-    own = own.astype(jnp.bfloat16)
-    everywhere = [own] + [exchange(own, square, d) for d in range(1, pieces)]
+    from_y = swap_edges(halo[0], halo[1], "ty")
+    from_x = swap_edges(halo[2], halo[3], "tx")
+    everywhere = {0: own.astype(jnp.bfloat16)}
+    bit = pieces // 2
+    while bit:
+        if bit == 1:
+            everywhere, from_x, from_y = lax.optimization_barrier((everywhere, from_x, from_y))
+        for d, piece in list(everywhere.items()):
+            everywhere[d | bit] = exchange(piece, square, bit)
+        bit //= 2
+    grad_input = finish(dmixed, dext, send_rows.reshape(1, -1), from_x, from_y)
+    everywhere = [everywhere[d] for d in range(pieces)]
     count = voxels * lax.axis_size("tx") * lax.axis_size("ty") * lax.axis_size("rep")
-    conv, head = assemble(everywhere, square, 1.0 / math.sqrt(count), offsets * chans)
-    return grad_input, conv.reshape(offsets, chans, chans), head[:classes].T
+    conv, head = assemble(everywhere, square, 1.0 / math.sqrt(count), offsets * chans, classes)
+    return grad_input, conv.reshape(offsets, chans, chans), head.T
 
 
 def solution(mesh):

time: 132 us -> 123 us (0.932)
  waiting for transfers between devices: 10.6 us -> 4.21 us
  starting transfers between devices: 20.5 us -> 18.4 us
  local copies, waits for them, and re-layouts: 7.38 us -> 5.8 us
    ppermute x6, waiting for transfers between devices: 10.6 us -> 4.19 us  [the longest x4 4.19 us: swap_edges(): got = [lax.ppermute(over_even, axis, even_pairs)]]
    ppermute x6, starting transfers between devices: 10.8 us -> 8.59 us  [the longest x4 7.29 us: swap_edges(): got = [lax.ppermute(over_even, axis, even_pairs)]]
    unnamed x14 -> x10, local copies, waits for them, and re-layouts: 5.17 us -> 4.17 us
  transfers between devices with their start and end apart: 15 -> 15, of which waited for: 2 -> 3; matrix products, arithmetic and copies ran while one was open for 1% -> 1% of each run, Pallas kernels for 34% -> 37%
where the time goes in v5:
time: 123 us
  Pallas kernels  91.1 us (74%)
  starting transfers between devices  18.4 us (15%)
  local copies, waits for them, and re-layouts  5.8 us (5%)
  waiting for transfers between devices  4.21 us (3%)
  other arithmetic  2.48 us (2%)
    pallas_call x2, Pallas kernels, scatter(): pl.pallas_call(functools.partial(scatter_kernel, first, offsets, has_befo...  42.4 us
    pallas_call x1, Pallas kernels, forward(): pl.pallas_call(functools.partial(forward_kernel, classes), out_shape=(jax...  41.8 us
    ppermute x9, starting transfers between devices, exchange(): lax.ppermute(shard, axes, [(i, i ^ distance) for i in range(group_size(ax...  9.82 us
    ppermute x4, starting transfers between devices, swap_edges(): got = [lax.ppermute(over_even, axis, even_pairs)]  7.29 us
    ppermute x4, waiting for transfers between devices, swap_edges(): got = [lax.ppermute(over_even, axis, even_pairs)]  4.19 us
    unnamed x10, local copies, waits for them, and re-layouts  4.17 us
    pallas_call x1, Pallas kernels, outgoing(): pl.pallas_call(functools.partial(outgoing_kernel, ('ty', 'tx')), out_shap...  2.79 us
    pallas_call x1, Pallas kernels, finish(): pl.pallas_call(finish_kernel, out_shape=jax.ShapeDtypeStruct(dmixed.shape...  2.73 us
  transfers between devices with their start and end apart: 15, of which 3 were waited for; matrix products, arithmetic and copies ran while one was open for 1% of the time, Pallas kernels for 37%

profile of v5, /device:TPU:0, one launch (start us, length us, event | category | flops | bytes accessed | tf_op | source)
XLA Modules:
  0.0 122.8 jit_solution(12545623653789659252)
XLA Ops:
  0.6 2.8 %outgoing.1 = (bf16[128,128]{1,0:T(8,128)(2,1)}, bf16[128,128]{1,0:T(8,128)(2,1)}, bf16[128,128]{1,0:T(8,128)(2,1)}, bf16[128,128]{1,0:T(8,128)(2,1)}) custom-call(s32[4,128]{1,0:T(4,128)} %send_hbm.1, bf16[2048,128]{1,0:T(8,128)(2,1)} %own_hbm.3), custom_call_target="tpu_custom_call" | custom-call | bytes 8388608 | tf_op jit(solution)/shard_map/outgoing/pallas_call | solution.py:333
  3.4 3.1 %collective-permute-start = (bf16[128,128]{1,0:T(8,128)(2,1)}, bf16[128,128]{1,0:T(8,128)(2,1)S(1)}, u32[]{:S(2)}, u32[]{:S(2)}) collective-permute-start(bf16[128,128]{1,0:T(8,128)(2,1)} %get-tuple-element.40), channel_id=1, source_target_pairs={{0,4},{4,0},{8,12},{12,8},{1,5},{5,1},{9,13},{13,9},{2,6},{6,2},{1... | collective-permute-start | bytes 98312 | tf_op jit(solution)/shard_map/ppermute | solution.py:411
  6.5 0.7 collective-permute-start.1
  7.2 1.6 %collective-permute-start.2 = (bf16[128,128]{1,0:T(8,128)(2,1)}, bf16[128,128]{1,0:T(8,128)(2,1)S(1)}, u32[]{:S(2)}, u32[]{:S(2)}) collective-permute-start(bf16[128,128]{1,0:T(8,128)(2,1)} %get-tuple-element.42), channel_id=1, source_target_pairs={{0,2},{2,0},{1,3},{3,1},{4,6},{6,4},{5,7},{7,5},{8,10},{10,8},{9,1... | collective-permute-start | bytes 98312 | tf_op jit(solution)/shard_map/ppermute | solution.py:411
  8.7 1.0 fusion
  9.8 0.7 pad.4.class_ref
  10.5 0.8 collective-permute-done.2.y_refs_0_
  11.4 1.0 copy-done.1
  12.4 1.2 copy-done.3
  13.6 0.7 copy-done.4
  14.3 41.8 %forward.1 = (f32[2048,128]{1,0:T(8,128)S(1)}, f32[2048,128]{1,0:T(8,128)S(1)}, f32[3520,128]{1,0:T(8,128)S(1)}, bf16[3456,128]{1,0:T(8,128)(2,1)S(1)}) custom-call(s32[55296]{0:T(1024)S(1)} %reshape.30.map_hbm, s32[8,8,256]{2,1,0:T(8,128)S(1)} %bitcast.15, bf16[2048,128]{1,0:T(8,128)(2,1)S(1)} %copy-done.1, ...), custom_call_target="tpu_custom_call" | custom-call | flops 3623878656 | bytes 157286400 | tf_op jit(solution)/shard_map/forward/pallas_call | solution.py:164
  56.1 1.3 %copy-done = f32[3520,128]{1,0:T(8,128)} copy-done((f32[3520,128]{1,0:T(8,128)}, f32[3520,128]{1,0:T(8,128)S(1)}, u32[]{:S(2)}) %copy-start) | copy-done | bytes 1802264
  57.3 0.9 dynamic-slice_convert_fusion
  58.2 1.5 %collective-permute-start.4 = (bf16[880,128]{1,0:T(8,128)(2,1)}, bf16[880,128]{1,0:T(8,128)(2,1)}, u32[]{:S(2)}, u32[]{:S(2)}) collective-permute-start(bf16[880,128]{1,0:T(8,128)(2,1)} %get-tuple-element.47), channel_id=1, source_target_pairs={{0,2},{1,3},{2,0},{3,1},{4,6},{5,7},{6,4},{7,5},{8,10},{9,11},{10,... | collective-permute-start | bytes 675848 | tf_op jit(solution)/shard_map/ppermute | solution.py:399
  59.7 0.4 collective-permute-start.5
  60.1 20.2 %scatter_0.1.refs_0_ = f32[2592,128]{1,0:T(8,128)S(1)} custom-call(s32[55296]{0:T(1024)S(1)} %reshape.30.map_hbm, f32[2,1024,128]{2,1,0:T(8,128)S(1)} %bitcast.13, bf16[3456,128]{1,0:T(8,128)(2,1)S(1)} %get-tuple-element.50.weight_ref), custom_call_target="tpu_custom_call" | custom-call | flops 872415232 | bytes 41943040 | tf_op jit(solution)/shard_map/scatter_0/pallas_call | solution.py:247
  80.3 0.0 collective-permute-done.3
  80.3 0.0 collective-permute-done.4
  80.3 1.4 %add_convert_fusion.1 = bf16[880,128]{1,0:T(8,128)(2,1)S(1)} fusion(bf16[880,128]{1,0:T(8,128)(2,1)} %collective-permute-done.5, bf16[880,128]{1,0:T(8,128)(2,1)} %collective-permute-done.4, bf16[880,128]{1,0:T(8,128)(2,1)S(1)} %collective-permute-done.3, f32[3520,128]{1,0:T(8,128)} %copy-done, s32[]{:T(128)S(6)} %select_n.22), kind=kLoop, calls=%fused_computation.2 | loop fusion | flops 788480 | bytes 1351684 | tf_op jit(solution)/shard_map/convert_element_type | solution.py:482
  81.7 2.5 %collective-permute-start.8 = (bf16[880,128]{1,0:T(8,128)(2,1)S(1)}, bf16[880,128]{1,0:T(8,128)(2,1)S(1)}, u32[]{:S(2)}, u32[]{:S(2)}) collective-permute-start(bf16[880,128]{1,0:T(8,128)(2,1)S(1)} %add_convert_fusion.1), channel_id=1, source_target_pairs={{0,12},{4,8},{8,4},{12,0},{1,13},{5,9},{9,5},{13,1},{2,14},{6,10},... | collective-permute-start | bytes 675848 | tf_op jit(solution)/shard_map/ppermute | solution.py:399
  84.2 3.4 %collective-permute-start.7 = (bf16[880,128]{1,0:T(8,128)(2,1)S(1)}, bf16[880,128]{1,0:T(8,128)(2,1)S(1)}, u32[]{:S(2)}, u32[]{:S(2)}) collective-permute-start(bf16[880,128]{1,0:T(8,128)(2,1)S(1)} %add_convert_fusion.1), channel_id=1, source_target_pairs={{0,8},{4,12},{8,0},{12,4},{1,9},{5,13},{9,1},{13,5},{2,10},{6,14},... | collective-permute-start | bytes 675848 | tf_op jit(solution)/shard_map/ppermute | solution.py:399
  87.6 22.2 %scatter_13.1 = (f32[2592,128]{1,0:T(8,128)S(1)}, bf16[128,128]{1,0:T(8,128)(2,1)S(1)}, bf16[128,128]{1,0:T(8,128)(2,1)}, bf16[128,128]{1,0:T(8,128)(2,1)S(1)}, bf16[128,128]{1,0:T(8,128)(2,1)S(1)}) custom-call(s32[55296]{0:T(1024)S(1)} %reshape.30.map_hbm, f32[2,1024,128]{2,1,0:T(8,128)S(1)} %bitcast.14, ...), custom_call_target="tpu_custom_call" | custom-call | flops 939524096 | bytes 41943040 | tf_op jit(solution)/shard_map/scatter_13/pallas_call | solution.py:247
  109.8 0.1 add_convert_fusion.refs_0_
  110.0 1.5 %collective-permute-start.9 = (bf16[880,128]{1,0:T(8,128)(2,1)S(1)}, bf16[880,128]{1,0:T(8,128)(2,1)S(1)}, u32[]{:S(2)}, u32[]{:S(2)}) collective-permute-start(bf16[880,128]{1,0:T(8,128)(2,1)S(1)} %add_convert_fusion.refs_0_), channel_id=1, source_target_pairs={{0,2},{1,3},{2,0},{3,1},{4,6},{5,7},{6,4},{7,5},{8,10},{9,11},{10,... | collective-permute-start | bytes 675848 | tf_op jit(solution)/shard_map/ppermute | solution.py:399
  111.5 2.0 %collective-permute-start.10 = (bf16[128,128]{1,0:T(8,128)(2,1)S(1)}, bf16[128,128]{1,0:T(8,128)(2,1)S(1)}, u32[]{:S(2)}, u32[]{:S(2)}) collective-permute-start(bf16[128,128]{1,0:T(8,128)(2,1)S(1)} %get-tuple-element.67), channel_id=1, source_target_pairs={{0,4},{4,0},{8,12},{12,8},{1,5},{5,1},{9,13},{13,9},{2,6},{6,2},{1... | collective-permute-start | bytes 98312 | tf_op jit(solution)/shard_map/ppermute | solution.py:411
  113.5 0.7 collective-permute-start.11
  114.2 0.6 collective-permute-start.12
  114.8 0.6 collective-permute-done.10.x_refs_0_
  115.4 2.7 %collective-permute-done.12.y_refs_0_ = bf16[128,128]{1,0:T(8,128)(2,1)S(1)} collective-permute-done((bf16[128,128]{1,0:T(8,128)(2,1)S(1)}, bf16[128,128]{1,0:T(8,128)(2,1)S(1)}, u32[]{:S(2)}, u32[]{:S(2)}) %collective-permute-start.12) | collective-permute-done | bytes 32800 | tf_op jit(solution)/shard_map/ppermute | solution.py:411
  118.2 0.5 collective-permute-start.14
  118.7 2.7 %finish.1 = f32[2048,128]{1,0:T(8,128)} custom-call(f32[2048,128]{1,0:T(8,128)S(1)} %get-tuple-element.43.dmixed_ref, f32[2592,128]{1,0:T(8,128)S(1)} %get-tuple-element.62.dext_ref, s32[1,512]{1,0:T(1,128)S(1)} %bitcast.16, bf16[128,128]{1,0:T(8,128)(2,1)S(1)} %collective-permute-done.10.x_refs_0_, bf16[128,128]{1,0:T(8,128)(2,1)S(1)} %collective-permute-done.11.x_refs_1_, ...), custom_call_target="tpu_custom_call" | custom-call | flops 268435456 | bytes 4194304 | tf_op jit(solution)/shard_map/finish/pallas_call | solution.py:289
  121.4 1.4 %assemble.1 = (f32[3456,128]{1,0:T(8,128)}, f32[19,128]{1,0:T(8,128)}) custom-call(bf16[880,128]{1,0:T(8,128)(2,1)S(1)} %add_convert_fusion.refs_0_, bf16[880,128]{1,0:T(8,128)(2,1)S(1)} %collective-permute-done.13.refs_1_, bf16[880,128]{1,0:T(8,128)(2,1)S(1)} %collective-permute-done.9.refs_2_, bf16[880,128]{1,0:T(8,128)(2,1)S(1)} %collective-permute-done.14.refs_3_), custom_call_target="tpu_custom_call" | custom-call | tf_op jit(solution)/shard_map/assemble/pallas_call | solution.py:374
  (21 shorter events, 0.1 us)
Async XLA Ops:
  3.4 7.1 %collective-permute-start = (bf16[128,128]{1,0:T(8,128)(2,1)}, bf16[128,128]{1,0:T(8,128)(2,1)S(1)}, u32[]{:S(2)}, u32[]{:S(2)}) collective-permute-start(bf16[128,128]{1,0:T(8,128)(2,1)} %get-tuple-element.40), channel_id=1, source_target_pairs={{0,4},{4,0},{8,12},{12,8},{1,5},{5,1},{9,13},{13,9},{2,6},{6,2},{1... | collective-permute-start | bytes 98312 | tf_op jit(solution)/shard_map/ppermute | solution.py:411
  6.5 4.0 %collective-permute-start.1 = (bf16[128,128]{1,0:T(8,128)(2,1)}, bf16[128,128]{1,0:T(8,128)(2,1)S(1)}, u32[]{:S(2)}, u32[]{:S(2)}) collective-permute-start(bf16[128,128]{1,0:T(8,128)(2,1)} %get-tuple-element.41), channel_id=1, source_target_pairs={{4,8},{8,4},{5,9},{9,5},{6,10},{10,6},{7,11},{11,7},{20,24},{24,20... | collective-permute-start | bytes 98312 | tf_op jit(solution)/shard_map/ppermute | solution.py:413
  7.2 4.2 %collective-permute-start.2 = (bf16[128,128]{1,0:T(8,128)(2,1)}, bf16[128,128]{1,0:T(8,128)(2,1)S(1)}, u32[]{:S(2)}, u32[]{:S(2)}) collective-permute-start(bf16[128,128]{1,0:T(8,128)(2,1)} %get-tuple-element.42), channel_id=1, source_target_pairs={{0,2},{2,0},{1,3},{3,1},{4,6},{6,4},{5,7},{7,5},{8,10},{10,8},{9,1... | collective-permute-start | bytes 98312 | tf_op jit(solution)/shard_map/ppermute | solution.py:411
  11.4 1.0 copy-start.1
  12.4 1.2 copy-start.3
  13.6 0.7 copy-start.4
  56.1 1.3 %copy-start = (f32[3520,128]{1,0:T(8,128)}, f32[3520,128]{1,0:T(8,128)S(1)}, u32[]{:S(2)}) copy-start(f32[3520,128]{1,0:T(8,128)S(1)} %get-tuple-element.44) | copy-start | bytes 5406724
  58.2 22.1 %collective-permute-start.3 = (bf16[880,128]{1,0:T(8,128)(2,1)}, bf16[880,128]{1,0:T(8,128)(2,1)S(1)}, u32[]{:S(2)}, u32[]{:S(2)}) collective-permute-start(bf16[880,128]{1,0:T(8,128)(2,1)} %get-tuple-element.46), channel_id=1, source_target_pairs={{0,1},{1,0},{2,3},{3,2},{4,5},{5,4},{6,7},{7,6},{8,9},{9,8},{10,11... | collective-permute-start | bytes 675848 | tf_op jit(solution)/shard_map/ppermute | solution.py:399
  58.2 22.1 %collective-permute-start.4 = (bf16[880,128]{1,0:T(8,128)(2,1)}, bf16[880,128]{1,0:T(8,128)(2,1)}, u32[]{:S(2)}, u32[]{:S(2)}) collective-permute-start(bf16[880,128]{1,0:T(8,128)(2,1)} %get-tuple-element.47), channel_id=1, source_target_pairs={{0,2},{1,3},{2,0},{3,1},{4,6},{5,7},{6,4},{7,5},{8,10},{9,11},{10,... | collective-permute-start | bytes 675848 | tf_op jit(solution)/shard_map/ppermute | solution.py:399
  59.7 20.6 %collective-permute-start.5 = (bf16[880,128]{1,0:T(8,128)(2,1)}, bf16[880,128]{1,0:T(8,128)(2,1)}, u32[]{:S(2)}, u32[]{:S(2)}) collective-permute-start(bf16[880,128]{1,0:T(8,128)(2,1)} %get-tuple-element.48), channel_id=1, source_target_pairs={{0,3},{1,2},{2,1},{3,0},{4,7},{5,6},{6,5},{7,4},{8,11},{9,10},{10,... | collective-permute-start | bytes 675848 | tf_op jit(solution)/shard_map/ppermute | solution.py:399
  81.7 28.1 %collective-permute-start.8 = (bf16[880,128]{1,0:T(8,128)(2,1)S(1)}, bf16[880,128]{1,0:T(8,128)(2,1)S(1)}, u32[]{:S(2)}, u32[]{:S(2)}) collective-permute-start(bf16[880,128]{1,0:T(8,128)(2,1)S(1)} %add_convert_fusion.1), channel_id=1, source_target_pairs={{0,12},{4,8},{8,4},{12,0},{1,13},{5,9},{9,5},{13,1},{2,14},{6,10},... | collective-permute-start | bytes 675848 | tf_op jit(solution)/shard_map/ppermute | solution.py:399
  84.2 25.7 %collective-permute-start.7 = (bf16[880,128]{1,0:T(8,128)(2,1)S(1)}, bf16[880,128]{1,0:T(8,128)(2,1)S(1)}, u32[]{:S(2)}, u32[]{:S(2)}) collective-permute-start(bf16[880,128]{1,0:T(8,128)(2,1)S(1)} %add_convert_fusion.1), channel_id=1, source_target_pairs={{0,8},{4,12},{8,0},{12,4},{1,9},{5,13},{9,1},{13,5},{2,10},{6,14},... | collective-permute-start | bytes 675848 | tf_op jit(solution)/shard_map/ppermute | solution.py:399
  87.6 22.3 %collective-permute-start.6 = (bf16[880,128]{1,0:T(8,128)(2,1)S(1)}, bf16[880,128]{1,0:T(8,128)(2,1)S(1)}, u32[]{:S(2)}, u32[]{:S(2)}) collective-permute-start(bf16[880,128]{1,0:T(8,128)(2,1)S(1)} %add_convert_fusion.1), channel_id=1, source_target_pairs={{0,4},{4,0},{8,12},{12,8},{1,5},{5,1},{9,13},{13,9},{2,6},{6,2},{1... | collective-permute-start | bytes 675848 | tf_op jit(solution)/shard_map/ppermute | solution.py:399
  87.6 31.1 %copy-start.2 = (s32[4,128]{1,0:T(4,128)S(1)}, s32[4,128]{1,0:T(4,128)}, u32[]{:S(2)}) copy-start(s32[4,128]{1,0:T(4,128)} %send_hbm.1) | copy-start | bytes 6148
  110.0 8.2 %collective-permute-start.9 = (bf16[880,128]{1,0:T(8,128)(2,1)S(1)}, bf16[880,128]{1,0:T(8,128)(2,1)S(1)}, u32[]{:S(2)}, u32[]{:S(2)}) collective-permute-start(bf16[880,128]{1,0:T(8,128)(2,1)S(1)} %add_convert_fusion.refs_0_), channel_id=1, source_target_pairs={{0,2},{1,3},{2,0},{3,1},{4,6},{5,7},{6,4},{7,5},{8,10},{9,11},{10,... | collective-permute-start | bytes 675848 | tf_op jit(solution)/shard_map/ppermute | solution.py:399
  111.5 3.9 %collective-permute-start.10 = (bf16[128,128]{1,0:T(8,128)(2,1)S(1)}, bf16[128,128]{1,0:T(8,128)(2,1)S(1)}, u32[]{:S(2)}, u32[]{:S(2)}) collective-permute-start(bf16[128,128]{1,0:T(8,128)(2,1)S(1)} %get-tuple-element.67), channel_id=1, source_target_pairs={{0,4},{4,0},{8,12},{12,8},{1,5},{5,1},{9,13},{13,9},{2,6},{6,2},{1... | collective-permute-start | bytes 98312 | tf_op jit(solution)/shard_map/ppermute | solution.py:411
  113.5 1.9 %collective-permute-start.11 = (bf16[128,128]{1,0:T(8,128)(2,1)S(1)}, bf16[128,128]{1,0:T(8,128)(2,1)S(1)}, u32[]{:S(2)}, u32[]{:S(2)}) collective-permute-start(bf16[128,128]{1,0:T(8,128)(2,1)S(1)} %get-tuple-element.68), channel_id=1, source_target_pairs={{4,8},{8,4},{5,9},{9,5},{6,10},{10,6},{7,11},{11,7},{20,24},{24,20... | collective-permute-start | bytes 98312 | tf_op jit(solution)/shard_map/ppermute | solution.py:413
  114.2 4.0 %collective-permute-start.12 = (bf16[128,128]{1,0:T(8,128)(2,1)S(1)}, bf16[128,128]{1,0:T(8,128)(2,1)S(1)}, u32[]{:S(2)}, u32[]{:S(2)}) collective-permute-start(bf16[128,128]{1,0:T(8,128)(2,1)S(1)} %get-tuple-element.69), channel_id=1, source_target_pairs={{0,2},{2,0},{1,3},{3,1},{4,6},{6,4},{5,7},{7,5},{8,10},{10,8},{9,1... | collective-permute-start | bytes 98312 | tf_op jit(solution)/shard_map/ppermute | solution.py:411
  118.2 3.3 %collective-permute-start.13 = (bf16[880,128]{1,0:T(8,128)(2,1)S(1)}, bf16[880,128]{1,0:T(8,128)(2,1)S(1)}, u32[]{:S(2)}, u32[]{:S(2)}) collective-permute-start(bf16[880,128]{1,0:T(8,128)(2,1)S(1)} %add_convert_fusion.refs_0_), channel_id=1, source_target_pairs={{0,1},{1,0},{2,3},{3,2},{4,5},{5,4},{6,7},{7,6},{8,9},{9,8},{10,11... | collective-permute-start | bytes 675848 | tf_op jit(solution)/shard_map/ppermute | solution.py:399
  118.2 3.3 %collective-permute-start.14 = (bf16[880,128]{1,0:T(8,128)(2,1)S(1)}, bf16[880,128]{1,0:T(8,128)(2,1)S(1)}, u32[]{:S(2)}, u32[]{:S(2)}) collective-permute-start(bf16[880,128]{1,0:T(8,128)(2,1)S(1)} %collective-permute-done.9.refs_2_), channel_id=1, source_target_pairs={{0,1},{1,0},{2,3},{3,2},{4,5},{5,4},{6,7},{7,6},{8,9},{9,8},{10,11... | collective-permute-start | bytes 675848 | tf_op jit(solution)/shard_map/ppermute | solution.py:399

commit v6 on v5

--- a/solution.py
+++ b/solution.py
@@ -185,10 +185,7 @@
             pltpu.SemaphoreType.DMA((2, looped * STREAMS)),
         ]
         + [pltpu.SMEM((stream,), jnp.int32)] * (looped * STREAMS),
-        compiler_params=pltpu.CompilerParams(vmem_limit_bytes=20 << 20),
-        cost_estimate=pl.CostEstimate(
-            flops=4 * voxels * offsets * chans * chans, bytes_accessed=150 << 20, transcendentals=0
-        ),
+        compiler_params=pltpu.CompilerParams(vmem_limit_bytes=17 << 20),
         name="forward",
     )(map_flat, sparse, features, from_x, from_y, weights, class_t, label_blocks)
 
@@ -255,7 +252,7 @@
         ]
         + [pltpu.VMEM((table_rows, chans), jnp.float32)] * offsets
         + [pltpu.SMEM((stream,), jnp.int32)] * (offsets * SCATTER_STREAMS),
-        compiler_params=pltpu.CompilerParams(vmem_limit_bytes=28 << 20),
+        compiler_params=pltpu.CompilerParams(vmem_limit_bytes=21 << 20),
         cost_estimate=pl.CostEstimate(
             flops=2 * voxels * offsets * chans * chans, bytes_accessed=40 << 20, transcendentals=0
         ),
@@ -471,7 +468,7 @@
         piece = lax.dynamic_slice_in_dim(part, (mine ^ d) * height, height, axis=0)
         sent.append(piece.astype(jnp.bfloat16))
     own = lax.dynamic_slice_in_dim(part, mine * height, height, axis=0)
-    sent, dext = scatter_beside(sent, None)
+    (sent, own), dext = scatter_beside((sent, own), None)
     got = [exchange(piece, square, d + 1) for d, piece in enumerate(sent)]
     got, dext = lax.optimization_barrier((got, dext))
     own = own + sum(piece.astype(jnp.float32) for piece in got)

time: 123 us -> 118 us (0.959)
  local copies, waits for them, and re-layouts: 5.8 us -> 1.6 us
  other arithmetic: 2.48 us -> 1.23 us
    unnamed x10 -> x8, local copies, waits for them, and re-layouts: 4.17 us -> 0.71 us
    convert_element_type x1, other arithmetic: 1.36 us -> 0.12 us  [on_device(): own = own.astype(jnp.bfloat16)]
  transfers between devices with their start and end apart: 15 -> 15, of which waited for: 3 -> 3; matrix products, arithmetic and copies ran while one was open for 1% -> 1% of each run, Pallas kernels for 37% -> 38%
where the time goes in v6:
time: 118 us
  Pallas kernels  91.3 us (77%)
  starting transfers between devices  18.5 us (16%)
  waiting for transfers between devices  4.27 us (4%)
  local copies, waits for them, and re-layouts  1.6 us (1%)
  other arithmetic  1.23 us (1%)
    pallas_call x2, Pallas kernels, scatter(): pl.pallas_call(functools.partial(scatter_kernel, first, offsets, has_befo...  42.4 us
    pallas_call x1, Pallas kernels, forward(): pl.pallas_call(functools.partial(forward_kernel, classes), out_shape=(jax...  41.8 us
    ppermute x9, starting transfers between devices, exchange(): lax.ppermute(shard, axes, [(i, i ^ distance) for i in range(group_size(ax...  9.94 us
    ppermute x4, starting transfers between devices, swap_edges(): got = [lax.ppermute(over_even, axis, even_pairs)]  7.23 us
    ppermute x4, waiting for transfers between devices, swap_edges(): got = [lax.ppermute(over_even, axis, even_pairs)]  4.24 us
    pallas_call x1, Pallas kernels, outgoing(): pl.pallas_call(functools.partial(outgoing_kernel, ('ty', 'tx')), out_shap...  2.88 us
    pallas_call x1, Pallas kernels, finish(): pl.pallas_call(finish_kernel, out_shape=jax.ShapeDtypeStruct(dmixed.shape...  2.74 us
  transfers between devices with their start and end apart: 15, of which 3 were waited for; matrix products, arithmetic and copies ran while one was open for 1% of the time, Pallas kernels for 38%

profile of v6, /device:TPU:0, one launch (start us, length us, event | category | flops | bytes accessed | tf_op | source)
XLA Modules:
  0.0 117.7 jit_solution(9251546037300441689)
XLA Ops:
  0.6 2.9 %outgoing.1 = (bf16[128,128]{1,0:T(8,128)(2,1)}, bf16[128,128]{1,0:T(8,128)(2,1)}, bf16[128,128]{1,0:T(8,128)(2,1)}, bf16[128,128]{1,0:T(8,128)(2,1)}) custom-call(s32[4,128]{1,0:T(4,128)} %send_hbm.1, bf16[2048,128]{1,0:T(8,128)(2,1)} %own_hbm.3), custom_call_target="tpu_custom_call" | custom-call | bytes 8388608 | tf_op jit(solution)/shard_map/outgoing/pallas_call | solution.py:330
  3.5 3.1 %collective-permute-start = (bf16[128,128]{1,0:T(8,128)(2,1)}, bf16[128,128]{1,0:T(8,128)(2,1)S(1)}, u32[]{:S(2)}, u32[]{:S(2)}) collective-permute-start(bf16[128,128]{1,0:T(8,128)(2,1)} %get-tuple-element.41), channel_id=1, source_target_pairs={{0,4},{4,0},{8,12},{12,8},{1,5},{5,1},{9,13},{13,9},{2,6},{6,2},{1... | collective-permute-start | bytes 98312 | tf_op jit(solution)/shard_map/ppermute | solution.py:408
  6.6 0.7 collective-permute-start.1
  7.3 1.6 %collective-permute-start.2 = (bf16[128,128]{1,0:T(8,128)(2,1)}, bf16[128,128]{1,0:T(8,128)(2,1)S(1)}, u32[]{:S(2)}, u32[]{:S(2)}) collective-permute-start(bf16[128,128]{1,0:T(8,128)(2,1)} %get-tuple-element.43), channel_id=1, source_target_pairs={{0,2},{2,0},{1,3},{3,1},{4,6},{6,4},{5,7},{7,5},{8,10},{10,8},{9,1... | collective-permute-start | bytes 98312 | tf_op jit(solution)/shard_map/ppermute | solution.py:408
  8.8 1.0 fusion
  9.9 0.7 pad.4.class_ref
  10.7 0.8 collective-permute-done.2.y_refs_0_
  11.5 0.7 copy-done.2
  12.2 41.8 %forward.1 = (f32[2048,128]{1,0:T(8,128)S(1)}, f32[2048,128]{1,0:T(8,128)S(1)}, f32[3520,128]{1,0:T(8,128)S(1)}, bf16[3456,128]{1,0:T(8,128)(2,1)S(1)}) custom-call(s32[55296]{0:T(1024)S(1)} %reshape.30.map_hbm, s32[8,8,256]{2,1,0:T(8,128)S(1)} %bitcast.16, bf16[2048,128]{1,0:T(8,128)(2,1)S(1)} %copy-done, ...), custom_call_target="tpu_custom_call" | custom-call | tf_op jit(solution)/shard_map/forward/pallas_call | solution.py:164
  54.0 0.1 dynamic-slice_convert_fusion
  54.1 0.1 collective-permute-start.3
  54.2 1.6 %collective-permute-start.4 = (bf16[880,128]{1,0:T(8,128)(2,1)S(1)}, bf16[880,128]{1,0:T(8,128)(2,1)S(1)}, u32[]{:S(2)}, u32[]{:S(2)}) collective-permute-start(bf16[880,128]{1,0:T(8,128)(2,1)S(1)} %get-tuple-element.49), channel_id=1, source_target_pairs={{0,2},{1,3},{2,0},{3,1},{4,6},{5,7},{6,4},{7,5},{8,10},{9,11},{10,... | collective-permute-start | bytes 675848 | tf_op jit(solution)/shard_map/ppermute | solution.py:396
  55.8 0.3 collective-permute-start.5
  56.1 20.2 %scatter_0.1.refs_0_ = f32[2592,128]{1,0:T(8,128)S(1)} custom-call(s32[55296]{0:T(1024)S(1)} %reshape.30.map_hbm, f32[2,1024,128]{2,1,0:T(8,128)S(1)} %bitcast.13, bf16[3456,128]{1,0:T(8,128)(2,1)S(1)} %get-tuple-element.52.weight_ref), custom_call_target="tpu_custom_call" | custom-call | flops 872415232 | bytes 41943040 | tf_op jit(solution)/shard_map/scatter_0/pallas_call | solution.py:244
  76.3 0.0 collective-permute-done.3
  76.3 0.0 collective-permute-done.5
  76.3 0.1 add_convert_fusion.1
  76.4 2.5 %collective-permute-start.8 = (bf16[880,128]{1,0:T(8,128)(2,1)S(1)}, bf16[880,128]{1,0:T(8,128)(2,1)S(1)}, u32[]{:S(2)}, u32[]{:S(2)}) collective-permute-start(bf16[880,128]{1,0:T(8,128)(2,1)S(1)} %add_convert_fusion.1), channel_id=1, source_target_pairs={{0,12},{4,8},{8,4},{12,0},{1,13},{5,9},{9,5},{13,1},{2,14},{6,10},... | collective-permute-start | bytes 675848 | tf_op jit(solution)/shard_map/ppermute | solution.py:396
  79.0 3.4 %collective-permute-start.7 = (bf16[880,128]{1,0:T(8,128)(2,1)S(1)}, bf16[880,128]{1,0:T(8,128)(2,1)S(1)}, u32[]{:S(2)}, u32[]{:S(2)}) collective-permute-start(bf16[880,128]{1,0:T(8,128)(2,1)S(1)} %add_convert_fusion.1), channel_id=1, source_target_pairs={{0,8},{4,12},{8,0},{12,4},{1,9},{5,13},{9,1},{13,5},{2,10},{6,14},... | collective-permute-start | bytes 675848 | tf_op jit(solution)/shard_map/ppermute | solution.py:396
  82.3 22.2 %scatter_13.1 = (f32[2592,128]{1,0:T(8,128)S(1)}, bf16[128,128]{1,0:T(8,128)(2,1)S(1)}, bf16[128,128]{1,0:T(8,128)(2,1)}, bf16[128,128]{1,0:T(8,128)(2,1)S(1)}, bf16[128,128]{1,0:T(8,128)(2,1)S(1)}) custom-call(s32[55296]{0:T(1024)S(1)} %reshape.30.map_hbm, f32[2,1024,128]{2,1,0:T(8,128)S(1)} %bitcast.14, ...), custom_call_target="tpu_custom_call" | custom-call | flops 939524096 | bytes 41943040 | tf_op jit(solution)/shard_map/scatter_13/pallas_call | solution.py:244
  104.6 0.0 collective-permute-done.7
  104.6 0.0 collective-permute-done.6
  104.6 0.1 add_convert_fusion.refs_0_
  104.8 1.6 %collective-permute-start.9 = (bf16[880,128]{1,0:T(8,128)(2,1)S(1)}, bf16[880,128]{1,0:T(8,128)(2,1)S(1)}, u32[]{:S(2)}, u32[]{:S(2)}) collective-permute-start(bf16[880,128]{1,0:T(8,128)(2,1)S(1)} %add_convert_fusion.refs_0_), channel_id=1, source_target_pairs={{0,2},{1,3},{2,0},{3,1},{4,6},{5,7},{6,4},{7,5},{8,10},{9,11},{10,... | collective-permute-start | bytes 675848 | tf_op jit(solution)/shard_map/ppermute | solution.py:396
  106.4 2.0 %collective-permute-start.10 = (bf16[128,128]{1,0:T(8,128)(2,1)S(1)}, bf16[128,128]{1,0:T(8,128)(2,1)S(1)}, u32[]{:S(2)}, u32[]{:S(2)}) collective-permute-start(bf16[128,128]{1,0:T(8,128)(2,1)S(1)} %get-tuple-element.69), channel_id=1, source_target_pairs={{0,4},{4,0},{8,12},{12,8},{1,5},{5,1},{9,13},{13,9},{2,6},{6,2},{1... | collective-permute-start | bytes 98312 | tf_op jit(solution)/shard_map/ppermute | solution.py:408
  108.4 0.7 collective-permute-start.11
  109.0 0.6 collective-permute-start.12
  109.6 0.7 collective-permute-done.10.x_refs_0_
  110.3 2.7 %collective-permute-done.12.y_refs_0_ = bf16[128,128]{1,0:T(8,128)(2,1)S(1)} collective-permute-done((bf16[128,128]{1,0:T(8,128)(2,1)S(1)}, bf16[128,128]{1,0:T(8,128)(2,1)S(1)}, u32[]{:S(2)}, u32[]{:S(2)}) %collective-permute-start.12) | collective-permute-done | bytes 32800 | tf_op jit(solution)/shard_map/ppermute | solution.py:408
  113.0 0.5 collective-permute-start.14
  113.5 2.7 %finish.1 = f32[2048,128]{1,0:T(8,128)} custom-call(f32[2048,128]{1,0:T(8,128)S(1)} %get-tuple-element.44.dmixed_ref, f32[2592,128]{1,0:T(8,128)S(1)} %get-tuple-element.64.dext_ref, s32[1,512]{1,0:T(1,128)S(1)} %bitcast.18, bf16[128,128]{1,0:T(8,128)(2,1)S(1)} %collective-permute-done.10.x_refs_0_, bf16[128,128]{1,0:T(8,128)(2,1)S(1)} %collective-permute-done.11.x_refs_1_, ...), custom_call_target="tpu_custom_call" | custom-call | flops 268435456 | bytes 4194304 | tf_op jit(solution)/shard_map/finish/pallas_call | solution.py:286
  116.3 1.4 %assemble.1 = (f32[3456,128]{1,0:T(8,128)}, f32[19,128]{1,0:T(8,128)}) custom-call(bf16[880,128]{1,0:T(8,128)(2,1)S(1)} %add_convert_fusion.refs_0_, bf16[880,128]{1,0:T(8,128)(2,1)S(1)} %collective-permute-done.13.refs_1_, bf16[880,128]{1,0:T(8,128)(2,1)S(1)} %collective-permute-done.9.refs_2_, bf16[880,128]{1,0:T(8,128)(2,1)S(1)} %collective-permute-done.14.refs_3_), custom_call_target="tpu_custom_call" | custom-call | tf_op jit(solution)/shard_map/assemble/pallas_call | solution.py:371
  (20 shorter events, 0.1 us)
Async XLA Ops:
  0.6 10.9 %copy-start = (bf16[2048,128]{1,0:T(8,128)(2,1)S(1)}, bf16[2048,128]{1,0:T(8,128)(2,1)}, u32[]{:S(2)}) copy-start(bf16[2048,128]{1,0:T(8,128)(2,1)} %own_hbm.3) | copy-start | bytes 1572868
  0.6 10.8 %copy-start.1 = (bf16[27,128,128]{2,1,0:T(8,128)(2,1)S(1)}, bf16[27,128,128]{2,1,0:T(8,128)(2,1)}, u32[]{:S(2)}) copy-start(bf16[27,128,128]{2,1,0:T(8,128)(2,1)} %param.7) | copy-start | bytes 2654212
  3.5 7.1 %collective-permute-start = (bf16[128,128]{1,0:T(8,128)(2,1)}, bf16[128,128]{1,0:T(8,128)(2,1)S(1)}, u32[]{:S(2)}, u32[]{:S(2)}) collective-permute-start(bf16[128,128]{1,0:T(8,128)(2,1)} %get-tuple-element.41), channel_id=1, source_target_pairs={{0,4},{4,0},{8,12},{12,8},{1,5},{5,1},{9,13},{13,9},{2,6},{6,2},{1... | collective-permute-start | bytes 98312 | tf_op jit(solution)/shard_map/ppermute | solution.py:408
  6.6 4.0 %collective-permute-start.1 = (bf16[128,128]{1,0:T(8,128)(2,1)}, bf16[128,128]{1,0:T(8,128)(2,1)S(1)}, u32[]{:S(2)}, u32[]{:S(2)}) collective-permute-start(bf16[128,128]{1,0:T(8,128)(2,1)} %get-tuple-element.42), channel_id=1, source_target_pairs={{4,8},{8,4},{5,9},{9,5},{6,10},{10,6},{7,11},{11,7},{20,24},{24,20... | collective-permute-start | bytes 98312 | tf_op jit(solution)/shard_map/ppermute | solution.py:410
  7.3 4.2 %collective-permute-start.2 = (bf16[128,128]{1,0:T(8,128)(2,1)}, bf16[128,128]{1,0:T(8,128)(2,1)S(1)}, u32[]{:S(2)}, u32[]{:S(2)}) collective-permute-start(bf16[128,128]{1,0:T(8,128)(2,1)} %get-tuple-element.43), channel_id=1, source_target_pairs={{0,2},{2,0},{1,3},{3,1},{4,6},{6,4},{5,7},{7,5},{8,10},{10,8},{9,1... | collective-permute-start | bytes 98312 | tf_op jit(solution)/shard_map/ppermute | solution.py:408
  11.5 0.7 copy-start.2
  54.1 22.2 %collective-permute-start.3 = (bf16[880,128]{1,0:T(8,128)(2,1)S(1)}, bf16[880,128]{1,0:T(8,128)(2,1)S(1)}, u32[]{:S(2)}, u32[]{:S(2)}) collective-permute-start(bf16[880,128]{1,0:T(8,128)(2,1)S(1)} %get-tuple-element.48), channel_id=1, source_target_pairs={{0,1},{1,0},{2,3},{3,2},{4,5},{5,4},{6,7},{7,6},{8,9},{9,8},{10,11... | collective-permute-start | bytes 675848 | tf_op jit(solution)/shard_map/ppermute | solution.py:396
  54.2 22.1 %collective-permute-start.4 = (bf16[880,128]{1,0:T(8,128)(2,1)S(1)}, bf16[880,128]{1,0:T(8,128)(2,1)S(1)}, u32[]{:S(2)}, u32[]{:S(2)}) collective-permute-start(bf16[880,128]{1,0:T(8,128)(2,1)S(1)} %get-tuple-element.49), channel_id=1, source_target_pairs={{0,2},{1,3},{2,0},{3,1},{4,6},{5,7},{6,4},{7,5},{8,10},{9,11},{10,... | collective-permute-start | bytes 675848 | tf_op jit(solution)/shard_map/ppermute | solution.py:396
  55.8 20.5 %collective-permute-start.5 = (bf16[880,128]{1,0:T(8,128)(2,1)S(1)}, bf16[880,128]{1,0:T(8,128)(2,1)S(1)}, u32[]{:S(2)}, u32[]{:S(2)}) collective-permute-start(bf16[880,128]{1,0:T(8,128)(2,1)S(1)} %get-tuple-element.50), channel_id=1, source_target_pairs={{0,3},{1,2},{2,1},{3,0},{4,7},{5,6},{6,5},{7,4},{8,11},{9,10},{10,... | collective-permute-start | bytes 675848 | tf_op jit(solution)/shard_map/ppermute | solution.py:396
  76.4 28.2 %collective-permute-start.8 = (bf16[880,128]{1,0:T(8,128)(2,1)S(1)}, bf16[880,128]{1,0:T(8,128)(2,1)S(1)}, u32[]{:S(2)}, u32[]{:S(2)}) collective-permute-start(bf16[880,128]{1,0:T(8,128)(2,1)S(1)} %add_convert_fusion.1), channel_id=1, source_target_pairs={{0,12},{4,8},{8,4},{12,0},{1,13},{5,9},{9,5},{13,1},{2,14},{6,10},... | collective-permute-start | bytes 675848 | tf_op jit(solution)/shard_map/ppermute | solution.py:396
  79.0 25.6 %collective-permute-start.7 = (bf16[880,128]{1,0:T(8,128)(2,1)S(1)}, bf16[880,128]{1,0:T(8,128)(2,1)S(1)}, u32[]{:S(2)}, u32[]{:S(2)}) collective-permute-start(bf16[880,128]{1,0:T(8,128)(2,1)S(1)} %add_convert_fusion.1), channel_id=1, source_target_pairs={{0,8},{4,12},{8,0},{12,4},{1,9},{5,13},{9,1},{13,5},{2,10},{6,14},... | collective-permute-start | bytes 675848 | tf_op jit(solution)/shard_map/ppermute | solution.py:396
  82.3 22.3 %collective-permute-start.6 = (bf16[880,128]{1,0:T(8,128)(2,1)S(1)}, bf16[880,128]{1,0:T(8,128)(2,1)S(1)}, u32[]{:S(2)}, u32[]{:S(2)}) collective-permute-start(bf16[880,128]{1,0:T(8,128)(2,1)S(1)} %add_convert_fusion.1), channel_id=1, source_target_pairs={{0,4},{4,0},{8,12},{12,8},{1,5},{5,1},{9,13},{13,9},{2,6},{6,2},{1... | collective-permute-start | bytes 675848 | tf_op jit(solution)/shard_map/ppermute | solution.py:396
  82.3 31.2 %copy-start.3 = (s32[4,128]{1,0:T(4,128)S(1)}, s32[4,128]{1,0:T(4,128)}, u32[]{:S(2)}) copy-start(s32[4,128]{1,0:T(4,128)} %send_hbm.1) | copy-start | bytes 6148
  104.8 8.3 %collective-permute-start.9 = (bf16[880,128]{1,0:T(8,128)(2,1)S(1)}, bf16[880,128]{1,0:T(8,128)(2,1)S(1)}, u32[]{:S(2)}, u32[]{:S(2)}) collective-permute-start(bf16[880,128]{1,0:T(8,128)(2,1)S(1)} %add_convert_fusion.refs_0_), channel_id=1, source_target_pairs={{0,2},{1,3},{2,0},{3,1},{4,6},{5,7},{6,4},{7,5},{8,10},{9,11},{10,... | collective-permute-start | bytes 675848 | tf_op jit(solution)/shard_map/ppermute | solution.py:396
  106.4 3.9 %collective-permute-start.10 = (bf16[128,128]{1,0:T(8,128)(2,1)S(1)}, bf16[128,128]{1,0:T(8,128)(2,1)S(1)}, u32[]{:S(2)}, u32[]{:S(2)}) collective-permute-start(bf16[128,128]{1,0:T(8,128)(2,1)S(1)} %get-tuple-element.69), channel_id=1, source_target_pairs={{0,4},{4,0},{8,12},{12,8},{1,5},{5,1},{9,13},{13,9},{2,6},{6,2},{1... | collective-permute-start | bytes 98312 | tf_op jit(solution)/shard_map/ppermute | solution.py:408
  108.4 1.9 %collective-permute-start.11 = (bf16[128,128]{1,0:T(8,128)(2,1)S(1)}, bf16[128,128]{1,0:T(8,128)(2,1)S(1)}, u32[]{:S(2)}, u32[]{:S(2)}) collective-permute-start(bf16[128,128]{1,0:T(8,128)(2,1)S(1)} %get-tuple-element.70), channel_id=1, source_target_pairs={{4,8},{8,4},{5,9},{9,5},{6,10},{10,6},{7,11},{11,7},{20,24},{24,20... | collective-permute-start | bytes 98312 | tf_op jit(solution)/shard_map/ppermute | solution.py:410
  109.0 4.0 %collective-permute-start.12 = (bf16[128,128]{1,0:T(8,128)(2,1)S(1)}, bf16[128,128]{1,0:T(8,128)(2,1)S(1)}, u32[]{:S(2)}, u32[]{:S(2)}) collective-permute-start(bf16[128,128]{1,0:T(8,128)(2,1)S(1)} %get-tuple-element.71), channel_id=1, source_target_pairs={{0,2},{2,0},{1,3},{3,1},{4,6},{6,4},{5,7},{7,5},{8,10},{10,8},{9,1... | collective-permute-start | bytes 98312 | tf_op jit(solution)/shard_map/ppermute | solution.py:408
  113.0 3.3 %collective-permute-start.13 = (bf16[880,128]{1,0:T(8,128)(2,1)S(1)}, bf16[880,128]{1,0:T(8,128)(2,1)S(1)}, u32[]{:S(2)}, u32[]{:S(2)}) collective-permute-start(bf16[880,128]{1,0:T(8,128)(2,1)S(1)} %add_convert_fusion.refs_0_), channel_id=1, source_target_pairs={{0,1},{1,0},{2,3},{3,2},{4,5},{5,4},{6,7},{7,6},{8,9},{9,8},{10,11... | collective-permute-start | bytes 675848 | tf_op jit(solution)/shard_map/ppermute | solution.py:396
  113.0 3.3 %collective-permute-start.14 = (bf16[880,128]{1,0:T(8,128)(2,1)S(1)}, bf16[880,128]{1,0:T(8,128)(2,1)S(1)}, u32[]{:S(2)}, u32[]{:S(2)}) collective-permute-start(bf16[880,128]{1,0:T(8,128)(2,1)S(1)} %collective-permute-done.9.refs_2_), channel_id=1, source_target_pairs={{0,1},{1,0},{2,3},{3,2},{4,5},{5,4},{6,7},{7,6},{8,9},{9,8},{10,11... | collective-permute-start | bytes 675848 | tf_op jit(solution)/shard_map/ppermute | solution.py:396

commit v7 on v6

--- a/solution.py
+++ b/solution.py
@@ -270,7 +270,7 @@
     low_y, high_y = from_neighbours(y_refs, "ty")
     for n, value in enumerate((high_x, low_x, high_y, low_y)):
         back_ref[n * width : (n + 1) * width, :] = value.astype(jnp.bfloat16)
-    height = voxels // 8
+    height = voxels // 2
 
     def step(t, carry):
         at = pl.ds(pl.multiple_of(t * height, height), height)
@@ -439,7 +439,7 @@
     weights = conv_weight.reshape(offsets * chans, chans)
     class_t = jnp.pad(classifier.T, ((0, HEAD_ROWS - classes), (0, 0)))
     label_blocks = (
-        labels.reshape(STREAMS, voxels // block, SEGMENT).transpose(1, 0, 2)
+        jnp.minimum(labels, classes).reshape(STREAMS, voxels // block, SEGMENT).transpose(1, 0, 2)
         .reshape(voxels // block, 1, block)
     )
     dpre, dmixed, part, flipped = forward(

time: 118 us -> 116 us (0.983)
  transfers between devices with their start and end apart: 15 -> 15, of which waited for: 3 -> 3; matrix products, arithmetic and copies ran while one was open for 1% -> 2% of each run, Pallas kernels for 38% -> 38%
where the time goes in v7:
time: 116 us
  Pallas kernels  90.4 us (78%)
  starting transfers between devices  18.5 us (16%)
  waiting for transfers between devices  3.54 us (3%)
  other arithmetic  1.94 us (2%)
    pallas_call x2, Pallas kernels, scatter(): pl.pallas_call(functools.partial(scatter_kernel, first, offsets, has_befo...  42.4 us
    pallas_call x1, Pallas kernels, forward(): pl.pallas_call(functools.partial(forward_kernel, classes), out_shape=(jax...  41.8 us
    ppermute x9, starting transfers between devices, exchange(): lax.ppermute(shard, axes, [(i, i ^ distance) for i in range(group_size(ax...  9.92 us
    ppermute x4, starting transfers between devices, swap_edges(): got = [lax.ppermute(over_even, axis, even_pairs)]  7.29 us
    ppermute x4, waiting for transfers between devices, swap_edges(): got = [lax.ppermute(over_even, axis, even_pairs)]  3.51 us
    pallas_call x1, Pallas kernels, outgoing(): pl.pallas_call(functools.partial(outgoing_kernel, ('ty', 'tx')), out_shap...  2.9 us
  transfers between devices with their start and end apart: 15, of which 3 were waited for; matrix products, arithmetic and copies ran while one was open for 2% of the time, Pallas kernels for 38%

profile of v7, /device:TPU:0, one launch (start us, length us, event | category | flops | bytes accessed | tf_op | source)
XLA Modules:
  0.0 116.1 jit_solution(4784153833183541874)
XLA Ops:
  0.6 2.9 %outgoing.1 = (bf16[128,128]{1,0:T(8,128)(2,1)}, bf16[128,128]{1,0:T(8,128)(2,1)}, bf16[128,128]{1,0:T(8,128)(2,1)}, bf16[128,128]{1,0:T(8,128)(2,1)}) custom-call(s32[4,128]{1,0:T(4,128)} %send_hbm.1, bf16[2048,128]{1,0:T(8,128)(2,1)} %own_hbm.3), custom_call_target="tpu_custom_call" | custom-call | bytes 8388608 | tf_op jit(solution)/shard_map/outgoing/pallas_call | solution.py:330
  3.6 3.1 %collective-permute-start = (bf16[128,128]{1,0:T(8,128)(2,1)}, bf16[128,128]{1,0:T(8,128)(2,1)S(1)}, u32[]{:S(2)}, u32[]{:S(2)}) collective-permute-start(bf16[128,128]{1,0:T(8,128)(2,1)} %get-tuple-element.41), channel_id=1, source_target_pairs={{0,4},{4,0},{8,12},{12,8},{1,5},{5,1},{9,13},{13,9},{2,6},{6,2},{1... | collective-permute-start | bytes 98312 | tf_op jit(solution)/shard_map/ppermute | solution.py:408
  6.7 0.7 collective-permute-start.1
  7.3 1.6 %collective-permute-start.2 = (bf16[128,128]{1,0:T(8,128)(2,1)}, bf16[128,128]{1,0:T(8,128)(2,1)S(1)}, u32[]{:S(2)}, u32[]{:S(2)}) collective-permute-start(bf16[128,128]{1,0:T(8,128)(2,1)} %get-tuple-element.43), channel_id=1, source_target_pairs={{0,2},{2,0},{1,3},{3,1},{4,6},{6,4},{5,7},{7,5},{8,10},{10,8},{9,1... | collective-permute-start | bytes 98312 | tf_op jit(solution)/shard_map/ppermute | solution.py:408
  8.9 1.0 fusion
  9.9 0.7 broadcast_minimum_fusion
  10.6 0.7 pad.4.class_ref
  11.3 0.0 collective-permute-done.x_refs_0_
  11.3 0.0 collective-permute-done.1.x_refs_1_
  11.3 0.2 collective-permute-done.2.y_refs_0_
  11.5 41.8 %forward.1 = (f32[2048,128]{1,0:T(8,128)S(1)}, f32[2048,128]{1,0:T(8,128)S(1)}, f32[3520,128]{1,0:T(8,128)S(1)}, bf16[3456,128]{1,0:T(8,128)(2,1)S(1)}) custom-call(s32[55296]{0:T(1024)S(1)} %reshape.30.map_hbm, s32[8,8,256]{2,1,0:T(8,128)S(1)} %bitcast.16, bf16[2048,128]{1,0:T(8,128)(2,1)S(1)} %copy-done, ...), custom_call_target="tpu_custom_call" | custom-call | tf_op jit(solution)/shard_map/forward/pallas_call | solution.py:164
  53.3 0.1 dynamic-slice_convert_fusion
  53.4 0.1 collective-permute-start.3
  53.5 1.6 %collective-permute-start.4 = (bf16[880,128]{1,0:T(8,128)(2,1)S(1)}, bf16[880,128]{1,0:T(8,128)(2,1)S(1)}, u32[]{:S(2)}, u32[]{:S(2)}) collective-permute-start(bf16[880,128]{1,0:T(8,128)(2,1)S(1)} %get-tuple-element.49), channel_id=1, source_target_pairs={{0,2},{1,3},{2,0},{3,1},{4,6},{5,7},{6,4},{7,5},{8,10},{9,11},{10,... | collective-permute-start | bytes 675848 | tf_op jit(solution)/shard_map/ppermute | solution.py:396
  55.1 0.3 collective-permute-start.5
  55.4 20.2 %scatter_0.1.refs_0_ = f32[2592,128]{1,0:T(8,128)S(1)} custom-call(s32[55296]{0:T(1024)S(1)} %reshape.30.map_hbm, f32[2,1024,128]{2,1,0:T(8,128)S(1)} %bitcast.13, bf16[3456,128]{1,0:T(8,128)(2,1)S(1)} %get-tuple-element.52.weight_ref), custom_call_target="tpu_custom_call" | custom-call | flops 872415232 | bytes 41943040 | tf_op jit(solution)/shard_map/scatter_0/pallas_call | solution.py:244
  75.6 0.0 collective-permute-done.3
  75.6 0.0 collective-permute-done.5
  75.6 0.1 add_convert_fusion.1
  75.8 2.5 %collective-permute-start.8 = (bf16[880,128]{1,0:T(8,128)(2,1)S(1)}, bf16[880,128]{1,0:T(8,128)(2,1)S(1)}, u32[]{:S(2)}, u32[]{:S(2)}) collective-permute-start(bf16[880,128]{1,0:T(8,128)(2,1)S(1)} %add_convert_fusion.1), channel_id=1, source_target_pairs={{0,12},{4,8},{8,4},{12,0},{1,13},{5,9},{9,5},{13,1},{2,14},{6,10},... | collective-permute-start | bytes 675848 | tf_op jit(solution)/shard_map/ppermute | solution.py:396
  78.3 3.4 %collective-permute-start.7 = (bf16[880,128]{1,0:T(8,128)(2,1)S(1)}, bf16[880,128]{1,0:T(8,128)(2,1)S(1)}, u32[]{:S(2)}, u32[]{:S(2)}) collective-permute-start(bf16[880,128]{1,0:T(8,128)(2,1)S(1)} %add_convert_fusion.1), channel_id=1, source_target_pairs={{0,8},{4,12},{8,0},{12,4},{1,9},{5,13},{9,1},{13,5},{2,10},{6,14},... | collective-permute-start | bytes 675848 | tf_op jit(solution)/shard_map/ppermute | solution.py:396
  81.7 22.2 %scatter_13.1 = (f32[2592,128]{1,0:T(8,128)S(1)}, bf16[128,128]{1,0:T(8,128)(2,1)S(1)}, bf16[128,128]{1,0:T(8,128)(2,1)}, bf16[128,128]{1,0:T(8,128)(2,1)S(1)}, bf16[128,128]{1,0:T(8,128)(2,1)S(1)}) custom-call(s32[55296]{0:T(1024)S(1)} %reshape.30.map_hbm, f32[2,1024,128]{2,1,0:T(8,128)S(1)} %bitcast.14, ...), custom_call_target="tpu_custom_call" | custom-call | flops 939524096 | bytes 41943040 | tf_op jit(solution)/shard_map/scatter_13/pallas_call | solution.py:244
  104.0 0.1 add_convert_fusion.refs_0_
  104.1 1.5 %collective-permute-start.9 = (bf16[880,128]{1,0:T(8,128)(2,1)S(1)}, bf16[880,128]{1,0:T(8,128)(2,1)S(1)}, u32[]{:S(2)}, u32[]{:S(2)}) collective-permute-start(bf16[880,128]{1,0:T(8,128)(2,1)S(1)} %add_convert_fusion.refs_0_), channel_id=1, source_target_pairs={{0,2},{1,3},{2,0},{3,1},{4,6},{5,7},{6,4},{7,5},{8,10},{9,11},{10,... | collective-permute-start | bytes 675848 | tf_op jit(solution)/shard_map/ppermute | solution.py:396
  105.6 2.0 %collective-permute-start.10 = (bf16[128,128]{1,0:T(8,128)(2,1)S(1)}, bf16[128,128]{1,0:T(8,128)(2,1)S(1)}, u32[]{:S(2)}, u32[]{:S(2)}) collective-permute-start(bf16[128,128]{1,0:T(8,128)(2,1)S(1)} %get-tuple-element.69), channel_id=1, source_target_pairs={{0,4},{4,0},{8,12},{12,8},{1,5},{5,1},{9,13},{13,9},{2,6},{6,2},{1... | collective-permute-start | bytes 98312 | tf_op jit(solution)/shard_map/ppermute | solution.py:408
  107.7 0.7 collective-permute-start.11
  108.3 0.6 collective-permute-start.12
  109.0 0.6 collective-permute-done.10.x_refs_0_
  109.6 2.7 %collective-permute-done.12.y_refs_0_ = bf16[128,128]{1,0:T(8,128)(2,1)S(1)} collective-permute-done((bf16[128,128]{1,0:T(8,128)(2,1)S(1)}, bf16[128,128]{1,0:T(8,128)(2,1)S(1)}, u32[]{:S(2)}, u32[]{:S(2)}) %collective-permute-start.12) | collective-permute-done | bytes 32800 | tf_op jit(solution)/shard_map/ppermute | solution.py:408
  112.3 0.5 collective-permute-start.14
  112.8 1.9 %finish.1 = f32[2048,128]{1,0:T(8,128)} custom-call(f32[2048,128]{1,0:T(8,128)S(1)} %get-tuple-element.44.dmixed_ref, f32[2592,128]{1,0:T(8,128)S(1)} %get-tuple-element.64.dext_ref, s32[1,512]{1,0:T(1,128)S(1)} %bitcast.18, bf16[128,128]{1,0:T(8,128)(2,1)S(1)} %collective-permute-done.10.x_refs_0_, bf16[128,128]{1,0:T(8,128)(2,1)S(1)} %collective-permute-done.11.x_refs_1_, ...), custom_call_target="tpu_custom_call" | custom-call | flops 268435456 | bytes 4194304 | tf_op jit(solution)/shard_map/finish/pallas_call | solution.py:286
  114.7 1.4 %assemble.1 = (f32[3456,128]{1,0:T(8,128)}, f32[19,128]{1,0:T(8,128)}) custom-call(bf16[880,128]{1,0:T(8,128)(2,1)S(1)} %add_convert_fusion.refs_0_, bf16[880,128]{1,0:T(8,128)(2,1)S(1)} %collective-permute-done.13.refs_1_, bf16[880,128]{1,0:T(8,128)(2,1)S(1)} %collective-permute-done.9.refs_2_, bf16[880,128]{1,0:T(8,128)(2,1)S(1)} %collective-permute-done.14.refs_3_), custom_call_target="tpu_custom_call" | custom-call | tf_op jit(solution)/shard_map/assemble/pallas_call | solution.py:371
  (19 shorter events, 0.1 us)
Async XLA Ops:
  0.6 10.9 %copy-start = (bf16[2048,128]{1,0:T(8,128)(2,1)S(1)}, bf16[2048,128]{1,0:T(8,128)(2,1)}, u32[]{:S(2)}) copy-start(bf16[2048,128]{1,0:T(8,128)(2,1)} %own_hbm.3) | copy-start | bytes 1572868
  0.6 10.9 %copy-start.1 = (bf16[27,128,128]{2,1,0:T(8,128)(2,1)S(1)}, bf16[27,128,128]{2,1,0:T(8,128)(2,1)}, u32[]{:S(2)}) copy-start(bf16[27,128,128]{2,1,0:T(8,128)(2,1)} %param.7) | copy-start | bytes 2654212
  3.6 7.8 %collective-permute-start = (bf16[128,128]{1,0:T(8,128)(2,1)}, bf16[128,128]{1,0:T(8,128)(2,1)S(1)}, u32[]{:S(2)}, u32[]{:S(2)}) collective-permute-start(bf16[128,128]{1,0:T(8,128)(2,1)} %get-tuple-element.41), channel_id=1, source_target_pairs={{0,4},{4,0},{8,12},{12,8},{1,5},{5,1},{9,13},{13,9},{2,6},{6,2},{1... | collective-permute-start | bytes 98312 | tf_op jit(solution)/shard_map/ppermute | solution.py:408
  6.7 4.7 %collective-permute-start.1 = (bf16[128,128]{1,0:T(8,128)(2,1)}, bf16[128,128]{1,0:T(8,128)(2,1)S(1)}, u32[]{:S(2)}, u32[]{:S(2)}) collective-permute-start(bf16[128,128]{1,0:T(8,128)(2,1)} %get-tuple-element.42), channel_id=1, source_target_pairs={{4,8},{8,4},{5,9},{9,5},{6,10},{10,6},{7,11},{11,7},{20,24},{24,20... | collective-permute-start | bytes 98312 | tf_op jit(solution)/shard_map/ppermute | solution.py:410
  7.3 4.2 %collective-permute-start.2 = (bf16[128,128]{1,0:T(8,128)(2,1)}, bf16[128,128]{1,0:T(8,128)(2,1)S(1)}, u32[]{:S(2)}, u32[]{:S(2)}) collective-permute-start(bf16[128,128]{1,0:T(8,128)(2,1)} %get-tuple-element.43), channel_id=1, source_target_pairs={{0,2},{2,0},{1,3},{3,1},{4,6},{6,4},{5,7},{7,5},{8,10},{10,8},{9,1... | collective-permute-start | bytes 98312 | tf_op jit(solution)/shard_map/ppermute | solution.py:408
  53.4 22.2 %collective-permute-start.3 = (bf16[880,128]{1,0:T(8,128)(2,1)S(1)}, bf16[880,128]{1,0:T(8,128)(2,1)S(1)}, u32[]{:S(2)}, u32[]{:S(2)}) collective-permute-start(bf16[880,128]{1,0:T(8,128)(2,1)S(1)} %get-tuple-element.48), channel_id=1, source_target_pairs={{0,1},{1,0},{2,3},{3,2},{4,5},{5,4},{6,7},{7,6},{8,9},{9,8},{10,11... | collective-permute-start | bytes 675848 | tf_op jit(solution)/shard_map/ppermute | solution.py:396
  53.5 22.1 %collective-permute-start.4 = (bf16[880,128]{1,0:T(8,128)(2,1)S(1)}, bf16[880,128]{1,0:T(8,128)(2,1)S(1)}, u32[]{:S(2)}, u32[]{:S(2)}) collective-permute-start(bf16[880,128]{1,0:T(8,128)(2,1)S(1)} %get-tuple-element.49), channel_id=1, source_target_pairs={{0,2},{1,3},{2,0},{3,1},{4,6},{5,7},{6,4},{7,5},{8,10},{9,11},{10,... | collective-permute-start | bytes 675848 | tf_op jit(solution)/shard_map/ppermute | solution.py:396
  55.1 20.5 %collective-permute-start.5 = (bf16[880,128]{1,0:T(8,128)(2,1)S(1)}, bf16[880,128]{1,0:T(8,128)(2,1)S(1)}, u32[]{:S(2)}, u32[]{:S(2)}) collective-permute-start(bf16[880,128]{1,0:T(8,128)(2,1)S(1)} %get-tuple-element.50), channel_id=1, source_target_pairs={{0,3},{1,2},{2,1},{3,0},{4,7},{5,6},{6,5},{7,4},{8,11},{9,10},{10,... | collective-permute-start | bytes 675848 | tf_op jit(solution)/shard_map/ppermute | solution.py:396
  75.8 28.2 %collective-permute-start.8 = (bf16[880,128]{1,0:T(8,128)(2,1)S(1)}, bf16[880,128]{1,0:T(8,128)(2,1)S(1)}, u32[]{:S(2)}, u32[]{:S(2)}) collective-permute-start(bf16[880,128]{1,0:T(8,128)(2,1)S(1)} %add_convert_fusion.1), channel_id=1, source_target_pairs={{0,12},{4,8},{8,4},{12,0},{1,13},{5,9},{9,5},{13,1},{2,14},{6,10},... | collective-permute-start | bytes 675848 | tf_op jit(solution)/shard_map/ppermute | solution.py:396
  78.3 25.7 %collective-permute-start.7 = (bf16[880,128]{1,0:T(8,128)(2,1)S(1)}, bf16[880,128]{1,0:T(8,128)(2,1)S(1)}, u32[]{:S(2)}, u32[]{:S(2)}) collective-permute-start(bf16[880,128]{1,0:T(8,128)(2,1)S(1)} %add_convert_fusion.1), channel_id=1, source_target_pairs={{0,8},{4,12},{8,0},{12,4},{1,9},{5,13},{9,1},{13,5},{2,10},{6,14},... | collective-permute-start | bytes 675848 | tf_op jit(solution)/shard_map/ppermute | solution.py:396
  81.7 22.3 %collective-permute-start.6 = (bf16[880,128]{1,0:T(8,128)(2,1)S(1)}, bf16[880,128]{1,0:T(8,128)(2,1)S(1)}, u32[]{:S(2)}, u32[]{:S(2)}) collective-permute-start(bf16[880,128]{1,0:T(8,128)(2,1)S(1)} %add_convert_fusion.1), channel_id=1, source_target_pairs={{0,4},{4,0},{8,12},{12,8},{1,5},{5,1},{9,13},{13,9},{2,6},{6,2},{1... | collective-permute-start | bytes 675848 | tf_op jit(solution)/shard_map/ppermute | solution.py:396
  81.7 31.1 %copy-start.2 = (s32[4,128]{1,0:T(4,128)S(1)}, s32[4,128]{1,0:T(4,128)}, u32[]{:S(2)}) copy-start(s32[4,128]{1,0:T(4,128)} %send_hbm.1) | copy-start | bytes 6148
  104.1 8.2 %collective-permute-start.9 = (bf16[880,128]{1,0:T(8,128)(2,1)S(1)}, bf16[880,128]{1,0:T(8,128)(2,1)S(1)}, u32[]{:S(2)}, u32[]{:S(2)}) collective-permute-start(bf16[880,128]{1,0:T(8,128)(2,1)S(1)} %add_convert_fusion.refs_0_), channel_id=1, source_target_pairs={{0,2},{1,3},{2,0},{3,1},{4,6},{5,7},{6,4},{7,5},{8,10},{9,11},{10,... | collective-permute-start | bytes 675848 | tf_op jit(solution)/shard_map/ppermute | solution.py:396
  105.6 3.9 %collective-permute-start.10 = (bf16[128,128]{1,0:T(8,128)(2,1)S(1)}, bf16[128,128]{1,0:T(8,128)(2,1)S(1)}, u32[]{:S(2)}, u32[]{:S(2)}) collective-permute-start(bf16[128,128]{1,0:T(8,128)(2,1)S(1)} %get-tuple-element.69), channel_id=1, source_target_pairs={{0,4},{4,0},{8,12},{12,8},{1,5},{5,1},{9,13},{13,9},{2,6},{6,2},{1... | collective-permute-start | bytes 98312 | tf_op jit(solution)/shard_map/ppermute | solution.py:408
  107.7 1.9 %collective-permute-start.11 = (bf16[128,128]{1,0:T(8,128)(2,1)S(1)}, bf16[128,128]{1,0:T(8,128)(2,1)S(1)}, u32[]{:S(2)}, u32[]{:S(2)}) collective-permute-start(bf16[128,128]{1,0:T(8,128)(2,1)S(1)} %get-tuple-element.70), channel_id=1, source_target_pairs={{4,8},{8,4},{5,9},{9,5},{6,10},{10,6},{7,11},{11,7},{20,24},{24,20... | collective-permute-start | bytes 98312 | tf_op jit(solution)/shard_map/ppermute | solution.py:410
  108.3 4.0 %collective-permute-start.12 = (bf16[128,128]{1,0:T(8,128)(2,1)S(1)}, bf16[128,128]{1,0:T(8,128)(2,1)S(1)}, u32[]{:S(2)}, u32[]{:S(2)}) collective-permute-start(bf16[128,128]{1,0:T(8,128)(2,1)S(1)} %get-tuple-element.71), channel_id=1, source_target_pairs={{0,2},{2,0},{1,3},{3,1},{4,6},{6,4},{5,7},{7,5},{8,10},{10,8},{9,1... | collective-permute-start | bytes 98312 | tf_op jit(solution)/shard_map/ppermute | solution.py:408
  112.3 2.4 %collective-permute-start.13 = (bf16[880,128]{1,0:T(8,128)(2,1)S(1)}, bf16[880,128]{1,0:T(8,128)(2,1)S(1)}, u32[]{:S(2)}, u32[]{:S(2)}) collective-permute-start(bf16[880,128]{1,0:T(8,128)(2,1)S(1)} %add_convert_fusion.refs_0_), channel_id=1, source_target_pairs={{0,1},{1,0},{2,3},{3,2},{4,5},{5,4},{6,7},{7,6},{8,9},{9,8},{10,11... | collective-permute-start | bytes 675848 | tf_op jit(solution)/shard_map/ppermute | solution.py:396
  112.3 2.4 %collective-permute-start.14 = (bf16[880,128]{1,0:T(8,128)(2,1)S(1)}, bf16[880,128]{1,0:T(8,128)(2,1)S(1)}, u32[]{:S(2)}, u32[]{:S(2)}) collective-permute-start(bf16[880,128]{1,0:T(8,128)(2,1)S(1)} %collective-permute-done.9.refs_2_), channel_id=1, source_target_pairs={{0,1},{1,0},{2,3},{3,2},{4,5},{5,4},{6,7},{7,6},{8,9},{9,8},{10,11... | collective-permute-start | bytes 675848 | tf_op jit(solution)/shard_map/ppermute | solution.py:396

commit v8 on v7

--- a/solution.py
+++ b/solution.py
@@ -12,7 +12,7 @@
 SCATTER_STREAMS = 2
 SEGMENT = 256
 BY_MATMUL = 8
-SCATTER_STEPS = 64
+SCATTER_STEPS = 32
 FIRST_PART = 512
 CHUNKS = 2
 HEAD_ROWS = 32
@@ -200,10 +200,11 @@
     index = refs[offsets:]
     streams, stream, chans = dpre_ref.shape
     share = stream // SCATTER_STEPS
-    copies, = fetch(map_hbm, index, sems, first * streams, stream, (0, stream))
+    part = stream // 4
+    ready, later = fetch(map_hbm, index, sems, first * streams, stream, (0, part, stream))
     for table in tables:
         table[...] = jnp.zeros_like(table)
-    for copy in copies:
+    for copy in ready:
         copy.wait()
 
     def step(j, carry):
@@ -216,7 +217,10 @@
                     tables[k][where, :] = tables[k][where, :] + value
         return carry
 
-    lax.fori_loop(0, SCATTER_STEPS, step, 0)
+    lax.fori_loop(0, SCATTER_STEPS // 4, step, 0)
+    for copy in later:
+        copy.wait()
+    lax.fori_loop(SCATTER_STEPS // 4, SCATTER_STEPS, step, 0)
     tiles = 3
     height = out_ref.shape[0] // tiles
 
@@ -248,7 +252,7 @@
         in_specs=[HBM, VMEM, VMEM] + ([VMEM] if has_before else []),
         out_specs=[VMEM] * (5 if has_before else 1),
         scratch_shapes=[
-            pltpu.SemaphoreType.DMA((1, offsets * SCATTER_STREAMS)),
+            pltpu.SemaphoreType.DMA((2, offsets * SCATTER_STREAMS)),
         ]
         + [pltpu.VMEM((table_rows, chans), jnp.float32)] * offsets
         + [pltpu.SMEM((stream,), jnp.int32)] * (offsets * SCATTER_STREAMS),

time: 116 us -> 115 us (level)
  Pallas kernels: 90.4 us -> 89.1 us
    pallas_call x2, Pallas kernels: 42.4 us -> 41.1 us  [scatter(): pl.pallas_call(functools.partial(scatter_kernel, first, offsets, has_befo...]
  transfers between devices with their start and end apart: 15 -> 15, of which waited for: 3 -> 3; matrix products, arithmetic and copies ran while one was open for 2% -> 2% of each run, Pallas kernels for 38% -> 37%
where the time goes in v8:
time: 115 us
  Pallas kernels  89.1 us (77%)
  starting transfers between devices  18.5 us (16%)
  waiting for transfers between devices  3.53 us (3%)
  other arithmetic  1.94 us (2%)
    pallas_call x1, Pallas kernels, forward(): pl.pallas_call(functools.partial(forward_kernel, classes), out_shape=(jax...  41.8 us
    pallas_call x2, Pallas kernels, scatter(): pl.pallas_call(functools.partial(scatter_kernel, first, offsets, has_befo...  41.1 us
    ppermute x9, starting transfers between devices, exchange(): lax.ppermute(shard, axes, [(i, i ^ distance) for i in range(group_size(ax...  9.9 us
    ppermute x4, starting transfers between devices, swap_edges(): got = [lax.ppermute(over_even, axis, even_pairs)]  7.3 us
    ppermute x4, waiting for transfers between devices, swap_edges(): got = [lax.ppermute(over_even, axis, even_pairs)]  3.5 us
    pallas_call x1, Pallas kernels, outgoing(): pl.pallas_call(functools.partial(outgoing_kernel, ('ty', 'tx')), out_shap...  2.9 us
  transfers between devices with their start and end apart: 15, of which 3 were waited for; matrix products, arithmetic and copies ran while one was open for 2% of the time, Pallas kernels for 37%

profile of v8, /device:TPU:0, one launch (start us, length us, event | category | flops | bytes accessed | tf_op | source)
XLA Modules:
  0.0 114.7 jit_solution(1727344033504751064)
XLA Ops:
  0.6 2.9 %outgoing.1 = (bf16[128,128]{1,0:T(8,128)(2,1)}, bf16[128,128]{1,0:T(8,128)(2,1)}, bf16[128,128]{1,0:T(8,128)(2,1)}, bf16[128,128]{1,0:T(8,128)(2,1)}) custom-call(s32[4,128]{1,0:T(4,128)} %send_hbm.1, bf16[2048,128]{1,0:T(8,128)(2,1)} %own_hbm.3), custom_call_target="tpu_custom_call" | custom-call | bytes 8388608 | tf_op jit(solution)/shard_map/outgoing/pallas_call | solution.py:334
  3.6 3.1 %collective-permute-start = (bf16[128,128]{1,0:T(8,128)(2,1)}, bf16[128,128]{1,0:T(8,128)(2,1)S(1)}, u32[]{:S(2)}, u32[]{:S(2)}) collective-permute-start(bf16[128,128]{1,0:T(8,128)(2,1)} %get-tuple-element.41), channel_id=1, source_target_pairs={{0,4},{4,0},{8,12},{12,8},{1,5},{5,1},{9,13},{13,9},{2,6},{6,2},{1... | collective-permute-start | bytes 98312 | tf_op jit(solution)/shard_map/ppermute | solution.py:412
  6.7 0.7 collective-permute-start.1
  7.3 1.6 %collective-permute-start.2 = (bf16[128,128]{1,0:T(8,128)(2,1)}, bf16[128,128]{1,0:T(8,128)(2,1)S(1)}, u32[]{:S(2)}, u32[]{:S(2)}) collective-permute-start(bf16[128,128]{1,0:T(8,128)(2,1)} %get-tuple-element.43), channel_id=1, source_target_pairs={{0,2},{2,0},{1,3},{3,1},{4,6},{6,4},{5,7},{7,5},{8,10},{10,8},{9,1... | collective-permute-start | bytes 98312 | tf_op jit(solution)/shard_map/ppermute | solution.py:412
  8.9 1.0 fusion
  9.9 0.7 broadcast_minimum_fusion
  10.6 0.7 pad.4.class_ref
  11.3 0.0 collective-permute-done.x_refs_0_
  11.3 0.0 collective-permute-done.1.x_refs_1_
  11.3 0.2 collective-permute-done.2.y_refs_0_
  11.5 41.8 %forward.1 = (f32[2048,128]{1,0:T(8,128)S(1)}, f32[2048,128]{1,0:T(8,128)S(1)}, f32[3520,128]{1,0:T(8,128)S(1)}, bf16[3456,128]{1,0:T(8,128)(2,1)S(1)}) custom-call(s32[55296]{0:T(1024)S(1)} %reshape.30.map_hbm, s32[8,8,256]{2,1,0:T(8,128)S(1)} %bitcast.16, bf16[2048,128]{1,0:T(8,128)(2,1)S(1)} %copy-done, ...), custom_call_target="tpu_custom_call" | custom-call | tf_op jit(solution)/shard_map/forward/pallas_call | solution.py:164
  53.3 0.1 dynamic-slice_convert_fusion
  53.4 0.1 collective-permute-start.3
  53.5 1.5 %collective-permute-start.4 = (bf16[880,128]{1,0:T(8,128)(2,1)S(1)}, bf16[880,128]{1,0:T(8,128)(2,1)S(1)}, u32[]{:S(2)}, u32[]{:S(2)}) collective-permute-start(bf16[880,128]{1,0:T(8,128)(2,1)S(1)} %get-tuple-element.49), channel_id=1, source_target_pairs={{0,2},{1,3},{2,0},{3,1},{4,6},{5,7},{6,4},{7,5},{8,10},{9,11},{10,... | collective-permute-start | bytes 675848 | tf_op jit(solution)/shard_map/ppermute | solution.py:400
  55.1 0.3 collective-permute-start.5
  55.4 19.5 %scatter_0.1.refs_0_ = f32[2592,128]{1,0:T(8,128)S(1)} custom-call(s32[55296]{0:T(1024)S(1)} %reshape.30.map_hbm, f32[2,1024,128]{2,1,0:T(8,128)S(1)} %bitcast.13, bf16[3456,128]{1,0:T(8,128)(2,1)S(1)} %get-tuple-element.52.weight_ref), custom_call_target="tpu_custom_call" | custom-call | flops 872415232 | bytes 41943040 | tf_op jit(solution)/shard_map/scatter_0/pallas_call | solution.py:248
  74.9 0.0 collective-permute-done.4
  75.0 0.1 add_convert_fusion.1
  75.1 2.6 %collective-permute-start.8 = (bf16[880,128]{1,0:T(8,128)(2,1)S(1)}, bf16[880,128]{1,0:T(8,128)(2,1)S(1)}, u32[]{:S(2)}, u32[]{:S(2)}) collective-permute-start(bf16[880,128]{1,0:T(8,128)(2,1)S(1)} %add_convert_fusion.1), channel_id=1, source_target_pairs={{0,12},{4,8},{8,4},{12,0},{1,13},{5,9},{9,5},{13,1},{2,14},{6,10},... | collective-permute-start | bytes 675848 | tf_op jit(solution)/shard_map/ppermute | solution.py:400
  77.6 3.4 %collective-permute-start.7 = (bf16[880,128]{1,0:T(8,128)(2,1)S(1)}, bf16[880,128]{1,0:T(8,128)(2,1)S(1)}, u32[]{:S(2)}, u32[]{:S(2)}) collective-permute-start(bf16[880,128]{1,0:T(8,128)(2,1)S(1)} %add_convert_fusion.1), channel_id=1, source_target_pairs={{0,8},{4,12},{8,0},{12,4},{1,9},{5,13},{9,1},{13,5},{2,10},{6,14},... | collective-permute-start | bytes 675848 | tf_op jit(solution)/shard_map/ppermute | solution.py:400
  81.0 21.6 %scatter_13.1 = (f32[2592,128]{1,0:T(8,128)S(1)}, bf16[128,128]{1,0:T(8,128)(2,1)S(1)}, bf16[128,128]{1,0:T(8,128)(2,1)}, bf16[128,128]{1,0:T(8,128)(2,1)S(1)}, bf16[128,128]{1,0:T(8,128)(2,1)S(1)}) custom-call(s32[55296]{0:T(1024)S(1)} %reshape.30.map_hbm, f32[2,1024,128]{2,1,0:T(8,128)S(1)} %bitcast.14, ...), custom_call_target="tpu_custom_call" | custom-call | flops 939524096 | bytes 41943040 | tf_op jit(solution)/shard_map/scatter_13/pallas_call | solution.py:248
  102.6 0.0 collective-permute-done.8
  102.6 0.1 add_convert_fusion.refs_0_
  102.7 1.5 %collective-permute-start.9 = (bf16[880,128]{1,0:T(8,128)(2,1)S(1)}, bf16[880,128]{1,0:T(8,128)(2,1)S(1)}, u32[]{:S(2)}, u32[]{:S(2)}) collective-permute-start(bf16[880,128]{1,0:T(8,128)(2,1)S(1)} %add_convert_fusion.refs_0_), channel_id=1, source_target_pairs={{0,2},{1,3},{2,0},{3,1},{4,6},{5,7},{6,4},{7,5},{8,10},{9,11},{10,... | collective-permute-start | bytes 675848 | tf_op jit(solution)/shard_map/ppermute | solution.py:400
  104.3 2.0 %collective-permute-start.10 = (bf16[128,128]{1,0:T(8,128)(2,1)S(1)}, bf16[128,128]{1,0:T(8,128)(2,1)S(1)}, u32[]{:S(2)}, u32[]{:S(2)}) collective-permute-start(bf16[128,128]{1,0:T(8,128)(2,1)S(1)} %get-tuple-element.69), channel_id=1, source_target_pairs={{0,4},{4,0},{8,12},{12,8},{1,5},{5,1},{9,13},{13,9},{2,6},{6,2},{1... | collective-permute-start | bytes 98312 | tf_op jit(solution)/shard_map/ppermute | solution.py:412
  106.3 0.7 collective-permute-start.11
  106.9 0.6 collective-permute-start.12
  107.6 0.6 collective-permute-done.10.x_refs_0_
  108.2 2.7 %collective-permute-done.12.y_refs_0_ = bf16[128,128]{1,0:T(8,128)(2,1)S(1)} collective-permute-done((bf16[128,128]{1,0:T(8,128)(2,1)S(1)}, bf16[128,128]{1,0:T(8,128)(2,1)S(1)}, u32[]{:S(2)}, u32[]{:S(2)}) %collective-permute-start.12) | collective-permute-done | bytes 32800 | tf_op jit(solution)/shard_map/ppermute | solution.py:412
  110.9 0.5 collective-permute-start.14
  111.4 1.9 %finish.1 = f32[2048,128]{1,0:T(8,128)} custom-call(f32[2048,128]{1,0:T(8,128)S(1)} %get-tuple-element.44.dmixed_ref, f32[2592,128]{1,0:T(8,128)S(1)} %get-tuple-element.64.dext_ref, s32[1,512]{1,0:T(1,128)S(1)} %bitcast.18, bf16[128,128]{1,0:T(8,128)(2,1)S(1)} %collective-permute-done.10.x_refs_0_, bf16[128,128]{1,0:T(8,128)(2,1)S(1)} %collective-permute-done.11.x_refs_1_, ...), custom_call_target="tpu_custom_call" | custom-call | flops 268435456 | bytes 4194304 | tf_op jit(solution)/shard_map/finish/pallas_call | solution.py:290
  113.3 1.4 %assemble.1 = (f32[3456,128]{1,0:T(8,128)}, f32[19,128]{1,0:T(8,128)}) custom-call(bf16[880,128]{1,0:T(8,128)(2,1)S(1)} %add_convert_fusion.refs_0_, bf16[880,128]{1,0:T(8,128)(2,1)S(1)} %collective-permute-done.13.refs_1_, bf16[880,128]{1,0:T(8,128)(2,1)S(1)} %collective-permute-done.9.refs_2_, bf16[880,128]{1,0:T(8,128)(2,1)S(1)} %collective-permute-done.14.refs_3_), custom_call_target="tpu_custom_call" | custom-call | tf_op jit(solution)/shard_map/assemble/pallas_call | solution.py:375
  (19 shorter events, 0.1 us)
Async XLA Ops:
  0.6 10.9 %copy-start = (bf16[2048,128]{1,0:T(8,128)(2,1)S(1)}, bf16[2048,128]{1,0:T(8,128)(2,1)}, u32[]{:S(2)}) copy-start(bf16[2048,128]{1,0:T(8,128)(2,1)} %own_hbm.3) | copy-start | bytes 1572868
  0.6 10.9 %copy-start.1 = (bf16[27,128,128]{2,1,0:T(8,128)(2,1)S(1)}, bf16[27,128,128]{2,1,0:T(8,128)(2,1)}, u32[]{:S(2)}) copy-start(bf16[27,128,128]{2,1,0:T(8,128)(2,1)} %param.7) | copy-start | bytes 2654212
  3.6 7.8 %collective-permute-start = (bf16[128,128]{1,0:T(8,128)(2,1)}, bf16[128,128]{1,0:T(8,128)(2,1)S(1)}, u32[]{:S(2)}, u32[]{:S(2)}) collective-permute-start(bf16[128,128]{1,0:T(8,128)(2,1)} %get-tuple-element.41), channel_id=1, source_target_pairs={{0,4},{4,0},{8,12},{12,8},{1,5},{5,1},{9,13},{13,9},{2,6},{6,2},{1... | collective-permute-start | bytes 98312 | tf_op jit(solution)/shard_map/ppermute | solution.py:412
  6.7 4.7 %collective-permute-start.1 = (bf16[128,128]{1,0:T(8,128)(2,1)}, bf16[128,128]{1,0:T(8,128)(2,1)S(1)}, u32[]{:S(2)}, u32[]{:S(2)}) collective-permute-start(bf16[128,128]{1,0:T(8,128)(2,1)} %get-tuple-element.42), channel_id=1, source_target_pairs={{4,8},{8,4},{5,9},{9,5},{6,10},{10,6},{7,11},{11,7},{20,24},{24,20... | collective-permute-start | bytes 98312 | tf_op jit(solution)/shard_map/ppermute | solution.py:414
  7.3 4.2 %collective-permute-start.2 = (bf16[128,128]{1,0:T(8,128)(2,1)}, bf16[128,128]{1,0:T(8,128)(2,1)S(1)}, u32[]{:S(2)}, u32[]{:S(2)}) collective-permute-start(bf16[128,128]{1,0:T(8,128)(2,1)} %get-tuple-element.43), channel_id=1, source_target_pairs={{0,2},{2,0},{1,3},{3,1},{4,6},{6,4},{5,7},{7,5},{8,10},{10,8},{9,1... | collective-permute-start | bytes 98312 | tf_op jit(solution)/shard_map/ppermute | solution.py:412
  53.4 21.5 %collective-permute-start.3 = (bf16[880,128]{1,0:T(8,128)(2,1)S(1)}, bf16[880,128]{1,0:T(8,128)(2,1)S(1)}, u32[]{:S(2)}, u32[]{:S(2)}) collective-permute-start(bf16[880,128]{1,0:T(8,128)(2,1)S(1)} %get-tuple-element.48), channel_id=1, source_target_pairs={{0,1},{1,0},{2,3},{3,2},{4,5},{5,4},{6,7},{7,6},{8,9},{9,8},{10,11... | collective-permute-start | bytes 675848 | tf_op jit(solution)/shard_map/ppermute | solution.py:400
  53.5 21.4 %collective-permute-start.4 = (bf16[880,128]{1,0:T(8,128)(2,1)S(1)}, bf16[880,128]{1,0:T(8,128)(2,1)S(1)}, u32[]{:S(2)}, u32[]{:S(2)}) collective-permute-start(bf16[880,128]{1,0:T(8,128)(2,1)S(1)} %get-tuple-element.49), channel_id=1, source_target_pairs={{0,2},{1,3},{2,0},{3,1},{4,6},{5,7},{6,4},{7,5},{8,10},{9,11},{10,... | collective-permute-start | bytes 675848 | tf_op jit(solution)/shard_map/ppermute | solution.py:400
  55.1 19.9 %collective-permute-start.5 = (bf16[880,128]{1,0:T(8,128)(2,1)S(1)}, bf16[880,128]{1,0:T(8,128)(2,1)S(1)}, u32[]{:S(2)}, u32[]{:S(2)}) collective-permute-start(bf16[880,128]{1,0:T(8,128)(2,1)S(1)} %get-tuple-element.50), channel_id=1, source_target_pairs={{0,3},{1,2},{2,1},{3,0},{4,7},{5,6},{6,5},{7,4},{8,11},{9,10},{10,... | collective-permute-start | bytes 675848 | tf_op jit(solution)/shard_map/ppermute | solution.py:400
  75.1 27.5 %collective-permute-start.8 = (bf16[880,128]{1,0:T(8,128)(2,1)S(1)}, bf16[880,128]{1,0:T(8,128)(2,1)S(1)}, u32[]{:S(2)}, u32[]{:S(2)}) collective-permute-start(bf16[880,128]{1,0:T(8,128)(2,1)S(1)} %add_convert_fusion.1), channel_id=1, source_target_pairs={{0,12},{4,8},{8,4},{12,0},{1,13},{5,9},{9,5},{13,1},{2,14},{6,10},... | collective-permute-start | bytes 675848 | tf_op jit(solution)/shard_map/ppermute | solution.py:400
  77.6 25.0 %collective-permute-start.7 = (bf16[880,128]{1,0:T(8,128)(2,1)S(1)}, bf16[880,128]{1,0:T(8,128)(2,1)S(1)}, u32[]{:S(2)}, u32[]{:S(2)}) collective-permute-start(bf16[880,128]{1,0:T(8,128)(2,1)S(1)} %add_convert_fusion.1), channel_id=1, source_target_pairs={{0,8},{4,12},{8,0},{12,4},{1,9},{5,13},{9,1},{13,5},{2,10},{6,14},... | collective-permute-start | bytes 675848 | tf_op jit(solution)/shard_map/ppermute | solution.py:400
  81.0 21.6 %collective-permute-start.6 = (bf16[880,128]{1,0:T(8,128)(2,1)S(1)}, bf16[880,128]{1,0:T(8,128)(2,1)S(1)}, u32[]{:S(2)}, u32[]{:S(2)}) collective-permute-start(bf16[880,128]{1,0:T(8,128)(2,1)S(1)} %add_convert_fusion.1), channel_id=1, source_target_pairs={{0,4},{4,0},{8,12},{12,8},{1,5},{5,1},{9,13},{13,9},{2,6},{6,2},{1... | collective-permute-start | bytes 675848 | tf_op jit(solution)/shard_map/ppermute | solution.py:400
  81.0 30.4 %copy-start.2 = (s32[4,128]{1,0:T(4,128)S(1)}, s32[4,128]{1,0:T(4,128)}, u32[]{:S(2)}) copy-start(s32[4,128]{1,0:T(4,128)} %send_hbm.1) | copy-start | bytes 6148
  102.7 8.2 %collective-permute-start.9 = (bf16[880,128]{1,0:T(8,128)(2,1)S(1)}, bf16[880,128]{1,0:T(8,128)(2,1)S(1)}, u32[]{:S(2)}, u32[]{:S(2)}) collective-permute-start(bf16[880,128]{1,0:T(8,128)(2,1)S(1)} %add_convert_fusion.refs_0_), channel_id=1, source_target_pairs={{0,2},{1,3},{2,0},{3,1},{4,6},{5,7},{6,4},{7,5},{8,10},{9,11},{10,... | collective-permute-start | bytes 675848 | tf_op jit(solution)/shard_map/ppermute | solution.py:400
  104.3 3.9 %collective-permute-start.10 = (bf16[128,128]{1,0:T(8,128)(2,1)S(1)}, bf16[128,128]{1,0:T(8,128)(2,1)S(1)}, u32[]{:S(2)}, u32[]{:S(2)}) collective-permute-start(bf16[128,128]{1,0:T(8,128)(2,1)S(1)} %get-tuple-element.69), channel_id=1, source_target_pairs={{0,4},{4,0},{8,12},{12,8},{1,5},{5,1},{9,13},{13,9},{2,6},{6,2},{1... | collective-permute-start | bytes 98312 | tf_op jit(solution)/shard_map/ppermute | solution.py:412
  106.3 1.9 %collective-permute-start.11 = (bf16[128,128]{1,0:T(8,128)(2,1)S(1)}, bf16[128,128]{1,0:T(8,128)(2,1)S(1)}, u32[]{:S(2)}, u32[]{:S(2)}) collective-permute-start(bf16[128,128]{1,0:T(8,128)(2,1)S(1)} %get-tuple-element.70), channel_id=1, source_target_pairs={{4,8},{8,4},{5,9},{9,5},{6,10},{10,6},{7,11},{11,7},{20,24},{24,20... | collective-permute-start | bytes 98312 | tf_op jit(solution)/shard_map/ppermute | solution.py:414
  106.9 4.0 %collective-permute-start.12 = (bf16[128,128]{1,0:T(8,128)(2,1)S(1)}, bf16[128,128]{1,0:T(8,128)(2,1)S(1)}, u32[]{:S(2)}, u32[]{:S(2)}) collective-permute-start(bf16[128,128]{1,0:T(8,128)(2,1)S(1)} %get-tuple-element.71), channel_id=1, source_target_pairs={{0,2},{2,0},{1,3},{3,1},{4,6},{6,4},{5,7},{7,5},{8,10},{10,8},{9,1... | collective-permute-start | bytes 98312 | tf_op jit(solution)/shard_map/ppermute | solution.py:412
  110.9 2.4 %collective-permute-start.13 = (bf16[880,128]{1,0:T(8,128)(2,1)S(1)}, bf16[880,128]{1,0:T(8,128)(2,1)S(1)}, u32[]{:S(2)}, u32[]{:S(2)}) collective-permute-start(bf16[880,128]{1,0:T(8,128)(2,1)S(1)} %add_convert_fusion.refs_0_), channel_id=1, source_target_pairs={{0,1},{1,0},{2,3},{3,2},{4,5},{5,4},{6,7},{7,6},{8,9},{9,8},{10,11... | collective-permute-start | bytes 675848 | tf_op jit(solution)/shard_map/ppermute | solution.py:400
  110.9 2.4 %collective-permute-start.14 = (bf16[880,128]{1,0:T(8,128)(2,1)S(1)}, bf16[880,128]{1,0:T(8,128)(2,1)S(1)}, u32[]{:S(2)}, u32[]{:S(2)}) collective-permute-start(bf16[880,128]{1,0:T(8,128)(2,1)S(1)} %collective-permute-done.9.refs_2_), channel_id=1, source_target_pairs={{0,1},{1,0},{2,3},{3,2},{4,5},{5,4},{6,7},{7,6},{8,9},{9,8},{10,11... | collective-permute-start | bytes 675848 | tf_op jit(solution)/shard_map/ppermute | solution.py:400

commit v9 on v8

--- a/solution.py
+++ b/solution.py
@@ -13,6 +13,7 @@
 SEGMENT = 256
 BY_MATMUL = 8
 SCATTER_STEPS = 32
+STEPS_BEFORE = 24
 FIRST_PART = 512
 CHUNKS = 2
 HEAD_ROWS = 32
@@ -190,22 +191,10 @@
     )(map_flat, sparse, features, from_x, from_y, weights, class_t, label_blocks)
 
 
-def scatter_kernel(first, offsets, has_before, map_hbm, dpre_ref, weight_ref, *refs):
-    refs = list(refs)
-    before = refs.pop(0) if has_before else None
-    out_ref = refs.pop(0)
-    back_refs = [refs.pop(0) for _ in range(4)] if has_before else []
-    sems = refs.pop(0)
-    tables = refs[:offsets]
-    index = refs[offsets:]
+def add_rows(tables, index, dpre_ref, low, high):
+    offsets = len(tables)
     streams, stream, chans = dpre_ref.shape
     share = stream // SCATTER_STEPS
-    part = stream // 4
-    ready, later = fetch(map_hbm, index, sems, first * streams, stream, (0, part, stream))
-    for table in tables:
-        table[...] = jnp.zeros_like(table)
-    for copy in ready:
-        copy.wait()
 
     def step(j, carry):
         for n in range(share):
@@ -217,10 +206,55 @@
                     tables[k][where, :] = tables[k][where, :] + value
         return carry
 
-    lax.fori_loop(0, SCATTER_STEPS // 4, step, 0)
+    lax.fori_loop(low, high, step, 0)
+
+
+def open_kernel(first, steps, map_hbm, dpre_ref, *refs):
+    streams, stream, chans = dpre_ref.shape
+    offsets = len(refs) // (1 + streams)
+    tables, sems, index = refs[:offsets], refs[offsets], refs[offsets + 1 :]
+    parts = (0, stream // 4, stream * steps // SCATTER_STEPS)
+    ready, later = fetch(map_hbm, index, sems, first * streams, stream, parts)
+    for table in tables:
+        table[...] = jnp.zeros_like(table)
+    for copy in ready:
+        copy.wait()
+    add_rows(tables, index, dpre_ref, 0, SCATTER_STEPS // 4)
     for copy in later:
         copy.wait()
-    lax.fori_loop(SCATTER_STEPS // 4, SCATTER_STEPS, step, 0)
+    add_rows(tables, index, dpre_ref, SCATTER_STEPS // 4, steps)
+
+
+def close_kernel(first, offsets, steps, has_before, map_hbm, dpre_ref, weight_ref, *refs):
+    refs = list(refs)
+    before = refs.pop(0) if has_before else None
+    streams, stream, chans = dpre_ref.shape
+    given = steps > 0
+    if given:
+        refs = refs[offsets:]
+    out_ref = refs.pop(0)
+    back_refs = [refs.pop(0) for _ in range(4)] if has_before else []
+    if given:
+        tables = refs[:offsets]
+        refs = refs[offsets:]
+    sems = refs.pop(0)
+    if not given:
+        tables = refs[:offsets]
+        refs = refs[offsets:]
+    index = refs
+    low = stream * steps // SCATTER_STEPS
+    middle = steps + (SCATTER_STEPS - steps) // (2 if given else 4)
+    parts = (low, stream * middle // SCATTER_STEPS, stream)
+    ready, later = fetch(map_hbm, index, sems, first * streams, stream, parts)
+    if not given:
+        for table in tables:
+            table[...] = jnp.zeros_like(table)
+    for copy in ready:
+        copy.wait()
+    add_rows(tables, index, dpre_ref, steps, middle)
+    for copy in later:
+        copy.wait()
+    add_rows(tables, index, dpre_ref, middle, SCATTER_STEPS)
     tiles = 3
     height = out_ref.shape[0] // tiles
 
@@ -241,30 +275,52 @@
             back_ref[...] = value.astype(jnp.bfloat16)
 
 
-def scatter(map_flat, dpre, flipped, before, first, offsets, table_rows, width):
+def scatter_open(map_flat, dpre, first, offsets, table_rows):
+    voxels, chans = dpre.shape
+    stream = voxels // SCATTER_STREAMS
+    return pl.pallas_call(
+        functools.partial(open_kernel, first, STEPS_BEFORE),
+        out_shape=[jax.ShapeDtypeStruct((table_rows, chans), jnp.float32)] * offsets,
+        in_specs=[HBM, VMEM],
+        out_specs=[VMEM] * offsets,
+        scratch_shapes=[pltpu.SemaphoreType.DMA((2, offsets * SCATTER_STREAMS))]
+        + [pltpu.SMEM((stream,), jnp.int32)] * (offsets * SCATTER_STREAMS),
+        compiler_params=pltpu.CompilerParams(vmem_limit_bytes=8 << 20),
+        cost_estimate=pl.CostEstimate(flops=0, bytes_accessed=40 << 20, transcendentals=0),
+        name=f"scatter_open_{first}",
+    )(map_flat, dpre.reshape(SCATTER_STREAMS, stream, chans))
+
+
+def scatter(map_flat, dpre, flipped, before, first, offsets, table_rows, width, tables=()):
     voxels, chans = dpre.shape
     stream = voxels // SCATTER_STREAMS
     has_before = before is not None
-    return pl.pallas_call(
-        functools.partial(scatter_kernel, first, offsets, has_before),
-        out_shape=[jax.ShapeDtypeStruct((table_rows, chans), jnp.float32)]
-        + [jax.ShapeDtypeStruct((width, chans), jnp.bfloat16)] * (4 if has_before else 0),
-        in_specs=[HBM, VMEM, VMEM] + ([VMEM] if has_before else []),
-        out_specs=[VMEM] * (5 if has_before else 1),
-        scratch_shapes=[
-            pltpu.SemaphoreType.DMA((2, offsets * SCATTER_STREAMS)),
-        ]
-        + [pltpu.VMEM((table_rows, chans), jnp.float32)] * offsets
+    steps = STEPS_BEFORE if tables else 0
+    outs = 5 if has_before else 1
+    table_shape = jax.ShapeDtypeStruct((table_rows, chans), jnp.float32)
+    result = pl.pallas_call(
+        functools.partial(close_kernel, first, offsets, steps, has_before),
+        out_shape=[table_shape]
+        + [jax.ShapeDtypeStruct((width, chans), jnp.bfloat16)] * (outs - 1)
+        + [table_shape] * len(tables),
+        in_specs=[HBM, VMEM, VMEM] + ([VMEM] if has_before else []) + [VMEM] * len(tables),
+        out_specs=[VMEM] * (outs + len(tables)),
+        scratch_shapes=[pltpu.SemaphoreType.DMA((2, offsets * SCATTER_STREAMS))]
+        + ([] if tables else [pltpu.VMEM((table_rows, chans), jnp.float32)] * offsets)
         + [pltpu.SMEM((stream,), jnp.int32)] * (offsets * SCATTER_STREAMS),
-        compiler_params=pltpu.CompilerParams(vmem_limit_bytes=21 << 20),
+        input_output_aliases={
+            3 + has_before + n: outs + n for n in range(len(tables))
+        },
+        compiler_params=pltpu.CompilerParams(vmem_limit_bytes=(8 if tables else 21) << 20),
         cost_estimate=pl.CostEstimate(
-            flops=2 * voxels * offsets * chans * chans, bytes_accessed=40 << 20, transcendentals=0
+            flops=2 * voxels * offsets * chans * chans, bytes_accessed=20 << 20, transcendentals=0
         ),
         name=f"scatter_{first}",
     )(
         map_flat, dpre.reshape(SCATTER_STREAMS, stream, chans), flipped,
-        *([before] if has_before else []),
-    )
+        *([before] if has_before else []), *tables,
+    )
+    return result[:outs]
 
 
 def finish_kernel(dmixed_ref, dext_ref, send_ref, x_refs, y_refs, out_ref, back_ref):
@@ -477,32 +533,40 @@
     got, dext = lax.optimization_barrier((got, dext))
     own = own + sum(piece.astype(jnp.float32) for piece in got)
 
+    (first, last), = chunks
+    own = own.astype(jnp.bfloat16)
+    tables = None
     stride = 1
     while stride < lax.axis_size("tx"):
         radix = min(4, lax.axis_size("tx") // stride)
         own = own.astype(jnp.bfloat16)
-        if chunks:
-            own, dext = scatter_beside(own, dext)
+        if tables is None:
+            own, held = lax.optimization_barrier((own, dpre))
+            tables = scatter_open(map_flat, held, first, last - first, table_rows)
         got = [own] + [exchange(own, ("tx",), m * stride) for m in range(1, radix)]
-        got, dext, halo = lax.optimization_barrier((got, dext, halo))
+        got, tables = lax.optimization_barrier((got, tables))
         got = [piece.astype(jnp.float32) for piece in got]
         while len(got) > 1:
             got = [a + b for a, b in zip(got[::2], got[1::2])]
         own = got[0]
         stride *= radix
-    while chunks:
-        own, dext = scatter_beside(own, dext)
-
-    from_y = swap_edges(halo[0], halo[1], "ty")
-    from_x = swap_edges(halo[2], halo[3], "tx")
+
     everywhere = {0: own.astype(jnp.bfloat16)}
     bit = pieces // 2
     while bit:
         if bit == 1:
-            everywhere, from_x, from_y = lax.optimization_barrier((everywhere, from_x, from_y))
+            everywhere[0], tables = lax.optimization_barrier((everywhere[0], tables))
+            dext, *halo = scatter(
+                map_flat, dpre, flipped, dext, first, last - first, table_rows, width, tables
+            )
+            everywhere, dext, halo = lax.optimization_barrier((everywhere, dext, halo))
+        elif bit == pieces // 2:
+            everywhere[0], tables = lax.optimization_barrier((everywhere[0], tables))
         for d, piece in list(everywhere.items()):
             everywhere[d | bit] = exchange(piece, square, bit)
         bit //= 2
+    from_y = swap_edges(halo[0], halo[1], "ty")
+    from_x = swap_edges(halo[2], halo[3], "tx")
     grad_input = finish(dmixed, dext, send_rows.reshape(1, -1), from_x, from_y)
     everywhere = [everywhere[d] for d in range(pieces)]
     count = voxels * lax.axis_size("tx") * lax.axis_size("ty") * lax.axis_size("rep")

time: 115 us -> 123 us (1.070)
  Pallas kernels: 89.1 us -> 97.4 us
    pallas_call x2 -> x3, Pallas kernels: 41.1 us -> 49.5 us  [the longest x2 29.2 us: scatter(): pl.pallas_call(functools.partial(close_kernel, first, offsets, steps, has...]
  transfers between devices with their start and end apart: 15 -> 15, of which waited for: 3 -> 3; matrix products, arithmetic and copies ran while one was open for 2% -> 1% of each run, Pallas kernels for 37% -> 42%
where the time goes in v9:
time: 123 us
  Pallas kernels  97.4 us (79%)
  starting transfers between devices  18.6 us (15%)
  waiting for transfers between devices  4.21 us (3%)
  other arithmetic  1.94 us (2%)
    pallas_call x1, Pallas kernels, forward(): pl.pallas_call(functools.partial(forward_kernel, classes), out_shape=(jax...  41.8 us
    pallas_call x2, Pallas kernels, scatter(): pl.pallas_call(functools.partial(close_kernel, first, offsets, steps, has...  29.2 us
    pallas_call x1, Pallas kernels, scatter_open(): pl.pallas_call(functools.partial(open_kernel, first, STEPS_BEFORE), out_s...  20.2 us
    ppermute x9, starting transfers between devices, exchange(): lax.ppermute(shard, axes, [(i, i ^ distance) for i in range(group_size(ax...  11 us
    ppermute x4, starting transfers between devices, swap_edges(): got = [lax.ppermute(over_even, axis, even_pairs)]  6.3 us
    ppermute x4, waiting for transfers between devices, swap_edges(): got = [lax.ppermute(over_even, axis, even_pairs)]  4.19 us
    pallas_call x1, Pallas kernels, outgoing(): pl.pallas_call(functools.partial(outgoing_kernel, ('ty', 'tx')), out_shap...  2.89 us
  transfers between devices with their start and end apart: 15, of which 3 were waited for; matrix products, arithmetic and copies ran while one was open for 1% of the time, Pallas kernels for 42%

profile of v9, /device:TPU:0, one launch (start us, length us, event | category | flops | bytes accessed | tf_op | source)
XLA Modules:
  0.0 123.2 jit_solution(3292875901538308862)
XLA Ops:
  0.7 2.9 %outgoing.1 = (bf16[128,128]{1,0:T(8,128)(2,1)}, bf16[128,128]{1,0:T(8,128)(2,1)}, bf16[128,128]{1,0:T(8,128)(2,1)}, bf16[128,128]{1,0:T(8,128)(2,1)}) custom-call(s32[4,128]{1,0:T(4,128)} %send_hbm.1, bf16[2048,128]{1,0:T(8,128)(2,1)} %own_hbm.3), custom_call_target="tpu_custom_call" | custom-call | bytes 8388608 | tf_op jit(solution)/shard_map/outgoing/pallas_call | solution.py:390
  3.6 3.1 %collective-permute-start = (bf16[128,128]{1,0:T(8,128)(2,1)}, bf16[128,128]{1,0:T(8,128)(2,1)S(1)}, u32[]{:S(2)}, u32[]{:S(2)}) collective-permute-start(bf16[128,128]{1,0:T(8,128)(2,1)} %get-tuple-element.81), channel_id=1, source_target_pairs={{0,4},{4,0},{8,12},{12,8},{1,5},{5,1},{9,13},{13,9},{2,6},{6,2},{1... | collective-permute-start | bytes 98312 | tf_op jit(solution)/shard_map/ppermute | solution.py:468
  6.7 0.7 collective-permute-start.1
  7.3 1.6 %collective-permute-start.2 = (bf16[128,128]{1,0:T(8,128)(2,1)}, bf16[128,128]{1,0:T(8,128)(2,1)S(1)}, u32[]{:S(2)}, u32[]{:S(2)}) collective-permute-start(bf16[128,128]{1,0:T(8,128)(2,1)} %get-tuple-element.83), channel_id=1, source_target_pairs={{0,2},{2,0},{1,3},{3,1},{4,6},{6,4},{5,7},{7,5},{8,10},{10,8},{9,1... | collective-permute-start | bytes 98312 | tf_op jit(solution)/shard_map/ppermute | solution.py:468
  8.9 1.0 fusion
  9.9 0.7 broadcast_minimum_fusion
  10.7 0.0 collective-permute-done.1.x_refs_1_
  10.7 0.8 collective-permute-done.2.y_refs_0_
  11.5 41.8 %forward.1 = (f32[2048,128]{1,0:T(8,128)S(1)}, f32[2048,128]{1,0:T(8,128)S(1)}, f32[3520,128]{1,0:T(8,128)S(1)}, bf16[3456,128]{1,0:T(8,128)(2,1)S(1)}) custom-call(s32[55296]{0:T(1024)S(1)} %reshape.33.map_hbm, s32[8,8,256]{2,1,0:T(8,128)S(1)} %bitcast.18, bf16[2048,128]{1,0:T(8,128)(2,1)S(1)} %copy-done, ...), custom_call_target="tpu_custom_call" | custom-call | tf_op jit(solution)/shard_map/forward/pallas_call | solution.py:165
  53.3 0.1 dynamic-slice_convert_fusion
  53.4 0.1 collective-permute-start.3
  53.5 1.6 %collective-permute-start.4 = (bf16[880,128]{1,0:T(8,128)(2,1)S(1)}, bf16[880,128]{1,0:T(8,128)(2,1)S(1)}, u32[]{:S(2)}, u32[]{:S(2)}) collective-permute-start(bf16[880,128]{1,0:T(8,128)(2,1)S(1)} %get-tuple-element.89), channel_id=1, source_target_pairs={{0,2},{1,3},{2,0},{3,1},{4,6},{5,7},{6,4},{7,5},{8,10},{9,11},{10,... | collective-permute-start | bytes 675848 | tf_op jit(solution)/shard_map/ppermute | solution.py:456
  55.1 0.3 collective-permute-start.5
  55.4 19.5 %scatter_0.1.refs_0_ = f32[2592,128]{1,0:T(8,128)S(1)} custom-call(s32[55296]{0:T(1024)S(1)} %reshape.33.map_hbm, f32[2,1024,128]{2,1,0:T(8,128)S(1)} %bitcast.14, bf16[3456,128]{1,0:T(8,128)(2,1)S(1)} %get-tuple-element.92.weight_ref), custom_call_target="tpu_custom_call" | custom-call | flops 872415232 | bytes 20971520 | tf_op jit(solution)/shard_map/scatter_0/pallas_call | solution.py:301
  74.9 0.0 collective-permute-done.3
  74.9 0.0 collective-permute-done.5
  74.9 0.1 add_convert_fusion.1
  75.0 4.5 %collective-permute-start.6 = (bf16[880,128]{1,0:T(8,128)(2,1)S(1)}, bf16[880,128]{1,0:T(8,128)(2,1)S(1)}, u32[]{:S(2)}, u32[]{:S(2)}) collective-permute-start(bf16[880,128]{1,0:T(8,128)(2,1)S(1)} %add_convert_fusion.1), channel_id=1, source_target_pairs={{0,4},{4,0},{8,12},{12,8},{1,5},{5,1},{9,13},{13,9},{2,6},{6,2},{1... | collective-permute-start | bytes 675848 | tf_op jit(solution)/shard_map/ppermute | solution.py:456
  79.5 2.4 %collective-permute-start.8 = (bf16[880,128]{1,0:T(8,128)(2,1)S(1)}, bf16[880,128]{1,0:T(8,128)(2,1)S(1)}, u32[]{:S(2)}, u32[]{:S(2)}) collective-permute-start(bf16[880,128]{1,0:T(8,128)(2,1)S(1)} %add_convert_fusion.1), channel_id=1, source_target_pairs={{0,12},{4,8},{8,4},{12,0},{1,13},{5,9},{9,5},{13,1},{2,14},{6,10},... | collective-permute-start | bytes 675848 | tf_op jit(solution)/shard_map/ppermute | solution.py:456
  82.0 20.2 %scatter_open_13.1 = (f32[2592,128]{1,0:T(8,128)S(1)}, f32[2592,128]{1,0:T(8,128)S(1)}, f32[2592,128]{1,0:T(8,128)S(1)}, f32[2592,128]{1,0:T(8,128)S(1)}, f32[25...) custom-call(s32[55296]{0:T(1024)S(1)} %reshape.33.map_hbm, ...), custom_call_target="tpu_custom_call" | custom-call | bytes 41943040 | tf_op jit(solution)/shard_map/scatter_open_13/pallas_call | solution.py:281
  102.2 0.1 add_convert_fusion.refs_0_
  102.4 1.5 %collective-permute-start.9 = (bf16[880,128]{1,0:T(8,128)(2,1)S(1)}, bf16[880,128]{1,0:T(8,128)(2,1)S(1)}, u32[]{:S(2)}, u32[]{:S(2)}) collective-permute-start(bf16[880,128]{1,0:T(8,128)(2,1)S(1)} %add_convert_fusion.refs_0_), channel_id=1, source_target_pairs={{0,2},{1,3},{2,0},{3,1},{4,6},{5,7},{6,4},{7,5},{8,10},{9,11},{10,... | collective-permute-start | bytes 675848 | tf_op jit(solution)/shard_map/ppermute | solution.py:456
  103.9 9.7 %scatter_13.1 = (f32[2592,128]{1,0:T(8,128)S(1)}, bf16[128,128]{1,0:T(8,128)(2,1)S(1)}, bf16[128,128]{1,0:T(8,128)(2,1)}, bf16[128,128]{1,0:T(8,128)(2,1)S(1)}, ...) custom-call(s32[55296]{0:T(1024)S(1)} %reshape.33.map_hbm, ...), custom_call_target="tpu_custom_call", output_to_operand_aliasing={{5}: (4, {}), {6}: (5, {}), {7}: (6, {}), {8}: (7, {}), {9}... | custom-call | flops 939524096 | bytes 20971520 | tf_op jit(solution)/shard_map/scatter_13/pallas_call | solution.py:301
  113.6 0.1 collective-permute-start.13
  113.7 0.5 collective-permute-start.14
  114.2 1.1 collective-permute-start.10
  115.3 0.7 collective-permute-start.11
  115.9 0.6 collective-permute-start.12
  116.5 1.6 %collective-permute-done.10.x_refs_0_ = bf16[128,128]{1,0:T(8,128)(2,1)S(1)} collective-permute-done((bf16[128,128]{1,0:T(8,128)(2,1)S(1)}, bf16[128,128]{1,0:T(8,128)(2,1)S(1)}, u32[]{:S(2)}, u32[]{:S(2)}) %collective-permute-start.10) | collective-permute-done | bytes 32800 | tf_op jit(solution)/shard_map/ppermute | solution.py:468
  118.1 1.8 %collective-permute-done.12.y_refs_0_ = bf16[128,128]{1,0:T(8,128)(2,1)S(1)} collective-permute-done((bf16[128,128]{1,0:T(8,128)(2,1)S(1)}, bf16[128,128]{1,0:T(8,128)(2,1)S(1)}, u32[]{:S(2)}, u32[]{:S(2)}) %collective-permute-start.12) | collective-permute-done | bytes 32800 | tf_op jit(solution)/shard_map/ppermute | solution.py:468
  119.9 1.9 %finish.1 = f32[2048,128]{1,0:T(8,128)} custom-call(f32[2048,128]{1,0:T(8,128)S(1)} %get-tuple-element.84.dmixed_ref, f32[2592,128]{1,0:T(8,128)S(1)} %get-tuple-element.151.dext_ref, s32[1,512]{1,0:T(1,128)S(1)} %bitcast.20, bf16[128,128]{1,0:T(8,128)(2,1)S(1)} %collective-permute-done.10.x_refs_0_, bf16[128,128]{1,0:T(8,128)(2,1)S(1)} %collective-permute-done.11.x_refs_1_, ...), custom_call_target="tpu_custom_call" | custom-call | flops 268435456 | bytes 4194304 | tf_op jit(solution)/shard_map/finish/pallas_call | solution.py:346
  121.8 1.4 %assemble.1 = (f32[3456,128]{1,0:T(8,128)}, f32[19,128]{1,0:T(8,128)}) custom-call(bf16[880,128]{1,0:T(8,128)(2,1)S(1)} %add_convert_fusion.refs_0_, bf16[880,128]{1,0:T(8,128)(2,1)S(1)} %collective-permute-done.13.refs_1_, bf16[880,128]{1,0:T(8,128)(2,1)S(1)} %collective-permute-done.9.refs_2_, bf16[880,128]{1,0:T(8,128)(2,1)S(1)} %collective-permute-done.14.refs_3_), custom_call_target="tpu_custom_call" | custom-call | tf_op jit(solution)/shard_map/assemble/pallas_call | solution.py:431
  (22 shorter events, 0.1 us)
Async XLA Ops:
  0.6 10.9 %copy-start = (bf16[2048,128]{1,0:T(8,128)(2,1)S(1)}, bf16[2048,128]{1,0:T(8,128)(2,1)}, u32[]{:S(2)}) copy-start(bf16[2048,128]{1,0:T(8,128)(2,1)} %own_hbm.3) | copy-start | bytes 1572868
  0.6 10.0 %copy-start.3 = (bf16[128,19]{0,1:T(8,128)(2,1)S(1)}, bf16[128,19]{0,1:T(8,128)(2,1)}, u32[]{:S(2)}) copy-start(bf16[128,19]{0,1:T(8,128)(2,1)} %param.8) | copy-start | bytes 14596
  0.7 10.9 %copy-start.1 = (bf16[27,128,128]{2,1,0:T(8,128)(2,1)S(1)}, bf16[27,128,128]{2,1,0:T(8,128)(2,1)}, u32[]{:S(2)}) copy-start(bf16[27,128,128]{2,1,0:T(8,128)(2,1)} %param.7) | copy-start | bytes 2654212
  3.6 7.1 %collective-permute-start = (bf16[128,128]{1,0:T(8,128)(2,1)}, bf16[128,128]{1,0:T(8,128)(2,1)S(1)}, u32[]{:S(2)}, u32[]{:S(2)}) collective-permute-start(bf16[128,128]{1,0:T(8,128)(2,1)} %get-tuple-element.81), channel_id=1, source_target_pairs={{0,4},{4,0},{8,12},{12,8},{1,5},{5,1},{9,13},{13,9},{2,6},{6,2},{1... | collective-permute-start | bytes 98312 | tf_op jit(solution)/shard_map/ppermute | solution.py:468
  6.7 4.0 %collective-permute-start.1 = (bf16[128,128]{1,0:T(8,128)(2,1)}, bf16[128,128]{1,0:T(8,128)(2,1)S(1)}, u32[]{:S(2)}, u32[]{:S(2)}) collective-permute-start(bf16[128,128]{1,0:T(8,128)(2,1)} %get-tuple-element.82), channel_id=1, source_target_pairs={{4,8},{8,4},{5,9},{9,5},{6,10},{10,6},{7,11},{11,7},{20,24},{24,20... | collective-permute-start | bytes 98312 | tf_op jit(solution)/shard_map/ppermute | solution.py:470
  7.3 4.2 %collective-permute-start.2 = (bf16[128,128]{1,0:T(8,128)(2,1)}, bf16[128,128]{1,0:T(8,128)(2,1)S(1)}, u32[]{:S(2)}, u32[]{:S(2)}) collective-permute-start(bf16[128,128]{1,0:T(8,128)(2,1)} %get-tuple-element.83), channel_id=1, source_target_pairs={{0,2},{2,0},{1,3},{3,1},{4,6},{6,4},{5,7},{7,5},{8,10},{10,8},{9,1... | collective-permute-start | bytes 98312 | tf_op jit(solution)/shard_map/ppermute | solution.py:468
  53.4 21.5 %collective-permute-start.3 = (bf16[880,128]{1,0:T(8,128)(2,1)S(1)}, bf16[880,128]{1,0:T(8,128)(2,1)S(1)}, u32[]{:S(2)}, u32[]{:S(2)}) collective-permute-start(bf16[880,128]{1,0:T(8,128)(2,1)S(1)} %get-tuple-element.88), channel_id=1, source_target_pairs={{0,1},{1,0},{2,3},{3,2},{4,5},{5,4},{6,7},{7,6},{8,9},{9,8},{10,11... | collective-permute-start | bytes 675848 | tf_op jit(solution)/shard_map/ppermute | solution.py:456
  53.5 21.4 %collective-permute-start.4 = (bf16[880,128]{1,0:T(8,128)(2,1)S(1)}, bf16[880,128]{1,0:T(8,128)(2,1)S(1)}, u32[]{:S(2)}, u32[]{:S(2)}) collective-permute-start(bf16[880,128]{1,0:T(8,128)(2,1)S(1)} %get-tuple-element.89), channel_id=1, source_target_pairs={{0,2},{1,3},{2,0},{3,1},{4,6},{5,7},{6,4},{7,5},{8,10},{9,11},{10,... | collective-permute-start | bytes 675848 | tf_op jit(solution)/shard_map/ppermute | solution.py:456
  55.1 19.8 %collective-permute-start.5 = (bf16[880,128]{1,0:T(8,128)(2,1)S(1)}, bf16[880,128]{1,0:T(8,128)(2,1)S(1)}, u32[]{:S(2)}, u32[]{:S(2)}) collective-permute-start(bf16[880,128]{1,0:T(8,128)(2,1)S(1)} %get-tuple-element.90), channel_id=1, source_target_pairs={{0,3},{1,2},{2,1},{3,0},{4,7},{5,6},{6,5},{7,4},{8,11},{9,10},{10,... | collective-permute-start | bytes 675848 | tf_op jit(solution)/shard_map/ppermute | solution.py:456
  75.0 27.2 %collective-permute-start.6 = (bf16[880,128]{1,0:T(8,128)(2,1)S(1)}, bf16[880,128]{1,0:T(8,128)(2,1)S(1)}, u32[]{:S(2)}, u32[]{:S(2)}) collective-permute-start(bf16[880,128]{1,0:T(8,128)(2,1)S(1)} %add_convert_fusion.1), channel_id=1, source_target_pairs={{0,4},{4,0},{8,12},{12,8},{1,5},{5,1},{9,13},{13,9},{2,6},{6,2},{1... | collective-permute-start | bytes 675848 | tf_op jit(solution)/shard_map/ppermute | solution.py:456
  79.5 22.7 %collective-permute-start.7 = (bf16[880,128]{1,0:T(8,128)(2,1)S(1)}, bf16[880,128]{1,0:T(8,128)(2,1)S(1)}, u32[]{:S(2)}, u32[]{:S(2)}) collective-permute-start(bf16[880,128]{1,0:T(8,128)(2,1)S(1)} %add_convert_fusion.1), channel_id=1, source_target_pairs={{0,8},{4,12},{8,0},{12,4},{1,9},{5,13},{9,1},{13,5},{2,10},{6,14},... | collective-permute-start | bytes 675848 | tf_op jit(solution)/shard_map/ppermute | solution.py:456
  79.5 22.7 %collective-permute-start.8 = (bf16[880,128]{1,0:T(8,128)(2,1)S(1)}, bf16[880,128]{1,0:T(8,128)(2,1)S(1)}, u32[]{:S(2)}, u32[]{:S(2)}) collective-permute-start(bf16[880,128]{1,0:T(8,128)(2,1)S(1)} %add_convert_fusion.1), channel_id=1, source_target_pairs={{0,12},{4,8},{8,4},{12,0},{1,13},{5,9},{9,5},{13,1},{2,14},{6,10},... | collective-permute-start | bytes 675848 | tf_op jit(solution)/shard_map/ppermute | solution.py:456
  102.4 11.3 %collective-permute-start.9 = (bf16[880,128]{1,0:T(8,128)(2,1)S(1)}, bf16[880,128]{1,0:T(8,128)(2,1)S(1)}, u32[]{:S(2)}, u32[]{:S(2)}) collective-permute-start(bf16[880,128]{1,0:T(8,128)(2,1)S(1)} %add_convert_fusion.refs_0_), channel_id=1, source_target_pairs={{0,2},{1,3},{2,0},{3,1},{4,6},{5,7},{6,4},{7,5},{8,10},{9,11},{10,... | collective-permute-start | bytes 675848 | tf_op jit(solution)/shard_map/ppermute | solution.py:456
  103.9 16.0 %copy-start.2 = (s32[4,128]{1,0:T(4,128)S(1)}, s32[4,128]{1,0:T(4,128)}, u32[]{:S(2)}) copy-start(s32[4,128]{1,0:T(4,128)} %send_hbm.1) | copy-start | bytes 6148
  113.6 8.1 %collective-permute-start.13 = (bf16[880,128]{1,0:T(8,128)(2,1)S(1)}, bf16[880,128]{1,0:T(8,128)(2,1)S(1)}, u32[]{:S(2)}, u32[]{:S(2)}) collective-permute-start(bf16[880,128]{1,0:T(8,128)(2,1)S(1)} %add_convert_fusion.refs_0_), channel_id=1, source_target_pairs={{0,1},{1,0},{2,3},{3,2},{4,5},{5,4},{6,7},{7,6},{8,9},{9,8},{10,11... | collective-permute-start | bytes 675848 | tf_op jit(solution)/shard_map/ppermute | solution.py:456
  113.7 8.1 %collective-permute-start.14 = (bf16[880,128]{1,0:T(8,128)(2,1)S(1)}, bf16[880,128]{1,0:T(8,128)(2,1)S(1)}, u32[]{:S(2)}, u32[]{:S(2)}) collective-permute-start(bf16[880,128]{1,0:T(8,128)(2,1)S(1)} %collective-permute-done.9.refs_2_), channel_id=1, source_target_pairs={{0,1},{1,0},{2,3},{3,2},{4,5},{5,4},{6,7},{7,6},{8,9},{9,8},{10,11... | collective-permute-start | bytes 675848 | tf_op jit(solution)/shard_map/ppermute | solution.py:456
  114.2 3.9 %collective-permute-start.10 = (bf16[128,128]{1,0:T(8,128)(2,1)S(1)}, bf16[128,128]{1,0:T(8,128)(2,1)S(1)}, u32[]{:S(2)}, u32[]{:S(2)}) collective-permute-start(bf16[128,128]{1,0:T(8,128)(2,1)S(1)} %get-tuple-element.152), channel_id=1, source_target_pairs={{0,4},{4,0},{8,12},{12,8},{1,5},{5,1},{9,13},{13,9},{2,6},{6,2},{1... | collective-permute-start | bytes 98312 | tf_op jit(solution)/shard_map/ppermute | solution.py:468
  115.3 2.9 %collective-permute-start.11 = (bf16[128,128]{1,0:T(8,128)(2,1)S(1)}, bf16[128,128]{1,0:T(8,128)(2,1)S(1)}, u32[]{:S(2)}, u32[]{:S(2)}) collective-permute-start(bf16[128,128]{1,0:T(8,128)(2,1)S(1)} %get-tuple-element.153), channel_id=1, source_target_pairs={{4,8},{8,4},{5,9},{9,5},{6,10},{10,6},{7,11},{11,7},{20,24},{24,20... | collective-permute-start | bytes 98312 | tf_op jit(solution)/shard_map/ppermute | solution.py:470
  115.9 4.0 %collective-permute-start.12 = (bf16[128,128]{1,0:T(8,128)(2,1)S(1)}, bf16[128,128]{1,0:T(8,128)(2,1)S(1)}, u32[]{:S(2)}, u32[]{:S(2)}) collective-permute-start(bf16[128,128]{1,0:T(8,128)(2,1)S(1)} %get-tuple-element.154), channel_id=1, source_target_pairs={{0,2},{2,0},{1,3},{3,1},{4,6},{6,4},{5,7},{7,5},{8,10},{10,8},{9,1... | collective-permute-start | bytes 98312 | tf_op jit(solution)/shard_map/ppermute | solution.py:468

commit v10 on v8

--- a/solution.py
+++ b/solution.py
@@ -8,12 +8,12 @@
 from jax.experimental.pallas import tpu as pltpu
 from jax.sharding import PartitionSpec as P
 
-STREAMS = 1
+STREAMS = 2
 SCATTER_STREAMS = 2
-SEGMENT = 256
+SEGMENT = 128
 BY_MATMUL = 8
 SCATTER_STEPS = 32
-FIRST_PART = 512
+FIRST_PART = 256
 CHUNKS = 2
 HEAD_ROWS = 32
 VMEM = pl.BlockSpec(memory_space=pltpu.VMEM)

time: 115 us -> 115 us (level)
  no operation moved by 1% of the time
where the time goes in v10:
time: 115 us
  Pallas kernels  89.3 us (78%)
  starting transfers between devices  18.5 us (16%)
  waiting for transfers between devices  4.17 us (4%)
  other arithmetic  1.94 us (2%)
    pallas_call x1, Pallas kernels, forward(): pl.pallas_call(functools.partial(forward_kernel, classes), out_shape=(jax...  42 us
    pallas_call x2, Pallas kernels, scatter(): pl.pallas_call(functools.partial(scatter_kernel, first, offsets, has_befo...  41.1 us
    ppermute x9, starting transfers between devices, exchange(): lax.ppermute(shard, axes, [(i, i ^ distance) for i in range(group_size(ax...  9.95 us
    ppermute x4, starting transfers between devices, swap_edges(): got = [lax.ppermute(over_even, axis, even_pairs)]  7.29 us
    ppermute x4, waiting for transfers between devices, swap_edges(): got = [lax.ppermute(over_even, axis, even_pairs)]  4.14 us
    pallas_call x1, Pallas kernels, outgoing(): pl.pallas_call(functools.partial(outgoing_kernel, ('ty', 'tx')), out_shap...  2.88 us
  transfers between devices with their start and end apart: 15, of which 3 were waited for; matrix products, arithmetic and copies ran while one was open for 2% of the time, Pallas kernels for 37%

profile of v10, /device:TPU:0, one launch (start us, length us, event | category | flops | bytes accessed | tf_op | source)
XLA Modules:
  0.0 115.0 jit_solution(12083426186655836438)
XLA Ops:
  0.7 2.9 %outgoing.1 = (bf16[128,128]{1,0:T(8,128)(2,1)}, bf16[128,128]{1,0:T(8,128)(2,1)}, bf16[128,128]{1,0:T(8,128)(2,1)}, bf16[128,128]{1,0:T(8,128)(2,1)}) custom-call(s32[4,128]{1,0:T(4,128)} %send_hbm.1, bf16[2048,128]{1,0:T(8,128)(2,1)} %own_hbm.3), custom_call_target="tpu_custom_call" | custom-call | bytes 8388608 | tf_op jit(solution)/shard_map/outgoing/pallas_call | solution.py:334
  3.5 3.1 %collective-permute-start = (bf16[128,128]{1,0:T(8,128)(2,1)}, bf16[128,128]{1,0:T(8,128)(2,1)S(1)}, u32[]{:S(2)}, u32[]{:S(2)}) collective-permute-start(bf16[128,128]{1,0:T(8,128)(2,1)} %get-tuple-element.41), channel_id=1, source_target_pairs={{0,4},{4,0},{8,12},{12,8},{1,5},{5,1},{9,13},{13,9},{2,6},{6,2},{1... | collective-permute-start | bytes 98312 | tf_op jit(solution)/shard_map/ppermute | solution.py:412
  6.6 0.7 collective-permute-start.1
  7.3 1.6 %collective-permute-start.2 = (bf16[128,128]{1,0:T(8,128)(2,1)}, bf16[128,128]{1,0:T(8,128)(2,1)S(1)}, u32[]{:S(2)}, u32[]{:S(2)}) collective-permute-start(bf16[128,128]{1,0:T(8,128)(2,1)} %get-tuple-element.43), channel_id=1, source_target_pairs={{0,2},{2,0},{1,3},{3,1},{4,6},{6,4},{5,7},{7,5},{8,10},{10,8},{9,1... | collective-permute-start | bytes 98312 | tf_op jit(solution)/shard_map/ppermute | solution.py:412
  8.9 1.0 fusion
  9.9 0.7 minimum_bitcast_fusion
  10.7 0.0 collective-permute-done.1.x_refs_1_
  10.7 0.8 collective-permute-done.2.y_refs_0_
  11.5 42.0 %forward.1 = (f32[2048,128]{1,0:T(8,128)S(1)}, f32[2048,128]{1,0:T(8,128)S(1)}, f32[3520,128]{1,0:T(8,128)S(1)}, bf16[3456,128]{1,0:T(8,128)(2,1)S(1)}) custom-call(s32[55296]{0:T(1024)S(1)} %reshape.36.map_hbm, s32[8,8,256]{2,1,0:T(8,128)S(1)} %bitcast.21, bf16[2048,128]{1,0:T(8,128)(2,1)S(1)} %copy-done, ...), custom_call_target="tpu_custom_call" | custom-call | tf_op jit(solution)/shard_map/forward/pallas_call | solution.py:164
  53.6 0.1 dynamic-slice_convert_fusion
  53.7 0.1 collective-permute-start.3
  53.7 1.6 %collective-permute-start.4 = (bf16[880,128]{1,0:T(8,128)(2,1)S(1)}, bf16[880,128]{1,0:T(8,128)(2,1)S(1)}, u32[]{:S(2)}, u32[]{:S(2)}) collective-permute-start(bf16[880,128]{1,0:T(8,128)(2,1)S(1)} %get-tuple-element.49), channel_id=1, source_target_pairs={{0,2},{1,3},{2,0},{3,1},{4,6},{5,7},{6,4},{7,5},{8,10},{9,11},{10,... | collective-permute-start | bytes 675848 | tf_op jit(solution)/shard_map/ppermute | solution.py:400
  55.4 0.3 collective-permute-start.5
  55.6 19.5 %scatter_0.1.refs_0_ = f32[2592,128]{1,0:T(8,128)S(1)} custom-call(s32[55296]{0:T(1024)S(1)} %reshape.36.map_hbm, f32[2,1024,128]{2,1,0:T(8,128)S(1)} %bitcast.18, bf16[3456,128]{1,0:T(8,128)(2,1)S(1)} %get-tuple-element.52.weight_ref), custom_call_target="tpu_custom_call" | custom-call | flops 872415232 | bytes 41943040 | tf_op jit(solution)/shard_map/scatter_0/pallas_call | solution.py:248
  75.1 0.0 collective-permute-done.3
  75.2 0.0 collective-permute-done.4
  75.2 0.1 add_convert_fusion.1
  75.3 2.5 %collective-permute-start.8 = (bf16[880,128]{1,0:T(8,128)(2,1)S(1)}, bf16[880,128]{1,0:T(8,128)(2,1)S(1)}, u32[]{:S(2)}, u32[]{:S(2)}) collective-permute-start(bf16[880,128]{1,0:T(8,128)(2,1)S(1)} %add_convert_fusion.1), channel_id=1, source_target_pairs={{0,12},{4,8},{8,4},{12,0},{1,13},{5,9},{9,5},{13,1},{2,14},{6,10},... | collective-permute-start | bytes 675848 | tf_op jit(solution)/shard_map/ppermute | solution.py:400
  77.8 3.4 %collective-permute-start.7 = (bf16[880,128]{1,0:T(8,128)(2,1)S(1)}, bf16[880,128]{1,0:T(8,128)(2,1)S(1)}, u32[]{:S(2)}, u32[]{:S(2)}) collective-permute-start(bf16[880,128]{1,0:T(8,128)(2,1)S(1)} %add_convert_fusion.1), channel_id=1, source_target_pairs={{0,8},{4,12},{8,0},{12,4},{1,9},{5,13},{9,1},{13,5},{2,10},{6,14},... | collective-permute-start | bytes 675848 | tf_op jit(solution)/shard_map/ppermute | solution.py:400
  81.3 21.6 %scatter_13.1 = (f32[2592,128]{1,0:T(8,128)S(1)}, bf16[128,128]{1,0:T(8,128)(2,1)S(1)}, bf16[128,128]{1,0:T(8,128)(2,1)}, bf16[128,128]{1,0:T(8,128)(2,1)S(1)}, bf16[128,128]{1,0:T(8,128)(2,1)S(1)}) custom-call(s32[55296]{0:T(1024)S(1)} %reshape.36.map_hbm, f32[2,1024,128]{2,1,0:T(8,128)S(1)} %bitcast.19, ...), custom_call_target="tpu_custom_call" | custom-call | flops 939524096 | bytes 41943040 | tf_op jit(solution)/shard_map/scatter_13/pallas_call | solution.py:248
  102.9 0.0 collective-permute-done.8
  102.9 0.0 collective-permute-done.7
  102.9 0.1 add_convert_fusion.refs_0_
  103.0 1.5 %collective-permute-start.9 = (bf16[880,128]{1,0:T(8,128)(2,1)S(1)}, bf16[880,128]{1,0:T(8,128)(2,1)S(1)}, u32[]{:S(2)}, u32[]{:S(2)}) collective-permute-start(bf16[880,128]{1,0:T(8,128)(2,1)S(1)} %add_convert_fusion.refs_0_), channel_id=1, source_target_pairs={{0,2},{1,3},{2,0},{3,1},{4,6},{5,7},{6,4},{7,5},{8,10},{9,11},{10,... | collective-permute-start | bytes 675848 | tf_op jit(solution)/shard_map/ppermute | solution.py:400
  104.6 2.0 %collective-permute-start.10 = (bf16[128,128]{1,0:T(8,128)(2,1)S(1)}, bf16[128,128]{1,0:T(8,128)(2,1)S(1)}, u32[]{:S(2)}, u32[]{:S(2)}) collective-permute-start(bf16[128,128]{1,0:T(8,128)(2,1)S(1)} %get-tuple-element.69), channel_id=1, source_target_pairs={{0,4},{4,0},{8,12},{12,8},{1,5},{5,1},{9,13},{13,9},{2,6},{6,2},{1... | collective-permute-start | bytes 98312 | tf_op jit(solution)/shard_map/ppermute | solution.py:412
  106.6 0.7 collective-permute-start.11
  107.2 0.6 collective-permute-start.12
  107.9 0.6 collective-permute-done.10.x_refs_0_
  108.5 2.7 %collective-permute-done.12.y_refs_0_ = bf16[128,128]{1,0:T(8,128)(2,1)S(1)} collective-permute-done((bf16[128,128]{1,0:T(8,128)(2,1)S(1)}, bf16[128,128]{1,0:T(8,128)(2,1)S(1)}, u32[]{:S(2)}, u32[]{:S(2)}) %collective-permute-start.12) | collective-permute-done | bytes 32800 | tf_op jit(solution)/shard_map/ppermute | solution.py:412
  111.2 0.5 collective-permute-start.14
  111.7 1.9 %finish.1 = f32[2048,128]{1,0:T(8,128)} custom-call(f32[2048,128]{1,0:T(8,128)S(1)} %get-tuple-element.44.dmixed_ref, f32[2592,128]{1,0:T(8,128)S(1)} %get-tuple-element.64.dext_ref, s32[1,512]{1,0:T(1,128)S(1)} %bitcast.23, bf16[128,128]{1,0:T(8,128)(2,1)S(1)} %collective-permute-done.10.x_refs_0_, bf16[128,128]{1,0:T(8,128)(2,1)S(1)} %collective-permute-done.11.x_refs_1_, ...), custom_call_target="tpu_custom_call" | custom-call | flops 268435456 | bytes 4194304 | tf_op jit(solution)/shard_map/finish/pallas_call | solution.py:290
  113.6 1.4 %assemble.1 = (f32[3456,128]{1,0:T(8,128)}, f32[19,128]{1,0:T(8,128)}) custom-call(bf16[880,128]{1,0:T(8,128)(2,1)S(1)} %add_convert_fusion.refs_0_, bf16[880,128]{1,0:T(8,128)(2,1)S(1)} %collective-permute-done.13.refs_1_, bf16[880,128]{1,0:T(8,128)(2,1)S(1)} %collective-permute-done.9.refs_2_, bf16[880,128]{1,0:T(8,128)(2,1)S(1)} %collective-permute-done.14.refs_3_), custom_call_target="tpu_custom_call" | custom-call | tf_op jit(solution)/shard_map/assemble/pallas_call | solution.py:375
  (23 shorter events, 0.1 us)
Async XLA Ops:
  0.6 10.9 %copy-start = (bf16[2048,128]{1,0:T(8,128)(2,1)S(1)}, bf16[2048,128]{1,0:T(8,128)(2,1)}, u32[]{:S(2)}) copy-start(bf16[2048,128]{1,0:T(8,128)(2,1)} %own_hbm.3) | copy-start | bytes 1572868
  0.6 10.0 %copy-start.3 = (bf16[128,19]{0,1:T(8,128)(2,1)S(1)}, bf16[128,19]{0,1:T(8,128)(2,1)}, u32[]{:S(2)}) copy-start(bf16[128,19]{0,1:T(8,128)(2,1)} %param.8) | copy-start | bytes 14596
  0.7 10.8 %copy-start.1 = (bf16[27,128,128]{2,1,0:T(8,128)(2,1)S(1)}, bf16[27,128,128]{2,1,0:T(8,128)(2,1)}, u32[]{:S(2)}) copy-start(bf16[27,128,128]{2,1,0:T(8,128)(2,1)} %param.7) | copy-start | bytes 2654212
  3.5 7.1 %collective-permute-start = (bf16[128,128]{1,0:T(8,128)(2,1)}, bf16[128,128]{1,0:T(8,128)(2,1)S(1)}, u32[]{:S(2)}, u32[]{:S(2)}) collective-permute-start(bf16[128,128]{1,0:T(8,128)(2,1)} %get-tuple-element.41), channel_id=1, source_target_pairs={{0,4},{4,0},{8,12},{12,8},{1,5},{5,1},{9,13},{13,9},{2,6},{6,2},{1... | collective-permute-start | bytes 98312 | tf_op jit(solution)/shard_map/ppermute | solution.py:412
  6.6 4.1 %collective-permute-start.1 = (bf16[128,128]{1,0:T(8,128)(2,1)}, bf16[128,128]{1,0:T(8,128)(2,1)S(1)}, u32[]{:S(2)}, u32[]{:S(2)}) collective-permute-start(bf16[128,128]{1,0:T(8,128)(2,1)} %get-tuple-element.42), channel_id=1, source_target_pairs={{4,8},{8,4},{5,9},{9,5},{6,10},{10,6},{7,11},{11,7},{20,24},{24,20... | collective-permute-start | bytes 98312 | tf_op jit(solution)/shard_map/ppermute | solution.py:414
  7.3 4.2 %collective-permute-start.2 = (bf16[128,128]{1,0:T(8,128)(2,1)}, bf16[128,128]{1,0:T(8,128)(2,1)S(1)}, u32[]{:S(2)}, u32[]{:S(2)}) collective-permute-start(bf16[128,128]{1,0:T(8,128)(2,1)} %get-tuple-element.43), channel_id=1, source_target_pairs={{0,2},{2,0},{1,3},{3,1},{4,6},{6,4},{5,7},{7,5},{8,10},{10,8},{9,1... | collective-permute-start | bytes 98312 | tf_op jit(solution)/shard_map/ppermute | solution.py:412
  53.7 21.5 %collective-permute-start.3 = (bf16[880,128]{1,0:T(8,128)(2,1)S(1)}, bf16[880,128]{1,0:T(8,128)(2,1)S(1)}, u32[]{:S(2)}, u32[]{:S(2)}) collective-permute-start(bf16[880,128]{1,0:T(8,128)(2,1)S(1)} %get-tuple-element.48), channel_id=1, source_target_pairs={{0,1},{1,0},{2,3},{3,2},{4,5},{5,4},{6,7},{7,6},{8,9},{9,8},{10,11... | collective-permute-start | bytes 675848 | tf_op jit(solution)/shard_map/ppermute | solution.py:400
  53.7 21.4 %collective-permute-start.4 = (bf16[880,128]{1,0:T(8,128)(2,1)S(1)}, bf16[880,128]{1,0:T(8,128)(2,1)S(1)}, u32[]{:S(2)}, u32[]{:S(2)}) collective-permute-start(bf16[880,128]{1,0:T(8,128)(2,1)S(1)} %get-tuple-element.49), channel_id=1, source_target_pairs={{0,2},{1,3},{2,0},{3,1},{4,6},{5,7},{6,4},{7,5},{8,10},{9,11},{10,... | collective-permute-start | bytes 675848 | tf_op jit(solution)/shard_map/ppermute | solution.py:400
  55.4 19.8 %collective-permute-start.5 = (bf16[880,128]{1,0:T(8,128)(2,1)S(1)}, bf16[880,128]{1,0:T(8,128)(2,1)S(1)}, u32[]{:S(2)}, u32[]{:S(2)}) collective-permute-start(bf16[880,128]{1,0:T(8,128)(2,1)S(1)} %get-tuple-element.50), channel_id=1, source_target_pairs={{0,3},{1,2},{2,1},{3,0},{4,7},{5,6},{6,5},{7,4},{8,11},{9,10},{10,... | collective-permute-start | bytes 675848 | tf_op jit(solution)/shard_map/ppermute | solution.py:400
  75.3 27.6 %collective-permute-start.8 = (bf16[880,128]{1,0:T(8,128)(2,1)S(1)}, bf16[880,128]{1,0:T(8,128)(2,1)S(1)}, u32[]{:S(2)}, u32[]{:S(2)}) collective-permute-start(bf16[880,128]{1,0:T(8,128)(2,1)S(1)} %add_convert_fusion.1), channel_id=1, source_target_pairs={{0,12},{4,8},{8,4},{12,0},{1,13},{5,9},{9,5},{13,1},{2,14},{6,10},... | collective-permute-start | bytes 675848 | tf_op jit(solution)/shard_map/ppermute | solution.py:400
  77.8 25.0 %collective-permute-start.7 = (bf16[880,128]{1,0:T(8,128)(2,1)S(1)}, bf16[880,128]{1,0:T(8,128)(2,1)S(1)}, u32[]{:S(2)}, u32[]{:S(2)}) collective-permute-start(bf16[880,128]{1,0:T(8,128)(2,1)S(1)} %add_convert_fusion.1), channel_id=1, source_target_pairs={{0,8},{4,12},{8,0},{12,4},{1,9},{5,13},{9,1},{13,5},{2,10},{6,14},... | collective-permute-start | bytes 675848 | tf_op jit(solution)/shard_map/ppermute | solution.py:400
  81.3 21.6 %collective-permute-start.6 = (bf16[880,128]{1,0:T(8,128)(2,1)S(1)}, bf16[880,128]{1,0:T(8,128)(2,1)S(1)}, u32[]{:S(2)}, u32[]{:S(2)}) collective-permute-start(bf16[880,128]{1,0:T(8,128)(2,1)S(1)} %add_convert_fusion.1), channel_id=1, source_target_pairs={{0,4},{4,0},{8,12},{12,8},{1,5},{5,1},{9,13},{13,9},{2,6},{6,2},{1... | collective-permute-start | bytes 675848 | tf_op jit(solution)/shard_map/ppermute | solution.py:400
  81.3 30.4 %copy-start.2 = (s32[4,128]{1,0:T(4,128)S(1)}, s32[4,128]{1,0:T(4,128)}, u32[]{:S(2)}) copy-start(s32[4,128]{1,0:T(4,128)} %send_hbm.1) | copy-start | bytes 6148
  103.0 8.2 %collective-permute-start.9 = (bf16[880,128]{1,0:T(8,128)(2,1)S(1)}, bf16[880,128]{1,0:T(8,128)(2,1)S(1)}, u32[]{:S(2)}, u32[]{:S(2)}) collective-permute-start(bf16[880,128]{1,0:T(8,128)(2,1)S(1)} %add_convert_fusion.refs_0_), channel_id=1, source_target_pairs={{0,2},{1,3},{2,0},{3,1},{4,6},{5,7},{6,4},{7,5},{8,10},{9,11},{10,... | collective-permute-start | bytes 675848 | tf_op jit(solution)/shard_map/ppermute | solution.py:400
  104.6 3.9 %collective-permute-start.10 = (bf16[128,128]{1,0:T(8,128)(2,1)S(1)}, bf16[128,128]{1,0:T(8,128)(2,1)S(1)}, u32[]{:S(2)}, u32[]{:S(2)}) collective-permute-start(bf16[128,128]{1,0:T(8,128)(2,1)S(1)} %get-tuple-element.69), channel_id=1, source_target_pairs={{0,4},{4,0},{8,12},{12,8},{1,5},{5,1},{9,13},{13,9},{2,6},{6,2},{1... | collective-permute-start | bytes 98312 | tf_op jit(solution)/shard_map/ppermute | solution.py:412
  106.6 1.9 %collective-permute-start.11 = (bf16[128,128]{1,0:T(8,128)(2,1)S(1)}, bf16[128,128]{1,0:T(8,128)(2,1)S(1)}, u32[]{:S(2)}, u32[]{:S(2)}) collective-permute-start(bf16[128,128]{1,0:T(8,128)(2,1)S(1)} %get-tuple-element.70), channel_id=1, source_target_pairs={{4,8},{8,4},{5,9},{9,5},{6,10},{10,6},{7,11},{11,7},{20,24},{24,20... | collective-permute-start | bytes 98312 | tf_op jit(solution)/shard_map/ppermute | solution.py:414
  107.2 4.0 %collective-permute-start.12 = (bf16[128,128]{1,0:T(8,128)(2,1)S(1)}, bf16[128,128]{1,0:T(8,128)(2,1)S(1)}, u32[]{:S(2)}, u32[]{:S(2)}) collective-permute-start(bf16[128,128]{1,0:T(8,128)(2,1)S(1)} %get-tuple-element.71), channel_id=1, source_target_pairs={{0,2},{2,0},{1,3},{3,1},{4,6},{6,4},{5,7},{7,5},{8,10},{10,8},{9,1... | collective-permute-start | bytes 98312 | tf_op jit(solution)/shard_map/ppermute | solution.py:412
  111.2 2.4 %collective-permute-start.13 = (bf16[880,128]{1,0:T(8,128)(2,1)S(1)}, bf16[880,128]{1,0:T(8,128)(2,1)S(1)}, u32[]{:S(2)}, u32[]{:S(2)}) collective-permute-start(bf16[880,128]{1,0:T(8,128)(2,1)S(1)} %add_convert_fusion.refs_0_), channel_id=1, source_target_pairs={{0,1},{1,0},{2,3},{3,2},{4,5},{5,4},{6,7},{7,6},{8,9},{9,8},{10,11... | collective-permute-start | bytes 675848 | tf_op jit(solution)/shard_map/ppermute | solution.py:400
  111.2 2.4 %collective-permute-start.14 = (bf16[880,128]{1,0:T(8,128)(2,1)S(1)}, bf16[880,128]{1,0:T(8,128)(2,1)S(1)}, u32[]{:S(2)}, u32[]{:S(2)}) collective-permute-start(bf16[880,128]{1,0:T(8,128)(2,1)S(1)} %collective-permute-done.9.refs_2_), channel_id=1, source_target_pairs={{0,1},{1,0},{2,3},{3,2},{4,5},{5,4},{6,7},{7,6},{8,9},{9,8},{10,11... | collective-permute-start | bytes 675848 | tf_op jit(solution)/shard_map/ppermute | solution.py:400
